TPU v7x, 32 devices: a whole 2x2x4 slice. The times are simulated.
32 devices in a mesh: dp: 8 (over y, x, core), tensor: 4 (over z).
Axes of the slice: x: 2, y: 2, z: 4, core: 2. Of those that a mesh axis runs over, the one named last changes fastest.
Arguments:
- inputs: bfloat16 [2, 8192, 1024], P(None, ('dp', 'tensor')), may hold values from -6 to 6
- query_weight: bfloat16 [1024, 1024], P('dp', 'tensor'), may hold values from -0.1875 to 0.1875
- query_bias: float32 [1024], P('tensor'), may hold values from -3 to 3
- key_weight: bfloat16 [1024, 1024], P('dp', 'tensor'), may hold values from -0.1875 to 0.1875
- value_weight: bfloat16 [1024, 1024], P('dp', 'tensor'), may hold values from -0.1875 to 0.1875
- value_bias: float32 [1024], P('tensor'), may hold values from -3 to 3
- out_weight: bfloat16 [1024, 1024], P('tensor', 'dp'), may hold values from -4 to 4
- out_bias: float32 [1024], replicated, may hold values from -3 to 3
- first_gain: float32 [1024], replicated, may hold values from 0.5 to 1.5
- first_shift: float32 [1024], replicated, may hold values from -2 to 2
- up_weight: bfloat16 [1024, 4096], P('dp', 'tensor'), may hold values from -0.1875 to 0.1875
- up_bias: float32 [4096], P('tensor'), may hold values from -3 to 3
- down_weight: bfloat16 [4096, 1024], P('tensor', 'dp'), may hold values from -0.09375 to 0.09375
- down_bias: float32 [1024], replicated, may hold values from -3 to 3
- second_gain: float32 [1024], replicated, may hold values from 0.5 to 1.5
- second_shift: float32 [1024], replicated, may hold values from -2 to 2
- cotangent: bfloat16 [2, 8192, 1024], P(None, ('dp', 'tensor')), may hold values from -6 to 6
Outputs:
- outputs: bfloat16 [2, 8192, 1024], P(None, ('dp', 'tensor'))
- input_grad: float32 [2, 8192, 1024], P(None, ('dp', 'tensor'))
- query_weight_grad: float32 [1024, 1024], P('dp', 'tensor')
- query_bias_grad: float32 [1024], P('tensor')
- key_weight_grad: float32 [1024, 1024], P('dp', 'tensor')
- value_weight_grad: float32 [1024, 1024], P('dp', 'tensor')
- value_bias_grad: float32 [1024], P('tensor')
- out_weight_grad: float32 [1024, 1024], P('tensor', 'dp')
- out_bias_grad: float32 [1024], replicated
- first_gain_grad: float32 [1024], replicated
- first_shift_grad: float32 [1024], replicated
- up_weight_grad: float32 [1024, 4096], P('dp', 'tensor')
- up_bias_grad: float32 [4096], P('tensor')
- down_weight_grad: float32 [4096, 1024], P('tensor', 'dp')
- down_bias_grad: float32 [1024], replicated
- second_gain_grad: float32 [1024], replicated
- second_shift_grad: float32 [1024], replicated
All inputs are finite; a program needn't handle non-finite values.
Results may differ from a plain program's by a relative error of at most 0.017.
Values may be sent and summed in bfloat16 or wider, within the bound.
A program may use at most 192 MiB of HBM per device.

v0:
```python
import jax
import jax.numpy as jnp
from jax import lax
from jax.sharding import PartitionSpec as P

HD = 64
LEN = 1024


EPSILON = 1e-05


def exact_gelu(value):
    return jax.nn.gelu(value, approximate=False)


def norm_forward(hidden, gain, shift):
    average = jnp.mean(hidden, axis=-1, keepdims=True)
    center = hidden - average
    spread = jnp.mean(center * center, axis=-1, keepdims=True)
    inverse = lax.rsqrt(spread + EPSILON)
    normed = center * inverse
    return (normed * gain + shift, normed, inverse)


def norm_backward(grad, normed, inverse, gain):
    scaled = grad * gain
    average = jnp.mean(scaled, axis=-1, keepdims=True)
    along = jnp.mean(scaled * normed, axis=-1, keepdims=True)
    return (
        (scaled - average - normed * along) * inverse,
        jnp.sum(grad * normed, axis=0),
        jnp.sum(grad, axis=0),
    )


def dense(left, right):
    return jnp.dot(left, right, preferred_element_type=jnp.float32)


def dense_back(left, right):
    return lax.dot_general(
        left, right, (((1,), (1,)), ((), ())), preferred_element_type=jnp.float32
    )


def dense_outer(left, right):
    return lax.dot_general(
        left, right, (((0,), (0,)), ((), ())), preferred_element_type=jnp.float32
    )


def attend_forward(block):
    query, keys, values = block
    scores = jnp.einsum("qhd,khd->hqk", query, keys, preferred_element_type=jnp.float32)
    top = jnp.max(scores, axis=-1, keepdims=True)
    expo = jnp.exp(scores - top)
    total = jnp.sum(expo, axis=-1, keepdims=True)
    weights = (expo / total).astype(jnp.bfloat16)
    mixed = jnp.einsum("hqk,khd->qhd", weights, values, preferred_element_type=jnp.float32)
    return (mixed, top[..., 0] + jnp.log(total[..., 0]))


def attend_backward(block):
    query, keys, values, logsum, grad_mixed = block
    scores = jnp.einsum("qhd,khd->hqk", query, keys, preferred_element_type=jnp.float32)
    weights = jnp.exp(scores - logsum[..., None])
    grad_weights = jnp.einsum(
        "qhd,khd->hqk", grad_mixed, values, preferred_element_type=jnp.float32
    )
    inner = jnp.sum(weights * grad_weights, axis=-1, keepdims=True)
    grad_scores = (weights * (grad_weights - inner)).astype(jnp.bfloat16)
    grad_query = jnp.einsum(
        "hqk,khd->qhd", grad_scores, keys, preferred_element_type=jnp.float32
    ).astype(jnp.bfloat16)
    grad_keys = jnp.einsum(
        "hqk,qhd->khd", grad_scores, query, preferred_element_type=jnp.float32
    ).astype(jnp.bfloat16)
    grad_values = jnp.einsum(
        "hqk,qhd->khd", weights.astype(jnp.bfloat16), grad_mixed, preferred_element_type=jnp.float32
    ).astype(jnp.bfloat16)
    return (grad_query, grad_keys, grad_values)


def shards(
    inputs,
    query_weight,
    query_bias,
    key_weight,
    value_weight,
    value_bias,
    out_weight,
    out_bias,
    first_gain,
    first_shift,
    up_weight,
    up_bias,
    down_weight,
    down_bias,
    second_gain,
    second_shift,
    cotangent,
):
    tensor_count = lax.axis_size("tensor")
    tensor_place = lax.axis_index("tensor")
    micro_count = inputs.shape[0]
    rows = inputs.shape[1]
    group = rows * tensor_count
    number = group // LEN
    heads = query_weight.shape[1] // HD
    local_width = heads * HD
    hidden_width = up_bias.shape[0]
    scale = HD ** (-0.5)
    shape = (number, LEN, heads, HD)
    flat = (group, local_width)
    results = []
    input_grads = []
    weight_total = None
    small_total = None
    for micro in range(micro_count):
        current = (
            lax.all_gather(query_weight, "dp", axis=0, tiled=True),
            lax.all_gather(key_weight, "dp", axis=0, tiled=True),
            lax.all_gather(value_weight, "dp", axis=0, tiled=True),
            lax.all_gather(up_weight, "dp", axis=0, tiled=True),
            lax.all_gather(out_weight, "dp", axis=1, tiled=True),
            lax.all_gather(down_weight, "dp", axis=1, tiled=True),
        )
        full_query, full_key, full_value, full_up, full_out, full_down = current
        source = inputs[micro]
        whole = lax.all_gather(source, "tensor", axis=0, tiled=True)
        query = ((dense(whole, full_query) + query_bias) * scale).astype(jnp.bfloat16)
        keys = dense(whole, full_key).astype(jnp.bfloat16)
        values = (dense(whole, full_value) + value_bias).astype(jnp.bfloat16)
        mixed, logsum = lax.map(
            attend_forward, (query.reshape(shape), keys.reshape(shape), values.reshape(shape))
        )
        mixed_low = mixed.reshape(flat).astype(jnp.bfloat16)
        first_sum = (
            source.astype(jnp.float32)
            + lax.psum_scatter(
                dense(mixed_low, full_out), "tensor", scatter_dimension=0, tiled=True
            )
            + out_bias
        )
        first, first_normed, first_inverse = norm_forward(first_sum, first_gain, first_shift)
        whole_first = lax.all_gather(first.astype(jnp.bfloat16), "tensor", axis=0, tiled=True)
        upper = dense(whole_first, full_up) + up_bias
        gated_value, gelu_back = jax.vjp(exact_gelu, upper)
        gated = gated_value.astype(jnp.bfloat16)
        second_sum = (
            first
            + lax.psum_scatter(
                dense(gated, full_down).astype(jnp.bfloat16),
                "tensor",
                scatter_dimension=0,
                tiled=True,
            ).astype(jnp.float32)
            + down_bias
        )
        second, second_normed, second_inverse = norm_forward(second_sum, second_gain, second_shift)
        results.append(second.astype(jnp.bfloat16))
        back_weights = (
            lax.all_gather(query_weight, "dp", axis=0, tiled=True),
            lax.all_gather(key_weight, "dp", axis=0, tiled=True),
            lax.all_gather(value_weight, "dp", axis=0, tiled=True),
            lax.all_gather(up_weight, "dp", axis=0, tiled=True),
            lax.all_gather(out_weight, "dp", axis=1, tiled=True),
            lax.all_gather(down_weight, "dp", axis=1, tiled=True),
        )
        back_query, back_key, back_value, back_up, back_out, back_down = back_weights
        grad_second, second_gain_part, second_shift_part = norm_backward(
            cotangent[micro].astype(jnp.float32), second_normed, second_inverse, second_gain
        )
        whole_grad_second = lax.all_gather(
            grad_second.astype(jnp.bfloat16), "tensor", axis=0, tiled=True
        )
        down_part = dense_outer(gated, whole_grad_second)
        grad_upper = gelu_back(dense_back(whole_grad_second, back_down))[0].astype(jnp.bfloat16)
        up_part = dense_outer(whole_first, grad_upper)
        up_bias_part = jnp.sum(grad_upper.astype(jnp.float32), axis=0)
        grad_first_sum = (
            lax.psum_scatter(
                dense_back(grad_upper, back_up), "tensor", scatter_dimension=0, tiled=True
            )
            + grad_second
        )
        grad_first, first_gain_part, first_shift_part = norm_backward(
            grad_first_sum, first_normed, first_inverse, first_gain
        )
        whole_grad_first = lax.all_gather(
            grad_first.astype(jnp.bfloat16), "tensor", axis=0, tiled=True
        )
        out_part = dense_outer(mixed_low, whole_grad_first)
        grad_mixed = dense_back(whole_grad_first, back_out).astype(jnp.bfloat16)
        grad_query, grad_keys, grad_values = lax.map(
            attend_backward,
            (
                query.reshape(shape),
                keys.reshape(shape),
                values.reshape(shape),
                logsum,
                grad_mixed.reshape(shape),
            ),
        )
        grad_query = grad_query.reshape(flat) * scale
        grad_keys = grad_keys.reshape(flat)
        grad_values = grad_values.reshape(flat)
        query_part = dense_outer(whole, grad_query)
        key_part = dense_outer(whole, grad_keys)
        value_part = dense_outer(whole, grad_values)
        input_grads.append(
            lax.psum_scatter(
                (
                    dense_back(grad_query, back_query)
                    + dense_back(grad_keys, back_key)
                    + dense_back(grad_values, back_value)
                ).astype(jnp.bfloat16),
                "tensor",
                scatter_dimension=0,
                tiled=True,
            ).astype(jnp.float32)
            + grad_first
        )
        weight_part = (query_part, key_part, value_part, up_part, out_part, down_part)
        small_part = (
            jnp.sum(grad_query.astype(jnp.float32), axis=0),
            jnp.sum(grad_values.astype(jnp.float32), axis=0),
            up_bias_part,
            jnp.sum(grad_first, axis=0),
            jnp.sum(grad_second, axis=0),
            first_gain_part,
            first_shift_part,
            second_gain_part,
            second_shift_part,
        )
        if weight_total is None:
            weight_total = weight_part
            small_total = small_part
        else:
            weight_total = jax.tree.map(jnp.add, weight_total, weight_part)
            small_total = jax.tree.map(jnp.add, small_total, small_part)
    weight_total = (
        lax.psum_scatter(weight_total[0], "dp", scatter_dimension=0, tiled=True),
        lax.psum_scatter(weight_total[1], "dp", scatter_dimension=0, tiled=True),
        lax.psum_scatter(weight_total[2], "dp", scatter_dimension=0, tiled=True),
        lax.psum_scatter(weight_total[3], "dp", scatter_dimension=0, tiled=True),
        lax.psum_scatter(weight_total[4], "dp", scatter_dimension=1, tiled=True),
        lax.psum_scatter(weight_total[5], "dp", scatter_dimension=1, tiled=True),
    )
    query_bias_full = lax.dynamic_update_slice_in_dim(
        jnp.zeros((local_width * tensor_count,), jnp.float32),
        small_total[0],
        tensor_place * local_width,
        0,
    )
    value_bias_full = lax.dynamic_update_slice_in_dim(
        jnp.zeros((local_width * tensor_count,), jnp.float32),
        small_total[1],
        tensor_place * local_width,
        0,
    )
    up_bias_full = lax.dynamic_update_slice_in_dim(
        jnp.zeros((hidden_width * tensor_count,), jnp.float32),
        small_total[2],
        tensor_place * hidden_width,
        0,
    )
    summed = lax.psum(
        (
            query_bias_full,
            value_bias_full,
            up_bias_full,
            small_total[3],
            small_total[4],
            small_total[5],
            small_total[6],
            small_total[7],
            small_total[8],
        ),
        ("dp", "tensor"),
    )
    query_bias_grad = lax.dynamic_slice_in_dim(summed[0], tensor_place * local_width, local_width)
    value_bias_grad = lax.dynamic_slice_in_dim(summed[1], tensor_place * local_width, local_width)
    up_bias_grad = lax.dynamic_slice_in_dim(summed[2], tensor_place * hidden_width, hidden_width)
    return (
        jnp.stack(results),
        jnp.stack(input_grads),
        weight_total[0],
        query_bias_grad,
        weight_total[1],
        weight_total[2],
        value_bias_grad,
        weight_total[4],
        summed[3],
        summed[5],
        summed[6],
        weight_total[3],
        up_bias_grad,
        weight_total[5],
        summed[4],
        summed[7],
        summed[8],
    )


def solution(mesh):
    return jax.shard_map(
        shards,
        mesh=mesh,
        in_specs=(
            P(None, ("dp", "tensor"), None),
            P("dp", "tensor"),
            P("tensor"),
            P("dp", "tensor"),
            P("dp", "tensor"),
            P("tensor"),
            P("tensor", "dp"),
            P(),
            P(),
            P(),
            P("dp", "tensor"),
            P("tensor"),
            P("tensor", "dp"),
            P(),
            P(),
            P(),
            P(None, ("dp", "tensor"), None),
        ),
        out_specs=(
            P(None, ("dp", "tensor"), None),
            P(None, ("dp", "tensor"), None),
            P("dp", "tensor"),
            P("tensor"),
            P("dp", "tensor"),
            P("dp", "tensor"),
            P("tensor"),
            P("tensor", "dp"),
            P(),
            P(),
            P(),
            P("dp", "tensor"),
            P("tensor"),
            P("tensor", "dp"),
            P(),
            P(),
            P(),
        ),
        check_vma=False,
    )
```

profile of v0, /device:TPU:8, one launch (start us, length us, event | category | flops | bytes accessed | tf_op | source)
XLA Modules:
  0.0 1244.5 jit_solution(13753837523179244803)
XLA Ops:
  11.2 10.2 all_gather.30
  21.3 9.5 all_gather.31
  30.9 9.2 all_gather.29
  40.0 9.7 all_gather.64
  49.7 6.9 all-gather.31.cloned.1.call-done
  56.6 2.3 fusion.109
  58.9 2.5 fusion.94
  61.5 8.5 fusion.152
  70.0 8.2 fusion.1
  79.0 7.6 fusion.118
  87.5 2.8 fusion.154
  90.8 12.5 %all-gather.29.cloned.1.call-done = bf16[1,1024,1024]{2,1,0:T(8,128)(2,1)} async-done(((bf16[1,256,1024]{2,1,0:T(8,128)(2,1)}), bf16[1,1024,1024]{2,1,0:T(8,128)(2,1)}) %all-gather.29.cloned.1.call-update) | async-done | bytes 2097168 | tf_op jit(solution)/shard_map/all_gather | solution.py:131
  103.4 2.5 fusion.106
  105.9 2.5 fusion.97
  109.3 8.6 fusion.151
  117.8 8.1 fusion
  125.9 7.5 fusion.119
  134.2 2.7 fusion.153
  137.6 45.2 %reduce-scatter.19.cloned.1.call-done = f32[256,1024]{1,0:T(8,128)} async-done(((f32[1024,1024]{1,0:T(8,128)}), f32[256,1024]{1,0:T(8,128)}) %reduce-scatter.19.cloned.1.call-update) | async-done | bytes 1048592 | tf_op jit(solution)/shard_map/reduce_scatter | solution.py:141
  182.8 79.5 %reduce-scatter.15.cloned.1.call-done = f32[256,1024]{1,0:T(8,128)} async-done(((f32[1024,1024]{1,0:T(8,128)}), f32[256,1024]{1,0:T(8,128)}) %reduce-scatter.15.cloned.1.call-update) | async-done | bytes 1048592 | tf_op jit(solution)/shard_map/reduce_scatter | solution.py:141
  267.8 43.3 %all-gather.19.cloned.1.call-done = bf16[1024,1024]{1,0:T(8,128)(2,1)} async-done(((bf16[256,1024]{1,0:T(8,128)(2,1)}), bf16[1024,1024]{1,0:T(8,128)(2,1)}) %all-gather.19.cloned.1.call-update) | async-done | bytes 2097168 | tf_op jit(solution)/shard_map/all_gather | solution.py:147
  311.1 6.6 fusion.155
  317.7 39.8 %all-gather.13.cloned.1.call-done = bf16[1024,1024]{1,0:T(8,128)(2,1)} async-done(((bf16[256,1024]{1,0:T(8,128)(2,1)}), bf16[1024,1024]{1,0:T(8,128)(2,1)}) %all-gather.13.cloned.1.call-update) | async-done | bytes 2097168 | tf_op jit(solution)/shard_map/all_gather | solution.py:147
  357.5 24.1 %multiply_convert_fusion.3 = (bf16[1024,1024]{1,0:T(8,128)(2,1)}, f32[1024,1024]{1,0:T(8,128)}, bf16[1024,1024]{1,0:T(8,128)(2,1)}, f32[1024,1024]{1,0:T(8,128)}, f32[1024,1024]{1,0:T(8,128)}) fusion(f32[1024]{0:T(1024)S(1)} %copy-done.62, f32[1024,1024]{1,0:T(8,128)} %fusion.155, bf16[1024,1024]{1,0:T(8,128)(2,1)} %all-gather.13.cloned.1.call-done, ...), kind=kOutput, calls=%fused_computation.43 | convolution fusion | flops 2285895680 | bytes 25169920 | tf_op jit(solution)/shard_map/dot_general | solution.py:38
  381.5 6.0 all-gather.17.cloned.1.call-done
  387.6 5.9 convolution_convert_fusion.1
  393.5 5.9 convolution_convert_fusion
  399.8 36.5 %reduce-scatter.17.cloned.1.call-done = bf16[256,1024]{1,0:T(8,128)(2,1)} async-done(((bf16[1024,1024]{1,0:T(8,128)(2,1)}), bf16[256,1024]{1,0:T(8,128)(2,1)}) %reduce-scatter.17.cloned.1.call-update) | async-done | bytes 524304 | tf_op jit(solution)/shard_map/reduce_scatter | solution.py:153
  436.3 45.1 %reduce-scatter.21.cloned.1.call-done = bf16[256,1024]{1,0:T(8,128)(2,1)} async-done(((bf16[1024,1024]{1,0:T(8,128)(2,1)}), bf16[256,1024]{1,0:T(8,128)(2,1)}) %reduce-scatter.21.cloned.1.call-update) | async-done | bytes 524304 | tf_op jit(solution)/shard_map/reduce_scatter | solution.py:153
  491.1 42.1 %all-gather.25.cloned.1.call-done = bf16[1024,1024]{1,0:T(8,128)(2,1)} async-done(((bf16[256,1024]{1,0:T(8,128)(2,1)}), bf16[1024,1024]{1,0:T(8,128)(2,1)}) %all-gather.25.cloned.1.call-update) | async-done | bytes 2097168 | tf_op jit(solution)/shard_map/all_gather | solution.py:175
  533.2 6.6 fusion.159
  539.9 39.8 %all-gather.21.cloned.1.call-done = bf16[1024,1024]{1,0:T(8,128)(2,1)} async-done(((bf16[256,1024]{1,0:T(8,128)(2,1)}), bf16[1024,1024]{1,0:T(8,128)(2,1)}) %all-gather.21.cloned.1.call-update) | async-done | bytes 2097168 | tf_op jit(solution)/shard_map/all_gather | solution.py:175
  579.6 13.3 %convert_reduce_fusion.1 = (f32[1024]{0:T(1024)S(1)}, bf16[1024,1024]{1,0:T(8,128)(2,1)S(1)}, f32[1024]{0:T(1024)S(1)}, bf16[1024,1024]{1,0:T(8,128)(2,1)}) fusion(f32[1024,1024]{1,0:T(8,128)} %get-tuple-element.168, f32[1024,1024]{1,0:T(8,128)} %get-tuple-element.203, f32[1024]{0:T(1024)S(1)} %copy-done.62, f32[1024,1024]{1,0:T(8,128)} %fusion.159, ...), kind=kOutput, calls=%fused_computation.25 | convolution fusion | flops 2183133184 | bytes 29372416 | tf_op jit(solution)/shard_map/dot_general | solution.py:42
  594.3 4.4 fusion.156
  598.8 6.5 fusion.160
  605.8 70.0 %reduce-scatter.23.cloned.1.call-done = f32[256,1024]{1,0:T(8,128)} async-done(((f32[1024,1024]{1,0:T(8,128)}), f32[256,1024]{1,0:T(8,128)}) %reduce-scatter.23.cloned.1.call-update) | async-done | bytes 1048592 | tf_op jit(solution)/shard_map/reduce_scatter | solution.py:183
  675.7 2.9 multiply_reduce_fusion.3
  678.6 76.7 %reduce-scatter.27.cloned.1.call-done = f32[256,1024]{1,0:T(8,128)} async-done(((f32[1024,1024]{1,0:T(8,128)}), f32[256,1024]{1,0:T(8,128)}) %reduce-scatter.27.cloned.1.call-update) | async-done | bytes 1048592 | tf_op jit(solution)/shard_map/reduce_scatter | solution.py:183
  755.3 3.3 fusion.141
  763.2 42.2 %all-gather.23.cloned.1.call-done = bf16[1024,1024]{1,0:T(8,128)(2,1)} async-done(((bf16[256,1024]{1,0:T(8,128)(2,1)}), bf16[1024,1024]{1,0:T(8,128)(2,1)}) %all-gather.23.cloned.1.call-update) | async-done | bytes 2097168 | tf_op jit(solution)/shard_map/all_gather | solution.py:191
  805.3 2.3 convolution_convert_fusion.7
  807.7 9.3 convert_reduce_fusion.5
  817.0 10.7 multiply_reduce_fusion.1
  827.7 24.2 %all-gather.27.cloned.1.call-done = bf16[1024,1024]{1,0:T(8,128)(2,1)} async-done(((bf16[256,1024]{1,0:T(8,128)(2,1)}), bf16[1024,1024]{1,0:T(8,128)(2,1)}) %all-gather.27.cloned.1.call-update) | async-done | bytes 2097168 | tf_op jit(solution)/shard_map/all_gather | solution.py:191
  854.3 8.6 convert_reduce_fusion.4
  862.9 11.1 multiply_reduce_fusion
  877.7 12.6 %multiply_convert_fusion.1 = bf16[4,1024,1024]{1,2,0:T(8,128)(2,1)S(1)} fusion(f32[4,1024,1024]{1,2,0:T(8,128)} %get-tuple-element.207, f32[4,1024,1024]{1,2,0:T(8,128)} %get-tuple-element.200, f32[4,1024]{1,0:T(4,128)S(1)} %get-tuple-element.206, f32[4,1024]{1,0:T(4,128)S(1)} %log_add_fusion.1), kind=kLoop, calls=%fused_computation.3 | loop fusion | flops 16777216 | bytes 41975808 | tf_op jit(solution)/shard_map/while/body/eval_jaxpr/convert_element_type | solution.py:72
  891.9 3.8 slice-done.2
  896.9 10.6 multiply_convert_fusion
  907.5 6.4 convolution_convert_fusion.2
  915.4 2.7 convolution_convert_fusion.4
  920.7 5.3 convert_reduce_fusion.6
  941.1 4.8 fusion.165
  946.0 4.5 convolution_add_fusion
  950.8 4.9 fusion.164
  955.8 4.5 convolution_add_fusion.1
  961.3 2.4 fusion.163
  963.8 2.9 convolution_add_fusion.2
  969.9 41.7 %all-reduce = (f32[1024]{0:T(1024)S(1)}, f32[1024]{0:T(1024)S(1)}, f32[1024]{0:T(1024)}, f32[1024]{0:T(1024)}, f32[1024]{0:T(1024)}, /*index=5*/f32[4096]{0:T(10...) all-reduce(f32[1024]{0:T(1024)S(1)} %dynamic_update_slice.32, ...), channel_id=1, replica_groups=mesh['dp'=8,'tensor'=4] {'dp','tensor'}, use_global_device_ids=true, to_apply=%region_33.34 | all-reduce | flops 12288 | bytes 98304 | tf_op jit(solution)/shard_map/psum | solution.py:269
  1018.4 22.6 %reduce-scatter.25.cloned.1.call-done = bf16[256,1024]{1,0:T(8,128)(2,1)} async-done(((bf16[1024,1024]{1,0:T(8,128)(2,1)}), bf16[256,1024]{1,0:T(8,128)(2,1)}) %reduce-scatter.25.cloned.1.call-update) | async-done | bytes 524304 | tf_op jit(solution)/shard_map/reduce_scatter | solution.py:213
  1042.2 43.9 %reduce-scatter.29.cloned.1.call-done = bf16[256,1024]{1,0:T(8,128)(2,1)} async-done(((bf16[1024,1024]{1,0:T(8,128)(2,1)}), bf16[256,1024]{1,0:T(8,128)(2,1)}) %reduce-scatter.29.cloned.1.call-update) | async-done | bytes 524304 | tf_op jit(solution)/shard_map/reduce_scatter | solution.py:213
  1088.8 52.5 %reduce-scatter.41.cloned.1.call-done = f32[1024,128]{1,0:T(8,128)} async-done(((f32[1024,1024]{1,0:T(8,128)}), f32[1024,128]{1,0:T(8,128)}) %reduce-scatter.41.cloned.1.call-update) | async-done | bytes 524304 | tf_op jit(solution)/shard_map/reduce_scatter | solution.py:249
  1141.3 55.5 %reduce-scatter.39.cloned.1.call-done = f32[128,1024]{1,0:T(8,128)} async-done(((f32[1024,1024]{1,0:T(8,128)}), f32[128,1024]{1,0:T(8,128)}) %reduce-scatter.39.cloned.1.call-update) | async-done | bytes 524304 | tf_op jit(solution)/shard_map/reduce_scatter | solution.py:247
  1196.8 39.8 %reduce-scatter.37.cloned.1.call-done = f32[256,128]{1,0:T(8,128)} async-done(((f32[256,1024]{1,0:T(8,128)}), f32[256,128]{1,0:T(8,128)}) %reduce-scatter.37.cloned.1.call-update) | async-done | bytes 131088 | tf_op jit(solution)/shard_map/reduce_scatter | solution.py:248
  (271 shorter events, 71.9 us)
Async XLA Ops:
  8.0 22.8 %copy-start.50 = (bf16[128,256]{1,0:T(8,128)(2,1)S(1)}, bf16[128,256]{1,0:T(8,128)(2,1)}, u32[]{:S(2)}) copy-start(bf16[128,256]{1,0:T(8,128)(2,1)} %param.21) | copy-start | bytes 196612
  8.0 32.0 %copy-start.51 = (bf16[256,128]{1,0:T(8,128)(2,1)S(1)}, bf16[256,128]{1,0:T(8,128)(2,1)}, u32[]{:S(2)}) copy-start(bf16[256,128]{1,0:T(8,128)(2,1)} %param.23) | copy-start | bytes 196612
  8.0 50.9 %copy-start.63 = (f32[256]{0:T(256)S(1)}, f32[256]{0:T(256)}, u32[]{:S(2)}) copy-start(f32[256]{0:T(256)} %param.19) | copy-start | bytes 3076
  8.1 48.5 %all-gather.31.cloned.1.call-start = ((), (), s32[]{:S(2)}) async-start(), calls=%async_computation.37 | async-start | bytes 2621440 | tf_op jit(solution)/shard_map/all_gather | solution.py:131
  10.4 93.0 %all-gather.29.cloned.1.call-start = ((), (), s32[]{:S(2)}) async-start(), calls=%async_computation.36 | async-start | bytes 2621440 | tf_op jit(solution)/shard_map/all_gather | solution.py:131
  11.1 171.7 %reduce-scatter.19.cloned.1.call-start = ((), (), s32[]{:S(2)}) async-start(), calls=%async_computation.19 | async-start | bytes 5242880 | tf_op jit(solution)/shard_map/reduce_scatter | solution.py:141
  21.3 84.6 %copy-start.26 = (bf16[1024,256]{1,0:T(8,128)(2,1)}, bf16[1024,256]{1,0:T(8,128)(2,1)S(1)}, u32[]{:S(2)}) copy-start(bf16[1024,256]{1,0:T(8,128)(2,1)S(1)} %all_gather.30) | copy-start | bytes 1572868
  30.9 72.5 %copy-start.29 = (bf16[1024,256]{1,0:T(8,128)(2,1)}, bf16[1024,256]{1,0:T(8,128)(2,1)S(1)}, u32[]{:S(2)}) copy-start(bf16[1024,256]{1,0:T(8,128)(2,1)S(1)} %all_gather.31) | copy-start | bytes 1572868
  40.0 68.4 %copy-start.24 = (bf16[1024,256]{1,0:T(8,128)(2,1)}, bf16[1024,256]{1,0:T(8,128)(2,1)S(1)}, u32[]{:S(2)}) copy-start(bf16[1024,256]{1,0:T(8,128)(2,1)S(1)} %all_gather.29) | copy-start | bytes 1572868
  49.7 83.7 %copy-start.30 = (bf16[256,1024]{1,0:T(8,128)(2,1)}, bf16[256,1024]{1,0:T(8,128)(2,1)S(1)}, u32[]{:S(2)}) copy-start(bf16[256,1024]{1,0:T(8,128)(2,1)S(1)} %all_gather.64) | copy-start | bytes 1572868
  58.9 11.0 copy-start.36
  61.5 8.5 copy-start.39
  69.9 9.0 copy-start.47
  70.0 8.2 copy-start.2
  70.0 8.2 copy-start.64
  78.2 8.5 copy-start.52
  90.3 172.0 %reduce-scatter.15.cloned.1.call-start = ((), (), s32[]{:S(2)}) async-start(), calls=%async_computation.14 | async-start | bytes 5242880 | tf_op jit(solution)/shard_map/reduce_scatter | solution.py:141
  105.9 11.9 copy-start.37
  108.5 9.4 copy-start.40
  109.3 16.7 %copy-start.45 = (bf16[1024,256]{0,1:T(8,128)(2,1)}, bf16[1024,256]{0,1:T(8,128)(2,1)S(1)}, u32[]{:S(2)}) copy-start(bf16[1024,256]{0,1:T(8,128)(2,1)S(1)} %fusion.115) | copy-start | bytes 1572868
  136.9 125.4 %copy-start.32 = (bf16[2,256,1024]{2,1,0:T(8,128)(2,1)S(1)}, bf16[2,256,1024]{2,1,0:T(8,128)(2,1)}, u32[]{:S(2)}) copy-start(bf16[2,256,1024]{2,1,0:T(8,128)(2,1)} %param.17) | copy-start | bytes 3145732
  136.9 125.4 %copy-start.58 = (f32[1024]{0:T(1024)S(1)}, f32[1024]{0:T(1024)}, u32[]{:S(2)}) copy-start(f32[1024]{0:T(1024)} %param.24) | copy-start | bytes 12292
  136.9 127.9 %copy-start.49 = (f32[1024]{0:T(1024)S(1)}, f32[1024]{0:T(1024)}, u32[]{:S(2)}) copy-start(f32[1024]{0:T(1024)} %param.25) | copy-start | bytes 12292
  136.9 127.8 %copy-start.54 = (f32[1024]{0:T(1024)S(1)}, f32[1024]{0:T(1024)}, u32[]{:S(2)}) copy-start(f32[1024]{0:T(1024)} %param.26) | copy-start | bytes 12292
  137.0 130.8 %all-gather.15.cloned.1.call-start = ((), (), s32[]{:S(2)}) async-start(), calls=%async_computation.16 | async-start | bytes 2359296 | tf_op jit(solution)/shard_map/all_gather | solution.py:125
  137.5 173.5 %all-gather.19.cloned.1.call-start = ((), (), s32[]{:S(2)}) async-start(), calls=%async_computation.20 | async-start | bytes 2621440 | tf_op jit(solution)/shard_map/all_gather | solution.py:147
  266.2 91.3 %all-gather.13.cloned.1.call-start = ((), (), s32[]{:S(2)}) async-start(), calls=%async_computation.15 | async-start | bytes 2621440 | tf_op jit(solution)/shard_map/all_gather | solution.py:147
  266.8 120.8 %all-gather.17.cloned.1.call-start = ((), (), s32[]{:S(2)}) async-start(), calls=%async_computation.17 | async-start | bytes 2359296 | tf_op jit(solution)/shard_map/all_gather | solution.py:127
  267.5 90.0 %copy-start.62 = (f32[1024]{0:T(1024)S(1)}, f32[1024]{0:T(1024)}, u32[]{:S(2)}) copy-start(f32[1024]{0:T(1024)} %param.28) | copy-start | bytes 12292
  267.5 168.7 %reduce-scatter.17.cloned.1.call-start = ((), (), s32[]{:S(2)}) async-start(), calls=%async_computation.18 | async-start | bytes 2621440 | tf_op jit(solution)/shard_map/reduce_scatter | solution.py:153
  393.5 87.9 %reduce-scatter.21.cloned.1.call-start = ((), (), s32[]{:S(2)}) async-start(), calls=%async_computation.21 | async-start | bytes 2621440 | tf_op jit(solution)/shard_map/reduce_scatter | solution.py:153
  393.5 87.9 %copy-start.56 = (f32[1024]{0:T(1024)S(1)}, f32[1024]{0:T(1024)}, u32[]{:S(2)}) copy-start(f32[1024]{0:T(1024)} %param.30) | copy-start | bytes 12292
  399.5 84.3 %copy-start.8 = (bf16[2,256,1024]{2,1,0:T(8,128)(2,1)S(1)}, bf16[2,256,1024]{2,1,0:T(8,128)(2,1)}, u32[]{:S(2)}) copy-start(bf16[2,256,1024]{2,1,0:T(8,128)(2,1)} %param.33) | copy-start | bytes 3145732
  399.5 84.3 %copy-start.55 = (f32[1024]{0:T(1024)S(1)}, f32[1024]{0:T(1024)}, u32[]{:S(2)}) copy-start(f32[1024]{0:T(1024)} %param.31) | copy-start | bytes 12292
  399.5 85.3 %copy-start.57 = (f32[1024]{0:T(1024)S(1)}, f32[1024]{0:T(1024)}, u32[]{:S(2)}) copy-start(f32[1024]{0:T(1024)} %param.32) | copy-start | bytes 12292
  399.5 133.7 %all-gather.25.cloned.1.call-start = ((), (), s32[]{:S(2)}) async-start(), calls=%async_computation.26 | async-start | bytes 2621440 | tf_op jit(solution)/shard_map/all_gather | solution.py:175
  488.9 90.8 %all-gather.21.cloned.1.call-start = ((), (), s32[]{:S(2)}) async-start(), calls=%async_computation.22 | async-start | bytes 2621440 | tf_op jit(solution)/shard_map/all_gather | solution.py:175
  491.0 184.7 %reduce-scatter.23.cloned.1.call-start = ((), (), s32[]{:S(2)}) async-start(), calls=%async_computation.23 | async-start | bytes 5242880 | tf_op jit(solution)/shard_map/reduce_scatter | solution.py:183
  579.6 14.6 %copy-start.61 = (bf16[1024,1024]{1,0:T(8,128)(2,1)S(1)}, bf16[1024,1024]{1,0:T(8,128)(2,1)}, u32[]{:S(2)}) copy-start(bf16[1024,1024]{1,0:T(8,128)(2,1)} %all-gather.15.cloned.1.call-done) | copy-start | bytes 6291460
  598.7 156.6 %reduce-scatter.27.cloned.1.call-start = ((), (), s32[]{:S(2)}) async-start(), calls=%async_computation.27 | async-start | bytes 5242880 | tf_op jit(solution)/shard_map/reduce_scatter | solution.py:183
  605.3 150.0 %copy-start.13 = (f32[256,1024]{1,0:T(8,128)S(1)}, f32[256,1024]{1,0:T(8,128)}, u32[]{:S(2)}) copy-start(f32[256,1024]{1,0:T(8,128)} %copy-done.12) | copy-start | bytes 3145732
  605.3 200.0 %all-gather.23.cloned.1.call-start = ((), (), s32[]{:S(2)}) async-start(), calls=%async_computation.24 | async-start | bytes 2621440 | tf_op jit(solution)/shard_map/all_gather | solution.py:191
  758.6 46.7 %copy-start.31 = (bf16[256,1024]{1,0:T(8,128)(2,1)S(1)}, bf16[256,1024]{1,0:T(8,128)(2,1)}, u32[]{:S(2)}) copy-start(bf16[256,1024]{1,0:T(8,128)(2,1)} %copy-done.30) | copy-start | bytes 1572868
  760.5 91.4 %all-gather.27.cloned.1.call-start = ((), (), s32[]{:S(2)}) async-start(), calls=%async_computation.28 | async-start | bytes 2621440 | tf_op jit(solution)/shard_map/all_gather | solution.py:191
  763.1 250.3 %reduce-scatter.35.cloned.1.call-start = ((), (), s32[]{:S(2)}) async-start(), calls=%async_computation.32 | async-start | bytes 1179648 | tf_op jit(solution)/shard_map/reduce_scatter | solution.py:246
  807.7 9.3 copy-start.46
  854.2 8.6 copy-start.44
  862.9 11.2 copy-start.14
  862.9 11.2 copy-start.3
  862.9 11.9 copy-start.16
  877.4 137.6 %reduce-scatter.33.cloned.1.call-start = ((), (), s32[]{:S(2)}) async-start(), calls=%async_computation.31 | async-start | bytes 1179648 | tf_op jit(solution)/shard_map/reduce_scatter | solution.py:245
  877.6 12.6 %slice-start = ((s8[16777216]{0:T(1024)(128)(4,1)}), s8[4194304]{0:T(1024)(128)(4,1)S(1)}, s32[]{:S(2)}) async-start(s8[16777216]{0:T(1024)(128)(4,1)} %bitcast.240), calls=%async_computation.38 | async-start | bytes 8388608
  877.6 14.3 %slice-start.1 = ((s8[16777216]{0:T(1024)(128)(4,1)}), s8[4194304]{0:T(1024)(128)(4,1)S(1)}, s32[]{:S(2)}) async-start(s8[16777216]{0:T(1024)(128)(4,1)} %bitcast.240), calls=%async_computation.39 | async-start | bytes 8388608
  877.6 18.0 %slice-start.2 = ((s8[16777216]{0:T(1024)(128)(4,1)}), s8[4194304]{0:T(1024)(128)(4,1)S(1)}, s32[]{:S(2)}) async-start(s8[16777216]{0:T(1024)(128)(4,1)} %bitcast.240), calls=%async_computation.40 | async-start | bytes 8388608
  877.6 19.2 %slice-start.3 = ((s8[16777216]{0:T(1024)(128)(4,1)}), s8[4194304]{0:T(1024)(128)(4,1)S(1)}, s32[]{:S(2)}) async-start(s8[16777216]{0:T(1024)(128)(4,1)} %bitcast.240), calls=%async_computation.41 | async-start | bytes 8388608
  890.2 25.1 %copy-start = (bf16[4,1024,1024]{1,2,0:T(8,128)(2,1)}, bf16[4,1024,1024]{1,2,0:T(8,128)(2,1)S(1)}, u32[]{:S(2)}) copy-start(bf16[4,1024,1024]{1,2,0:T(8,128)(2,1)S(1)} %multiply_convert_fusion.1) | copy-start | bytes 25165828
  907.5 7.9 copy-start.41
  920.6 96.1 %reduce-scatter.31.cloned.1.call-start = ((), (), s32[]{:S(2)}) async-start(), calls=%async_computation.30 | async-start | bytes 1179648 | tf_op jit(solution)/shard_map/reduce_scatter | solution.py:244
  931.0 109.9 %reduce-scatter.25.cloned.1.call-start = ((), (), s32[]{:S(2)}) async-start(), calls=%async_computation.25 | async-start | bytes 2621440 | tf_op jit(solution)/shard_map/reduce_scatter | solution.py:213
  936.1 150.0 %reduce-scatter.29.cloned.1.call-start = ((), (), s32[]{:S(2)}) async-start(), calls=%async_computation.29 | async-start | bytes 2621440 | tf_op jit(solution)/shard_map/reduce_scatter | solution.py:213
  941.1 200.2 %reduce-scatter.41.cloned.1.call-start = ((), (), s32[]{:S(2)}) async-start(), calls=%async_computation.35 | async-start | bytes 4718592 | tf_op jit(solution)/shard_map/reduce_scatter | solution.py:249
  950.5 246.3 %reduce-scatter.39.cloned.1.call-start = ((), (), s32[]{:S(2)}) async-start(), calls=%async_computation.34 | async-start | bytes 4718592 | tf_op jit(solution)/shard_map/reduce_scatter | solution.py:247
  960.3 276.3 %reduce-scatter.37.cloned.1.call-start = ((), (), s32[]{:S(2)}) async-start(), calls=%async_computation.33 | async-start | bytes 1179648 | tf_op jit(solution)/shard_map/reduce_scatter | solution.py:248
  963.8 77.2 %copy-start.11 = (f32[256,1024]{1,0:T(8,128)S(1)}, f32[256,1024]{1,0:T(8,128)}, u32[]{:S(2)}) copy-start(f32[256,1024]{1,0:T(8,128)} %copy-done.10) | copy-start | bytes 3145732
  (32 other events, 98.3 us)
Sparse Core Ops, SparseCore 0:
  11.0 45.4 all-gather.30
  58.7 44.6 all-gather.28
  105.7 77.0 reduce-scatter.18
  185.0 77.2 reduce-scatter.14
  598.8 76.8 reduce-scatter.22
  678.0 77.2 reduce-scatter.26
Sparse Core Ops, SparseCore 1:
  139.3 28.1 all-gather.14
  266.3 44.7 all-gather.18
  313.1 44.3 all-gather.12
  359.4 28.1 all-gather.16
  393.5 42.7 reduce-scatter.16
  438.7 42.7 reduce-scatter.20
  488.9 44.2 all-gather.24
  535.2 44.3 all-gather.20
  760.6 44.7 all-gather.22
  807.5 44.3 all-gather.26
  877.5 36.1 reduce-scatter.34
  920.7 36.0 reduce-scatter.32
  959.8 36.1 reduce-scatter.30
  998.3 42.6 reduce-scatter.24
  1043.4 42.7 reduce-scatter.28
  1090.1 51.2 reduce-scatter.40
  1145.7 51.1 reduce-scatter.38
  1200.6 35.9 reduce-scatter.36
where the time goes:
time: 1260 us; the launch traced here: 1240 us
  waiting for transfers between devices  827 us (66%)
  matrix products  224 us (18%)
  blocking collectives  80.2 us (6%)
  other arithmetic  67.7 us (5%)
  local copies, waits for them, and re-layouts  25.6 us (2%)
  between operations  17.4 us (1%)
    reduce_scatter x2, waiting for transfers between devices, shards(): lax.psum_scatter(dense_back(grad_upper, back_up), 'tensor', scatter_dimen...  147 us
    reduce_scatter x2, waiting for transfers between devices, shards(): lax.psum_scatter(dense(mixed_low, full_out), 'tensor', scatter_dimension=...  125 us
    all_gather x2, waiting for transfers between devices, shards(): lax.all_gather(first.astype(jnp.bfloat16), 'tensor', axis=0, tiled=True)  83.1 us
    all_gather x2, waiting for transfers between devices, shards(): lax.all_gather(grad_second.astype(jnp.bfloat16), 'tensor', axis=0, tiled=...  81.9 us
    reduce_scatter x2, waiting for transfers between devices, shards(): lax.psum_scatter(dense(gated, full_down).astype(jnp.bfloat16), 'tensor',...  81.6 us
    reduce_scatter x2, waiting for transfers between devices, shards(): lax.psum_scatter((dense_back(grad_query, back_query) + dense_back(grad_ke...  66.5 us
    all_gather x2, waiting for transfers between devices, shards(): lax.all_gather(grad_first.astype(jnp.bfloat16), 'tensor', axis=0, tiled=T...  66.4 us
    dot_general x12, matrix products, dense(): return jnp.dot(left, right, preferred_element_type=jnp.float32)  59.4 us
  transfers between devices with their start and end apart: 24, of which 20 were waited for; matrix products, arithmetic and copies ran while one was open for 19% of the time, Pallas kernels for 0%

commit v1 on v0

v1 whole, which is shorter than its diff:
```python
import functools
import math

import jax
import jax.numpy as jnp
import numpy as np
from jax import lax
from jax.experimental import pallas as pl
from jax.experimental.pallas import tpu as pltpu
from jax.sharding import PartitionSpec as P

HD = 64
LEN = 1024
EPSILON = 1e-05
SCALE = HD ** (-0.5)
LOG2E = math.log2(math.e)
BF = jnp.bfloat16
F32 = jnp.float32
AXES = ("dp", "tensor")
MIB = 1 << 20


def dot_nn(left, right):
    return jnp.dot(left, right, preferred_element_type=F32)


def dot_nt(left, right):
    return lax.dot_general(left, right, (((1,), (1,)), ((), ())), preferred_element_type=F32)


def dot_tn(left, right):
    return lax.dot_general(left, right, (((0,), (0,)), ((), ())), preferred_element_type=F32)


def joined(refs, pick=None):
    parts = []
    for ref in refs:
        value = ref[...] if pick is None else ref[:, :, pick]
        parts.append(value.reshape(-1, value.shape[-1]))
    return parts[0] if len(parts) == 1 else jnp.concatenate(parts, axis=0)


def call(kernel, grid, in_specs, out_specs, out_shape, scratch, flops, moved, limit=48, exps=0):
    return pl.pallas_call(
        kernel,
        grid=grid,
        in_specs=in_specs,
        out_specs=out_specs,
        out_shape=out_shape,
        scratch_shapes=scratch,
        compiler_params=pltpu.CompilerParams(vmem_limit_bytes=limit * MIB),
        cost_estimate=pl.CostEstimate(flops=flops, bytes_accessed=moved, transcendentals=exps),
    )


def whole_spec(shape):
    return pl.BlockSpec(shape, lambda *_: (0,) * len(shape))


def row_tile(rows):
    return min(rows, 512)


def qkv_kernel(count, x_ref, *refs):
    w_refs, bias_ref, out_ref = refs[:count], refs[count], refs[count + 1]
    acc = dot_nn(x_ref[...], joined(w_refs))
    scale = jnp.where(pl.program_id(0) == 0, SCALE, 1.0)
    out_ref[0] = ((acc + bias_ref[0]) * scale).astype(BF)


def project_qkv(x, slots, bias):
    rows, width = x.shape
    parts, cols = slots[0].shape[1], slots[0].shape[-1]
    specs = [
        pl.BlockSpec((s.shape[0], 1, 1, s.shape[3], cols), lambda w, z: (0, z, w, 0, 0)) for s in slots
    ]
    return call(
        functools.partial(qkv_kernel, len(slots)),
        (3, parts),
        [whole_spec(x.shape)] + specs + [pl.BlockSpec((1, 1, cols), lambda w, z: (w, 0, z))],
        pl.BlockSpec((1, rows, cols), lambda w, z: (w, 0, z)),
        jax.ShapeDtypeStruct((3, rows, parts * cols), BF),
        [],
        2 * rows * width * 3 * parts * cols,
        2 * (rows * width * 4 + 3 * width * parts * cols),
    )(x, *slots, bias)


def plain_kernel(count, x_ref, *refs):
    w_refs, out_ref = refs[:count], refs[count]
    out_ref[...] = dot_nn(x_ref[...], joined(w_refs)).astype(BF)


def project_back(x, slots, which):
    rows, width = x.shape
    parts, cols = slots[0].shape[1], slots[0].shape[-1]
    specs = [
        pl.BlockSpec((s.shape[0], 1, 1, s.shape[3], cols), lambda z: (0, z, which, 0, 0)) for s in slots
    ]
    return call(
        functools.partial(plain_kernel, len(slots)),
        (parts,),
        [whole_spec(x.shape)] + specs,
        pl.BlockSpec((rows, cols), lambda z: (0, z)),
        jax.ShapeDtypeStruct((rows, parts * cols), BF),
        [],
        2 * rows * width * parts * cols,
        2 * (rows * width * 2 + width * parts * cols),
    )(x, *slots)


def attend_kernel(count, q_ref, *refs):
    k_refs, v_refs, m_ref, l_ref = refs[:count], refs[count : 2 * count], refs[-2], refs[-1]
    factor = LOG2E
    mixed = []
    for head in range(q_ref.shape[-1] // HD):
        cols = slice(head * HD, head * HD + HD)
        q = q_ref[0][:, cols]
        scores = [dot_nt(k[0][:, cols], q) for k in k_refs]
        top = functools.reduce(jnp.maximum, [jnp.max(s, axis=0, keepdims=True) for s in scores])
        base = top * factor
        expo = [jnp.exp2(s * factor - base) for s in scores]
        total = functools.reduce(jnp.add, [jnp.sum(e, axis=0, keepdims=True) for e in expo])
        inverse = 1.0 / total
        mixed.append(
            functools.reduce(
                jnp.add, [dot_tn((e * inverse).astype(BF), v[0][:, cols]) for e, v in zip(expo, v_refs)]
            )
        )
        l_ref[0, 0, head : head + 1, :] = base + jnp.log2(total)
    m_ref[...] = jnp.concatenate(mixed, axis=1).astype(BF)


def attend_forward(qkv, other):
    _, rows, width = qkv.shape
    span = min(rows, LEN)
    number = rows // span
    pairs = width // (2 * HD)
    one = lambda place: pl.BlockSpec((1, span, 2 * HD), lambda n, h: (place, n, h))
    sources = [qkv] if other is None else [qkv, other]
    keys = [one(1)] + ([one(0)] if other is not None else [])
    values = [one(2)] + ([one(1)] if other is not None else [])
    count = len(sources)
    return call(
        functools.partial(attend_kernel, count),
        (number, pairs),
        [one(0)] + keys + values,
        (
            pl.BlockSpec((span, 2 * HD), lambda n, h: (n, h)),
            pl.BlockSpec((1, 1, 2, span), lambda n, h: (n, h, 0, 0)),
        ),
        (
            jax.ShapeDtypeStruct((rows, width), BF),
            jax.ShapeDtypeStruct((number, pairs, 2, span), F32),
        ),
        [],
        4 * rows * LEN * width * 4,
        2 * rows * width * 6,
        exps=rows * LEN * (width // HD),
    )(qkv, *sources, *sources)


def attend_back_kernel(count, q_ref, *refs):
    k_refs, v_refs = refs[:count], refs[count : 2 * count]
    dm_ref, l_ref, dq_ref = refs[2 * count : 2 * count + 3]
    out_refs = refs[2 * count + 3 :]
    dqs, dks, dvs = [], [[] for _ in range(count)], [[] for _ in range(count)]
    for head in range(q_ref.shape[-1] // HD):
        cols = slice(head * HD, head * HD + HD)
        q = q_ref[0][:, cols]
        dm = dm_ref[...][:, cols]
        base = l_ref[0, 0, head : head + 1, :]
        weights = [jnp.exp2(dot_nt(k[0][:, cols], q) * LOG2E - base) for k in k_refs]
        grads = [dot_nt(v[0][:, cols], dm) for v in v_refs]
        inner = functools.reduce(
            jnp.add, [jnp.sum(w * g, axis=0, keepdims=True) for w, g in zip(weights, grads)]
        )
        dq = None
        for i in range(count):
            ds = (weights[i] * (grads[i] - inner)).astype(BF)
            part = dot_tn(ds, k_refs[i][0][:, cols])
            dq = part if dq is None else dq + part
            dks[i].append(dot_nn(ds, q))
            dvs[i].append(dot_nn(weights[i].astype(BF), dm))
        dqs.append(dq)
    dq_ref[...] = (jnp.concatenate(dqs, axis=1).astype(BF).astype(F32) * SCALE).astype(BF)
    for i in range(count):
        out_refs[i][0] = jnp.concatenate(dks[i], axis=1).astype(out_refs[i].dtype)
        out_refs[i][1] = jnp.concatenate(dvs[i], axis=1).astype(out_refs[i].dtype)


def attend_backward(qkv, other, dm, logs):
    _, rows, width = qkv.shape
    span = min(rows, LEN)
    number = rows // span
    pairs = width // (2 * HD)
    one = lambda place: pl.BlockSpec((1, span, 2 * HD), lambda n, h: (place, n, h))
    flat = pl.BlockSpec((span, 2 * HD), lambda n, h: (n, h))
    both = pl.BlockSpec((2, span, 2 * HD), lambda n, h: (0, n, h))
    sources = [qkv] if other is None else [qkv, other]
    keys = [one(1)] + ([one(0)] if other is not None else [])
    values = [one(2)] + ([one(1)] if other is not None else [])
    count = len(sources)
    outs = [jax.ShapeDtypeStruct((2, rows, width), F32 if other is not None else BF)]
    if other is not None:
        outs.append(jax.ShapeDtypeStruct((2, rows, width), BF))
    return call(
        functools.partial(attend_back_kernel, count),
        (number, pairs),
        [one(0)] + keys + values + [flat, pl.BlockSpec((1, 1, 2, span), lambda n, h: (n, h, 0, 0))],
        tuple([flat] + [both] * count),
        tuple([jax.ShapeDtypeStruct((rows, width), BF)] + outs),
        [],
        10 * rows * LEN * width * 4,
        2 * rows * width * 12,
        exps=rows * LEN * (width // HD),
    )(qkv, *sources, *sources, dm, logs)


OUT_BIAS, FIRST_GAIN, FIRST_SHIFT, DOWN_BIAS, SECOND_GAIN, SECOND_SHIFT = range(6)


def vector(ref, place):
    return ref[place : place + 1, :]


def normed(hidden):
    average = jnp.mean(hidden, axis=-1, keepdims=True)
    center = hidden - average
    spread = jnp.mean(center * center, axis=-1, keepdims=True)
    inverse = lax.rsqrt(spread + EPSILON)
    return center * inverse, inverse


def norm_back(grad, z, inverse, gain):
    scaled = grad * gain
    average = jnp.mean(scaled, axis=-1, keepdims=True)
    along = jnp.mean(scaled * z, axis=-1, keepdims=True)
    return (scaled - average - z * along) * inverse


def total_rows(value):
    return jnp.sum(value, axis=0, keepdims=True)


def add_sums(ref, first, rows):
    value = jnp.concatenate(rows + [jnp.zeros((8 - len(rows), rows[0].shape[1]), F32)], axis=0)

    @pl.when(first)
    def _():
        ref[...] = value

    @pl.when(jnp.logical_not(first))
    def _():
        ref[...] += value


def accumulate(acc_ref, step, value):
    @pl.when(step == 0)
    def _():
        acc_ref[...] = value

    @pl.when(step > 0)
    def _():
        acc_ref[...] += value


def first_norm_kernel(count, m_ref, *refs):
    w_refs = refs[:count]
    x_ref, vec_ref, z_ref, r_ref, y_ref, acc_ref = refs[count:]
    step = pl.program_id(1)
    accumulate(acc_ref, step, dot_nt(m_ref[...], joined(w_refs)))

    @pl.when(step == pl.num_programs(1) - 1)
    def _():
        hidden = x_ref[...].astype(F32) + acc_ref[...] + vector(vec_ref, OUT_BIAS)
        z, inverse = normed(hidden)
        z_ref[...] = z
        r_ref[...] = inverse
        y_ref[...] = (z * vector(vec_ref, FIRST_GAIN) + vector(vec_ref, FIRST_SHIFT)).astype(BF)


def first_norm(mixed, slots, x, vectors):
    rows, width = x.shape
    tile = row_tile(rows)
    parts, cols = slots[0].shape[1], slots[0].shape[-1]
    specs = [
        pl.BlockSpec((s.shape[0], 1, 1, s.shape[3], cols), lambda i, z: (0, z, 3, 0, 0)) for s in slots
    ]
    flat = pl.BlockSpec((tile, width), lambda i, z: (i, 0))
    return call(
        functools.partial(first_norm_kernel, len(slots)),
        (rows // tile, parts),
        [pl.BlockSpec((tile, cols), lambda i, z: (i, z))] + specs + [flat, whole_spec(vectors.shape)],
        (flat, pl.BlockSpec((tile, 1), lambda i, z: (i, 0)), flat),
        (
            jax.ShapeDtypeStruct((rows, width), F32),
            jax.ShapeDtypeStruct((rows, 1), F32),
            jax.ShapeDtypeStruct((rows, width), BF),
        ),
        [pltpu.VMEM((tile, width), F32)],
        2 * rows * width * width,
        2 * (rows * width * 5 + width * width),
    )(mixed, *slots, x, vectors)


def up_kernel(count, y_ref, *refs):
    w_refs, bias_ref, g_ref, slope_ref = refs[:count], refs[count], refs[count + 1], refs[count + 2]
    upper = dot_nn(y_ref[...], joined(w_refs)) + bias_ref[...]
    half = 0.5 + 0.5 * lax.erf(upper * (0.5**0.5))
    g_ref[...] = (upper * half).astype(BF)
    bell = jnp.exp(upper * upper * -0.5) * ((2 * math.pi) ** -0.5)
    slope_ref[...] = (half + upper * bell).astype(BF)


def up_gelu(y, slots, bias):
    rows, width = y.shape
    parts, full = slots[0].shape[1], slots[0].shape[-1]
    cols = min(512, full)
    per = full // cols
    tile = row_tile(rows)
    specs = [
        pl.BlockSpec((s.shape[0], 1, s.shape[2], cols), lambda i, z: (0, z // per, 0, z % per)) for s in slots
    ]
    out = pl.BlockSpec((tile, cols), lambda i, z: (i, z))
    shape = jax.ShapeDtypeStruct((rows, parts * full), BF)
    return call(
        functools.partial(up_kernel, len(slots)),
        (rows // tile, parts * per),
        [pl.BlockSpec((tile, width), lambda i, z: (i, 0))]
        + specs
        + [pl.BlockSpec((1, cols), lambda i, z: (0, z))],
        (out, out),
        (shape, shape),
        [],
        2 * rows * width * parts * full,
        2 * (rows * width + 2 * rows * parts * full + width * parts * full),
        exps=2 * rows * parts * full,
    )(y, *slots, bias)


def second_norm_kernel(count, g_ref, *refs):
    w_refs = refs[:count]
    z1_ref, c_ref, vec_ref, out_ref, dh_ref, b_ref, sum_ref, acc_ref = refs[count:]
    step = pl.program_id(1)
    first = pl.program_id(0) == 0
    accumulate(acc_ref, step, dot_nt(g_ref[...], joined(w_refs)))

    @pl.when(step == pl.num_programs(1) - 1)
    def _():
        y1 = z1_ref[...] * vector(vec_ref, FIRST_GAIN) + vector(vec_ref, FIRST_SHIFT)
        hidden = y1 + acc_ref[...] + vector(vec_ref, DOWN_BIAS)
        z, inverse = normed(hidden)
        gain = vector(vec_ref, SECOND_GAIN)
        out_ref[...] = (z * gain + vector(vec_ref, SECOND_SHIFT)).astype(BF)
        grad = c_ref[...].astype(F32)
        dh = norm_back(grad, z, inverse, gain)
        dh_ref[...] = dh
        b_ref[...] = dh.astype(BF)
        add_sums(sum_ref, first, [total_rows(grad * z), total_rows(grad), total_rows(dh)])


def second_norm(gated, slots, z1, cot, vectors):
    rows, width = z1.shape
    tile = row_tile(rows)
    parts, cols = slots[0].shape[1], slots[0].shape[-1]
    specs = [pl.BlockSpec((s.shape[0], 1, s.shape[2], cols), lambda i, z: (0, z, 0, 0)) for s in slots]
    flat = pl.BlockSpec((tile, width), lambda i, z: (i, 0))
    return call(
        functools.partial(second_norm_kernel, len(slots)),
        (rows // tile, parts),
        [pl.BlockSpec((tile, cols), lambda i, z: (i, z))]
        + specs
        + [flat, flat, whole_spec(vectors.shape)],
        (flat, flat, flat, whole_spec((8, width))),
        (
            jax.ShapeDtypeStruct((rows, width), BF),
            jax.ShapeDtypeStruct((rows, width), F32),
            jax.ShapeDtypeStruct((rows, width), BF),
            jax.ShapeDtypeStruct((8, width), F32),
        ),
        [pltpu.VMEM((tile, width), F32)],
        2 * rows * width * parts * cols,
        2 * (rows * width * 7 + (rows + width) * parts * cols),
    )(gated, *slots, z1, cot, vectors)


def gate_back_kernel(count, b_ref, *refs):
    w_refs, slope_ref, du_ref, sum_ref = refs[:count], refs[count], refs[count + 1], refs[count + 2]
    grad = dot_nn(b_ref[...], joined(w_refs))
    low = (grad * slope_ref[...].astype(F32)).astype(BF)
    du_ref[...] = low
    value = total_rows(low.astype(F32))
    first = pl.program_id(1) == 0

    @pl.when(first)
    def _():
        sum_ref[...] = value

    @pl.when(jnp.logical_not(first))
    def _():
        sum_ref[...] += value


def gate_back(b, slots, slope):
    rows, width = b.shape
    parts, full = slots[0].shape[1], slots[0].shape[-1]
    cols = min(512, full)
    per = full // cols
    tile = row_tile(rows)
    specs = [
        pl.BlockSpec((s.shape[0], 1, s.shape[2], cols), lambda z, i: (0, z // per, 0, z % per)) for s in slots
    ]
    out = pl.BlockSpec((tile, cols), lambda z, i: (i, z))
    return call(
        functools.partial(gate_back_kernel, len(slots)),
        (parts * per, rows // tile),
        [pl.BlockSpec((tile, width), lambda z, i: (i, 0))] + specs + [out],
        (out, pl.BlockSpec((1, cols), lambda z, i: (0, z))),
        (
            jax.ShapeDtypeStruct((rows, parts * full), BF),
            jax.ShapeDtypeStruct((1, parts * full), F32),
        ),
        [],
        2 * rows * width * parts * full,
        2 * (rows * width + 2 * rows * parts * full + width * parts * full),
    )(b, *slots, slope)


def first_back_kernel(count, du_ref, *refs):
    w_refs = refs[:count]
    dh2_ref, z1_ref, r1_ref, vec_ref, dh_ref, b_ref, sum_ref, acc_ref = refs[count:]
    step = pl.program_id(1)
    first = pl.program_id(0) == 0
    accumulate(acc_ref, step, dot_nt(du_ref[...], joined(w_refs)))

    @pl.when(step == pl.num_programs(1) - 1)
    def _():
        grad = acc_ref[...] + dh2_ref[...]
        z = z1_ref[...]
        dh = norm_back(grad, z, r1_ref[...], vector(vec_ref, FIRST_GAIN))
        dh_ref[...] = dh
        b_ref[...] = dh.astype(BF)
        add_sums(sum_ref, first, [total_rows(grad * z), total_rows(grad), total_rows(dh)])


def first_back(du, slots, dh2, z1, r1, vectors):
    rows, width = z1.shape
    tile = row_tile(rows)
    parts, cols = slots[0].shape[1], slots[0].shape[-1]
    specs = [pl.BlockSpec((s.shape[0], 1, s.shape[2], cols), lambda i, z: (0, z, 0, 0)) for s in slots]
    flat = pl.BlockSpec((tile, width), lambda i, z: (i, 0))
    return call(
        functools.partial(first_back_kernel, len(slots)),
        (rows // tile, parts),
        [pl.BlockSpec((tile, cols), lambda i, z: (i, z))]
        + specs
        + [flat, flat, pl.BlockSpec((tile, 1), lambda i, z: (i, 0)), whole_spec(vectors.shape)],
        (flat, flat, whole_spec((8, width))),
        (
            jax.ShapeDtypeStruct((rows, width), F32),
            jax.ShapeDtypeStruct((rows, width), BF),
            jax.ShapeDtypeStruct((8, width), F32),
        ),
        [pltpu.VMEM((tile, width), F32)],
        2 * rows * width * parts * cols,
        2 * (rows * width * 8 + (rows + width) * parts * cols),
    )(du, *slots, dh2, z1, r1, vectors)


def input_back_kernel(count, dq_ref, dkv_ref, *refs):
    w_refs = refs[:count]
    dh_ref, out_ref, acc_ref = refs[count:]
    step = pl.program_id(1)
    value = dot_nt(dq_ref[...], joined(w_refs, 0))
    value += dot_nt(dkv_ref[0], joined(w_refs, 1))
    value += dot_nt(dkv_ref[1], joined(w_refs, 2))
    accumulate(acc_ref, step, value)

    @pl.when(step == pl.num_programs(1) - 1)
    def _():
        out_ref[...] = (acc_ref[...] + dh_ref[...]).astype(BF)


def input_back(dq, dkv, slots, dh1):
    rows, width = dh1.shape
    tile = row_tile(rows)
    parts, kinds, cols = slots[0].shape[1], slots[0].shape[2], slots[0].shape[-1]
    specs = [
        pl.BlockSpec((s.shape[0], 1, kinds, s.shape[3], cols), lambda i, z: (0, z, 0, 0, 0)) for s in slots
    ]
    flat = pl.BlockSpec((tile, width), lambda i, z: (i, 0))
    return call(
        functools.partial(input_back_kernel, len(slots)),
        (rows // tile, parts),
        [
            pl.BlockSpec((tile, cols), lambda i, z: (i, z)),
            pl.BlockSpec((2, tile, cols), lambda i, z: (0, i, z)),
        ]
        + specs
        + [flat],
        flat,
        jax.ShapeDtypeStruct((rows, width), BF),
        [pltpu.VMEM((tile, width), F32)],
        6 * rows * width * parts * cols,
        2 * (rows * width * 6 + 4 * width * parts * cols),
    )(dq, dkv, *slots, dh1)


def outer_kernel(left_ref, right_ref, out_ref):
    shape = out_ref.shape
    right = right_ref[...].reshape(right_ref.shape[-2:])
    out_ref[...] = dot_tn(left_ref[...], right).astype(BF).reshape(shape)


def outer(left, right, begin, count, depth, parts):
    rows = left.shape[0]
    cols = right.shape[-1] // parts
    return call(
        outer_kernel,
        (parts,),
        [
            pl.BlockSpec((rows, count * depth), lambda z: (0, begin // count)),
            pl.BlockSpec((rows, cols), lambda z: (0, z)),
        ],
        pl.BlockSpec((count, 1, depth, cols), lambda z: (0, z, 0, 0)),
        jax.ShapeDtypeStruct((count, parts, depth, parts * cols // parts), BF),
        [],
        2 * rows * count * depth * parts * cols,
        2 * (rows * (count * depth + parts * cols) + count * depth * parts * cols),
    )(left, right)


def outer_stack(left, stack, begin, count, depth, parts):
    rows = left.shape[0]
    kinds = stack.shape[0]
    cols = stack.shape[-1] // parts
    return call(
        outer_kernel,
        (kinds, parts),
        [
            pl.BlockSpec((rows, count * depth), lambda k, z: (0, begin // count)),
            pl.BlockSpec((1, rows, cols), lambda k, z: (k, 0, z)),
        ],
        pl.BlockSpec((count, 1, 1, depth, cols), lambda k, z: (0, z, k, 0, 0)),
        jax.ShapeDtypeStruct((count, parts, kinds, depth, cols), BF),
        [],
        2 * rows * count * depth * parts * cols * kinds,
        2 * kinds * (rows * (count * depth + parts * cols) + count * depth * parts * cols),
    )(left, stack)


class Links:
    def __init__(self, count, parts):
        self.count, self.parts = count, parts
        self.cube = count == 8
        self.place = lax.axis_index("dp")
        self.core = self.place % 2
        if self.cube:
            masks = [[0, 2, 4, 6, 1, 5, 3, 7], [0, 4, 2, 6, 1, 3, 5, 7]]
        else:
            masks = None
        if masks is None:
            self.owner = jnp.arange(count)
            self.inverse = jnp.arange(count)
        else:
            table = jnp.asarray(masks, jnp.int32)
            back = jnp.asarray([list(np.argsort(m)) for m in masks], jnp.int32)
            self.owner = table[self.core] ^ self.place
            self.inverse = back[self.core][jnp.arange(count) ^ self.place]

    def pairs(self, flip):
        out = []
        for place in range(self.count):
            for z in range(self.parts):
                out.append((place * self.parts + z, flip(place) * self.parts + z))
        return out

    def core_pairs(self):
        return self.pairs(lambda place: place ^ 1)

    def first_pairs(self):
        return self.pairs(lambda place: place ^ (4 if place % 2 else 2))

    def second_pairs(self):
        return self.pairs(lambda place: place ^ (2 if place % 2 else 4))

    def gather(self, local):
        block = lax.all_gather(local, "tensor", axis=0, tiled=False)
        if not self.cube:
            return [lax.all_gather(block, "dp", axis=0, tiled=False)]
        blocks = [block[None]]
        for pairs in (self.first_pairs(), self.second_pairs(), self.core_pairs()):
            blocks = blocks + [lax.ppermute(b, AXES, pairs) for b in blocks]
        return blocks

    def scatter(self, make):
        if not self.cube:
            full = lax.psum_scatter(make(0, self.count), "dp", scatter_dimension=0, tiled=False)
            return lax.psum_scatter(full, "tensor", scatter_dimension=0, tiled=False)
        far = lax.ppermute(make(4, 4), AXES, self.core_pairs())
        held = make(0, 4)
        away = summed(held[2:4], far[2:4])
        held = summed(held[0:2], far[0:2])
        far = lax.ppermute(away, AXES, self.second_pairs())
        away = summed(held[1:2], far[1:2])
        held = summed(held[0:1], far[0:1])
        far = lax.ppermute(away, AXES, self.first_pairs())
        held = summed(held, far)
        return lax.psum_scatter(held[0], "tensor", scatter_dimension=0, tiled=False)

    def row_pairs(self, second):
        half = self.parts // 2
        out = []
        for place in range(self.count):
            for z in range(self.parts):
                micro = (z + second) % 2
                target = (place // 2 * 2 + z // half) * self.parts + micro * half + place % 2
                out.append((place * self.parts + z, target))
        return out

    def rows_in(self, local):
        parity = lax.axis_index("tensor") % 2
        first = lax.dynamic_index_in_dim(local, parity, 0, keepdims=False)
        second = lax.dynamic_index_in_dim(local, 1 - parity, 0, keepdims=False)
        return jnp.concatenate(
            [
                lax.ppermute(first, AXES, self.row_pairs(0)),
                lax.ppermute(second, AXES, self.row_pairs(1)),
            ],
            axis=0,
        )

    def rows_out(self, held):
        parity = lax.axis_index("tensor") % 2
        rows = held.shape[0] // 2
        back = lambda second: [(b, a) for a, b in self.row_pairs(second)]
        first = lax.ppermute(held[:rows], AXES, back(0))
        second = lax.ppermute(held[rows:], AXES, back(1))
        swap = parity == 1
        return jnp.stack([jnp.where(swap, second, first), jnp.where(swap, first, second)])

    def total(self, value):
        step = 1
        while step < self.count:
            pairs = self.pairs(lambda place: place ^ step)
            value = value + lax.ppermute(value, AXES, pairs)
            step *= 2
        step = 1
        while step < self.parts:
            pairs = [
                (p * self.parts + z, p * self.parts + (z ^ step))
                for p in range(self.count)
                for z in range(self.parts)
            ]
            value = value + lax.ppermute(value, AXES, pairs)
            step *= 2
        return value


def summed(left, right):
    return (left.astype(F32) + right.astype(F32)).astype(BF)


def shards(
    inputs,
    query_weight,
    query_bias,
    key_weight,
    value_weight,
    value_bias,
    out_weight,
    out_bias,
    first_gain,
    first_shift,
    up_weight,
    up_bias,
    down_weight,
    down_bias,
    second_gain,
    second_shift,
    cotangent,
):
    count, parts = lax.axis_size("dp"), lax.axis_size("tensor")
    links = Links(count, parts)
    tensor_place = lax.axis_index("tensor")
    width = inputs.shape[-1]
    depth = width // count
    hidden = up_weight.shape[1] * parts

    source = jnp.repeat(links.owner, depth) * depth + jnp.tile(jnp.arange(depth), count)
    shuffle = (jnp.arange(width)[:, None] == source[None, :]).astype(BF)

    def ordered(rows):
        return dot_nn(rows, shuffle).astype(BF)

    def restored(rows):
        return dot_nt(rows, shuffle).astype(BF)

    def restored_vectors(rows):
        return rows.reshape(-1, count, depth)[:, links.inverse].reshape(-1, width)

    vectors = jnp.stack(
        [out_bias, first_gain, first_shift, down_bias, second_gain, second_shift]
        + [jnp.zeros_like(out_bias)] * 2
    )
    vectors = vectors.reshape(8, count, depth)[:, links.owner].reshape(8, width)

    shared = jnp.stack([query_weight, key_weight, value_weight, out_weight.T])
    att_slots = links.gather(shared)
    biases = lax.all_gather(
        jnp.concatenate([query_bias, value_bias, up_bias]), "tensor", axis=0, tiled=False
    )
    local = query_bias.shape[0]
    query_full = biases[:, :local].reshape(1, 1, -1)
    value_full = biases[:, local : 2 * local].reshape(1, 1, -1)
    up_full = biases[:, 2 * local :].reshape(1, -1)
    qkv_bias = jnp.concatenate([query_full, jnp.zeros_like(query_full), value_full], axis=0)
    x = ordered(links.rows_in(inputs))
    up_slots = links.gather(up_weight)
    cot = ordered(links.rows_in(cotangent))
    down_slots = links.gather(down_weight.T)

    qkv = project_qkv(x, att_slots, qkv_bias)
    share = x.shape[0] < LEN
    other = lax.ppermute(qkv[1:], AXES, links.core_pairs()) if share else None
    mixed, logs = attend_forward(qkv, other)
    z1, r1, y1 = first_norm(mixed, att_slots, x, vectors)
    gated, slope = up_gelu(y1, up_slots, up_full)
    out, dh2, b2, second_sums = second_norm(gated, down_slots, z1, cot, vectors)
    outputs = links.rows_out(restored(out))

    down_grad = links.scatter(lambda begin, n: outer(b2, gated, begin, n, depth, parts))
    du, up_bias_sum = gate_back(b2, down_slots, slope)
    up_grad = links.scatter(lambda begin, n: outer(y1, du, begin, n, depth, parts))
    dh1, b1, first_sums = first_back(du, up_slots, dh2, z1, r1, vectors)
    dm = project_back(b1, att_slots, 3)
    out_grad = links.scatter(lambda begin, n: outer(b1, mixed, begin, n, depth, parts))
    back = attend_backward(qkv, other, dm, logs)
    if share:
        dq, near, far = back
        dkv = (near + lax.ppermute(far, AXES, links.core_pairs()).astype(F32)).astype(BF)
    else:
        dq, dkv = back
    dx = input_back(dq, dkv, att_slots, dh1)
    input_grad = links.rows_out(restored(dx)).astype(F32)

    def qkv_outer(begin, n):
        return jnp.concatenate(
            [
                outer_stack(x, dq[None], begin, n, depth, parts),
                outer_stack(x, dkv, begin, n, depth, parts),
            ],
            axis=2,
        )

    qkv_grad = links.scatter(qkv_outer).astype(F32)

    sums = jnp.concatenate(
        [
            restored_vectors(jnp.concatenate([first_sums[:3], second_sums[:3]])),
            up_bias_sum.reshape(-1, width),
            jnp.sum(dq.astype(F32), axis=0, keepdims=True),
            jnp.sum(dkv[1].astype(F32), axis=0, keepdims=True),
        ]
    )
    sums = links.total(sums)
    wide = hidden // width

    def mine(vector_sum):
        size = vector_sum.shape[0] // parts
        return lax.dynamic_slice_in_dim(vector_sum, tensor_place * size, size)

    return (
        outputs,
        input_grad,
        qkv_grad[0],
        mine(sums[6 + wide]),
        qkv_grad[1],
        qkv_grad[2],
        mine(sums[7 + wide]),
        out_grad.astype(F32).T,
        sums[2],
        sums[0],
        sums[1],
        up_grad.astype(F32),
        mine(sums[6 : 6 + wide].reshape(-1)),
        down_grad.astype(F32).T,
        sums[5],
        sums[3],
        sums[4],
    )


def solution(mesh):
    rows = P(None, ("dp", "tensor"), None)
    return jax.shard_map(
        shards,
        mesh=mesh,
        in_specs=(
            rows,
            P("dp", "tensor"),
            P("tensor"),
            P("dp", "tensor"),
            P("dp", "tensor"),
            P("tensor"),
            P("tensor", "dp"),
            P(),
            P(),
            P(),
            P("dp", "tensor"),
            P("tensor"),
            P("tensor", "dp"),
            P(),
            P(),
            P(),
            rows,
        ),
        out_specs=(
            rows,
            rows,
            P("dp", "tensor"),
            P("tensor"),
            P("dp", "tensor"),
            P("dp", "tensor"),
            P("tensor"),
            P("tensor", "dp"),
            P(),
            P(),
            P(),
            P("dp", "tensor"),
            P("tensor"),
            P("tensor", "dp"),
            P(),
            P(),
            P(),
        ),
        check_vma=False,
    )
```

time: 1260 us -> 552 us (0.44)
  waiting for transfers between devices: 827 us -> 176 us
  matrix products: 224 us -> 9.91 us
  Pallas kernels: 0 us -> 164 us
  starting transfers between devices: 2.92 us -> 57.2 us
  blocking collectives: 80.2 us -> 51 us
  other arithmetic: 67.7 us -> 47.6 us
    reduce_scatter x14 -> x4, waiting for transfers between devices: 567 us -> 0.01 us  [scatter(): return lax.psum_scatter(held[0], 'tensor', scatter_dimension=0, tiled=False)]
    all_gather x10 -> x3, waiting for transfers between devices: 257 us -> 29.3 us  [gather(): block = lax.all_gather(local, 'tensor', axis=0, tiled=False)]
    dot_general x48 -> x4, matrix products: 224 us -> 9.91 us  [the longest x2 6 us: dot_nn(): return jnp.dot(left, right, preferred_element_type=F32)]
    pallas_call x0 -> x20, Pallas kernels: none -> 164 us  [the longest x1 31 us: attend_backward(): call(functools.partial(attend_back_kernel, count), (number, pairs), [one(...]
    ppermute x0 -> x48, waiting for transfers between devices: none -> 147 us  [the longest x21 62.5 us: gather(): blocks = blocks + [lax.ppermute(b, AXES, pairs) for b in blocks]]
    ppermute x0 -> x48, starting transfers between devices: none -> 56.9 us  [the longest x21 12.9 us: gather(): blocks = blocks + [lax.ppermute(b, AXES, pairs) for b in blocks]]
    psum x1 -> x0, blocking collectives: 41.7 us -> none  [shards(): lax.psum((query_bias_full, value_bias_full, up_bias_full, small_total[3],...]
    reduce_sum x13 -> x2, other arithmetic: 32.1 us -> 0.36 us  [the longest x1 0.18 us: shards(): jnp.sum(dq.astype(F32), axis=0, keepdims=True)]
  transfers between devices with their start and end apart: 24 -> 55, of which waited for: 20 -> 17; matrix products, arithmetic and copies ran while one was open for 19% -> 13% of each run, Pallas kernels for 0% -> 17%
where the time goes in v1:
time: 552 us; the launch traced here: 546 us
  waiting for transfers between devices  176 us (32%)
  Pallas kernels  164 us (30%)
  starting transfers between devices  57.2 us (10%)
  blocking collectives  51 us (9%)
  other arithmetic  47.6 us (9%)
  local copies, waits for them, and re-layouts  24.4 us (4%)
  between operations  15.2 us (3%)
  matrix products  9.91 us (2%)
    ppermute x21, waiting for transfers between devices, gather(): blocks = blocks + [lax.ppermute(b, AXES, pairs) for b in blocks]  62.5 us
    all_gather x1, blocking collectives, shards(): lax.all_gather(jnp.concatenate([query_bias, value_bias, up_bias]), 'tenso...  51 us
    pallas_call x1, Pallas kernels, attend_backward(): call(functools.partial(attend_back_kernel, count), (number, pairs), [one(...  31 us
    all_gather x3, waiting for transfers between devices, gather(): block = lax.all_gather(local, 'tensor', axis=0, tiled=False)  29.3 us
    pallas_call x6, Pallas kernels, outer(): call(outer_kernel, (parts,), [pl.BlockSpec((rows, count * depth), lambda...  25.4 us
    convert_element_type x8, other arithmetic, summed(): return (left.astype(F32) + right.astype(F32)).astype(BF)  23.1 us
    ppermute x4, waiting for transfers between devices, scatter(): far = lax.ppermute(away, AXES, self.first_pairs())  21.6 us
    pallas_call x1, Pallas kernels, attend_forward(): call(functools.partial(attend_kernel, count), (number, pairs), [one(0)] +...  20.8 us
  transfers between devices with their start and end apart: 55, of which 17 were waited for; matrix products, arithmetic and copies ran while one was open for 13% of the time, Pallas kernels for 17%

profile of v1, /device:TPU:8, one launch (start us, length us, event | category | flops | bytes accessed | tf_op | source)
XLA Modules:
  0.0 545.6 jit_solution(14796529064068752862)
XLA Ops:
  10.0 29.3 %all-gather.9.cloned.1.call-done = bf16[16,128,256]{2,1,0:T(8,128)(2,1)} async-done(((bf16[4,128,256]{2,1,0:T(8,128)(2,1)}), bf16[16,128,256]{2,1,0:T(8,128)(2,1)}) %all-gather.9.cloned.1.call-update) | async-done | bytes 1048592 | tf_op jit(solution)/shard_map/all_gather | solution.py:589
  42.3 23.2 %collective-permute-done.2.refs_1_ = bf16[1,4,4,128,256]{4,3,2,1,0:T(8,128)(2,1)S(1)} collective-permute-done((bf16[1,4,4,128,256]{4,3,2,1,0:T(8,128)(2,1)}, bf16[1,4,4,128,256]{4,3,2,1,0:T(8,128)(2,1)S(1)}, u32[]{:S(2)}, u32[]{:S(2)}) %collective-permute-start.2) | collective-permute-done | bytes 1048608 | tf_op jit(solution)/shard_map/ppermute | solution.py:594
  66.1 2.3 dynamic-slice_bitcast_fusion.3
  69.1 2.5 collective-permute-start
  72.6 4.9 collective-permute-start.25
  77.6 3.9 collective-permute-done.1
  81.4 6.1 %collective-permute-start.24 = (bf16[256,1024]{1,0:T(8,128)(2,1)}, bf16[256,1024]{1,0:T(8,128)(2,1)}, u32[]{:S(2)}, u32[]{:S(2)}) collective-permute-start(bf16[256,1024]{1,0:T(8,128)(2,1)} %get-tuple-element.122), channel_id=1, source_target_pairs={{0,0},{1,2},{2,4},{3,6},{4,1},{5,3},{6,5},{7,7},{8,8},{9,10},{10,1... | collective-permute-start | bytes 1572872 | tf_op jit(solution)/shard_map/ppermute | solution.py:628
  87.6 51.0 %all-gather.4 = f32[4,1,1536]{2,1,0:T(1,128)S(1)} all-gather(f32[1,1,1536]{2,1,0:T(1,128)S(1)} %reshape.198), channel_id=3, replica_groups=mesh['dp'=8,'tensor'=4] {'tensor'}, dimensions={0}, use_global_device_ids=true | all-gather | bytes 30720 | tf_op jit(solution)/shard_map/all_gather | solution.py:711
  139.8 1.7 collective-permute-start.10
  141.8 2.5 fusion.9.x_ref.refs_8_.left_ref
  144.3 2.6 copy.52
  149.3 10.6 %shard_map.314.q_ref.refs_0_.refs_2_ = bf16[3,512,1024]{2,1,0:T(8,128)(2,1)} custom-call(bf16[512,1024]{1,0:T(8,128)(2,1)S(1)} %fusion.9.x_ref.refs_8_.left_ref, bf16[1,4,4,128,256]{4,3,2,1,0:T(8,128)(2,1)S(1)} %bitcast.112, bf16[1,4,4,128,256]{4,3,2,1,0:T(8,128)(2,1)S(1)} %collective-permute-done.2.refs_1_, ...), custom_call_target="tpu_custom_call" | custom-call | flops 3221225472 | bytes 10485760 | tf_op jit(solution)/shard_map/pallas_call | solution.py:77
  160.0 3.1 slice.231
  163.1 10.2 %collective-permute-done.11.refs_2_ = bf16[1,4,128,1024]{3,2,1,0:T(8,128)(2,1)} collective-permute-done((bf16[1,4,128,1024]{3,2,1,0:T(8,128)(2,1)}, bf16[1,4,128,1024]{3,2,1,0:T(8,128)(2,1)}, u32[]{:S(2)}, u32[]{:S(2)}) %collective-permute-start.11) | collective-permute-done | bytes 1048608 | tf_op jit(solution)/shard_map/ppermute | solution.py:594
  174.2 9.0 %collective-permute-done.17.refs_1_ = bf16[1,4,128,1024]{3,2,1,0:T(8,128)(2,1)} collective-permute-done((bf16[1,4,128,1024]{3,2,1,0:T(8,128)(2,1)}, bf16[1,4,128,1024]{3,2,1,0:T(8,128)(2,1)}, u32[]{:S(2)}, u32[]{:S(2)}) %collective-permute-start.17) | collective-permute-done | bytes 1048608 | tf_op jit(solution)/shard_map/ppermute | solution.py:594
  183.1 4.5 collective-permute-done.18.refs_2_
  189.5 9.4 %collective-permute-done.12.refs_3_ = bf16[1,4,128,1024]{3,2,1,0:T(8,128)(2,1)S(1)} collective-permute-done((bf16[1,4,128,1024]{3,2,1,0:T(8,128)(2,1)}, bf16[1,4,128,1024]{3,2,1,0:T(8,128)(2,1)S(1)}, u32[]{:S(2)}, u32[]{:S(2)}) %collective-permute-start.12) | collective-permute-done | bytes 1048608 | tf_op jit(solution)/shard_map/ppermute | solution.py:594
  200.0 3.5 fusion.10.refs_9_
  204.0 6.3 %collective-permute-done.19.refs_3_ = bf16[1,4,128,1024]{3,2,1,0:T(8,128)(2,1)} collective-permute-done((bf16[1,4,128,1024]{3,2,1,0:T(8,128)(2,1)}, bf16[1,4,128,1024]{3,2,1,0:T(8,128)(2,1)}, u32[]{:S(2)}, u32[]{:S(2)}) %collective-permute-start.19) | collective-permute-done | bytes 1048608 | tf_op jit(solution)/shard_map/ppermute | solution.py:594
  211.0 20.8 %shard_map.315 = (bf16[512,1024]{1,0:T(8,128)(2,1)S(1)}, f32[1,8,2,512]{3,2,1,0:T(2,128)S(1)}) custom-call(bf16[3,512,1024]{2,1,0:T(8,128)(2,1)} %shard_map.314.q_ref.refs_0_.refs_2_, bf16[3,512,1024]{2,1,0:T(8,128)(2,1)} %shard_map.314.q_ref.refs_0_.refs_2_, bf16[2,512,1024]{2,1,0:T(8,128)(2,1)} %collective-permute-done.9.refs_1_.refs_3_, ...), custom_call_target="tpu_custom_call" | custom-call | flops 8589934592 | bytes 6291456 | tf_op jit(solution)/shard_map/pallas_call | solution.py:144
  231.8 6.8 %shard_map.316 = (f32[512,1024]{1,0:T(8,128)}, f32[512,1]{1,0:T(8,128)S(1)}, bf16[512,1024]{1,0:T(8,128)(2,1)S(1)}) custom-call(bf16[512,1024]{1,0:T(8,128)(2,1)S(1)} %get-tuple-element.36.m_ref.right_ref, bf16[1,4,4,128,256]{4,3,2,1,0:T(8,128)(2,1)S(1)} %bitcast.113, bf16[1,4,4,128,256]{4,3,2,1,0:T(8,128)(2,1)S(1)} %collective-permute-done.2.refs_1_, ...), custom_call_target="tpu_custom_call" | custom-call | flops 1073741824 | bytes 7340032 | tf_op jit(solution)/shard_map/pallas_call | solution.py:291
  239.6 12.4 %shard_map.317 = (bf16[512,4096]{1,0:T(8,128)(2,1)}, bf16[512,4096]{1,0:T(8,128)(2,1)}) custom-call(bf16[512,1024]{1,0:T(8,128)(2,1)S(1)} %get-tuple-element.37.y_ref.left_ref, bf16[1,4,128,1024]{3,2,1,0:T(8,128)(2,1)S(1)} %bitcast.121, bf16[1,4,128,1024]{3,2,1,0:T(8,128)(2,1)} %collective-permute-done.10.refs_1_, ...), custom_call_target="tpu_custom_call" | custom-call | flops 4294967296 | bytes 17825792 | tf_op jit(solution)/shard_map/pallas_call | solution.py:327
  253.6 12.4 %shard_map.318 = (bf16[512,1024]{1,0:T(8,128)(2,1)S(1)}, f32[512,1024]{1,0:T(8,128)}, bf16[512,1024]{1,0:T(8,128)(2,1)S(1)}, f32[8,1024]{1,0:T(8,128)S(1)}) custom-call(bf16[512,4096]{1,0:T(8,128)(2,1)} %get-tuple-element.38.g_ref.right_ref, bf16[1,4,128,1024]{3,2,1,0:T(8,128)(2,1)S(1)} %bitcast.126, ...), custom_call_target="tpu_custom_call" | custom-call | flops 4294967296 | bytes 19922944 | tf_op jit(solution)/shard_map/pallas_call | solution.py:369
  266.0 11.1 %shard_map.319 = (bf16[512,4096]{1,0:T(8,128)(2,1)}, f32[1,4096]{1,0:T(1,128)S(1)}) custom-call(bf16[512,1024]{1,0:T(8,128)(2,1)S(1)} %get-tuple-element.41.b_ref.left_ref, bf16[1,4,128,1024]{3,2,1,0:T(8,128)(2,1)S(1)} %bitcast.127, bf16[1,4,128,1024]{3,2,1,0:T(8,128)(2,1)} %collective-permute-done.17.refs_1_, bf16[1,4,128,1024]{3,2,1,0:T(8,128)(2,1)S(1)} %copy-done.11, ...), custom_call_target="tpu_custom_call" | custom-call | flops 4294967296 | bytes 17825792 | tf_op jit(solution)/shard_map/pallas_call | solution.py:415
  277.1 12.0 %shard_map.320 = (f32[512,1024]{1,0:T(8,128)}, bf16[512,1024]{1,0:T(8,128)(2,1)S(1)}, f32[8,1024]{1,0:T(8,128)S(1)}) custom-call(bf16[512,4096]{1,0:T(8,128)(2,1)} %get-tuple-element.43.du_ref.right_ref, bf16[1,4,128,1024]{3,2,1,0:T(8,128)(2,1)S(1)} %bitcast.122, bf16[1,4,128,1024]{3,2,1,0:T(8,128)(2,1)} %collective-permute-done.10.refs_1_, ...), custom_call_target="tpu_custom_call" | custom-call | flops 4294967296 | bytes 20971520 | tf_op jit(solution)/shard_map/pallas_call | solution.py:453
  289.1 3.5 shard_map.321.refs_4_
  292.6 31.0 %shard_map.322 = (bf16[512,1024]{1,0:T(8,128)(2,1)S(1)}, f32[2,512,1024]{2,1,0:T(8,128)}, bf16[2,512,1024]{2,1,0:T(8,128)(2,1)S(1)}) custom-call(bf16[3,512,1024]{2,1,0:T(8,128)(2,1)} %shard_map.314.q_ref.refs_0_.refs_2_, bf16[3,512,1024]{2,1,0:T(8,128)(2,1)} %shard_map.314.q_ref.refs_0_.refs_2_, ...), custom_call_target="tpu_custom_call" | custom-call | flops 21474836480 | bytes 12582912 | tf_op jit(solution)/shard_map/pallas_call | solution.py:207
  324.1 6.1 %shard_map.333 = bf16[4,4,128,1024]{3,2,1,0:T(8,128)(2,1)} custom-call(bf16[512,1024]{1,0:T(8,128)(2,1)S(1)} %get-tuple-element.41.b_ref.left_ref, bf16[512,4096]{1,0:T(8,128)(2,1)} %get-tuple-element.38.g_ref.right_ref), custom_call_target="tpu_custom_call" | custom-call | flops 2147483648 | bytes 8912896 | tf_op jit(solution)/shard_map/pallas_call | solution.py:519
  330.3 1.7 shard_map.326
  332.0 3.0 add_convert_fusion.4.dkv_ref.right_ref
  335.0 3.3 shard_map.327
  339.0 6.1 %shard_map.331 = bf16[4,4,128,1024]{3,2,1,0:T(8,128)(2,1)} custom-call(bf16[512,1024]{1,0:T(8,128)(2,1)S(1)} %get-tuple-element.37.y_ref.left_ref, bf16[512,4096]{1,0:T(8,128)(2,1)} %get-tuple-element.43.du_ref.right_ref), custom_call_target="tpu_custom_call" | custom-call | flops 2147483648 | bytes 8912896 | tf_op jit(solution)/shard_map/pallas_call | solution.py:519
  347.4 1.7 shard_map.324
  349.0 3.3 shard_map.325
  352.4 3.8 add_convert_fusion.6
  358.9 5.0 shard_map.332
  366.5 5.0 add_convert_fusion.1
  372.6 9.9 %collective-permute-done.40 = bf16[2,4,128,256]{3,2,1,0:T(8,128)(2,1)S(1)} collective-permute-done((bf16[2,4,128,256]{3,2,1,0:T(8,128)(2,1)S(1)}, bf16[2,4,128,256]{3,2,1,0:T(8,128)(2,1)S(1)}, u32[]{:S(2)}, u32[]{:S(2)}) %collective-permute-start.40) | collective-permute-done | bytes 524320 | tf_op jit(solution)/shard_map/ppermute | solution.py:605
  382.5 1.8 collective-permute-start.41
  384.3 2.2 add_convert_fusion.14
  386.8 5.0 shard_map.330
  391.8 2.0 copy-done.7
  394.7 5.9 %add_convert_fusion.3 = (bf16[2,4,128,1024]{3,2,1,0:T(8,128)(2,1)}, bf16[2,4,128,1024]{3,2,1,0:T(8,128)(2,1)}) fusion(bf16[4,4,128,1024]{3,2,1,0:T(8,128)(2,1)} %collective-permute-done.42, bf16[4,4,128,1024]{3,2,1,0:T(8,128)(2,1)} %copy-done.7), kind=kLoop, calls=%fused_computation.6 | loop fusion | flops 8388608 | bytes 12582912 | tf_op jit(solution)/shard_map/convert_element_type | solution.py:662
  401.7 7.1 %collective-permute-done.33 = bf16[1,4,3,128,256]{4,3,2,1,0:T(8,128)(2,1)} collective-permute-done((bf16[1,4,3,128,256]{4,3,2,1,0:T(8,128)(2,1)}, bf16[1,4,3,128,256]{4,3,2,1,0:T(8,128)(2,1)}, u32[]{:S(2)}, u32[]{:S(2)}) %collective-permute-start.33) | collective-permute-done | bytes 786464 | tf_op jit(solution)/shard_map/ppermute | solution.py:608
  408.8 2.6 fusion.21
  411.5 4.8 collective-permute-done.46
  416.3 2.9 add_convert_fusion.8
  419.2 1.7 collective-permute-start.47
  421.6 2.6 fusion.11
  425.2 4.6 collective-permute-start.27
  431.1 14.5 %collective-permute-done.47 = bf16[1,4,128,1024]{3,2,1,0:T(8,128)(2,1)} collective-permute-done((bf16[1,4,128,1024]{3,2,1,0:T(8,128)(2,1)}, bf16[1,4,128,1024]{3,2,1,0:T(8,128)(2,1)}, u32[]{:S(2)}, u32[]{:S(2)}) %collective-permute-start.47) | collective-permute-done | bytes 1048608 | tf_op jit(solution)/shard_map/ppermute | solution.py:608
  445.6 3.5 fusion.14
  453.0 1.8 collective-permute-start.44
  454.9 4.4 collective-permute-done.27
  463.0 6.2 %collective-permute-done.35 = f32[12,1024]{1,0:T(8,128)S(1)} collective-permute-done((f32[12,1024]{1,0:T(8,128)S(1)}, f32[12,1024]{1,0:T(8,128)S(1)}, u32[]{:S(2)}, u32[]{:S(2)}) %collective-permute-start.35) | collective-permute-done | bytes 49184 | tf_op jit(solution)/shard_map/ppermute | solution.py:647
  470.4 8.0 %shard_map.323 = bf16[512,1024]{1,0:T(8,128)(2,1)S(1)} custom-call(bf16[512,1024]{1,0:T(8,128)(2,1)S(1)} %get-tuple-element.48.dq_ref, bf16[2,512,1024]{2,1,0:T(8,128)(2,1)} %copy-done, bf16[1,4,4,128,256]{4,3,2,1,0:T(8,128)(2,1)S(1)} %bitcast.115, bf16[1,4,4,128,256]{4,3,2,1,0:T(8,128)(2,1)S(1)} %copy-done.6, ...), custom_call_target="tpu_custom_call" | custom-call | flops 3221225472 | bytes 14680064 | tf_op jit(solution)/shard_map/pallas_call | solution.py:493
  478.4 3.3 collective-permute-start.37
  481.8 2.9 fusion.13
  486.0 4.7 collective-permute-start.38
  490.9 3.1 collective-permute-start.30
  493.9 3.4 collective-permute-done.38
  501.3 15.5 %collective-permute-done.29 = bf16[256,1024]{1,0:T(8,128)(2,1)S(1)} collective-permute-done((bf16[256,1024]{1,0:T(8,128)(2,1)S(1)}, bf16[256,1024]{1,0:T(8,128)(2,1)S(1)}, u32[]{:S(2)}, u32[]{:S(2)}) %collective-permute-start.29) | collective-permute-done | bytes 524320 | tf_op jit(solution)/shard_map/ppermute | solution.py:639
  516.8 14.7 %collective-permute-done.30 = bf16[256,1024]{1,0:T(8,128)(2,1)S(1)} collective-permute-done((bf16[256,1024]{1,0:T(8,128)(2,1)S(1)}, bf16[256,1024]{1,0:T(8,128)(2,1)S(1)}, u32[]{:S(2)}, u32[]{:S(2)}) %collective-permute-start.30) | collective-permute-done | bytes 524320 | tf_op jit(solution)/shard_map/ppermute | solution.py:638
  536.8 1.8 bitcast_convert_fusion
  (222 shorter events, 54.1 us)
Async XLA Ops:
  7.2 64.4 %copy-start.18 = (bf16[2,256,1024]{2,1,0:T(8,128)(2,1)S(1)}, bf16[2,256,1024]{2,1,0:T(8,128)(2,1)}, u32[]{:S(2)}) copy-start(bf16[2,256,1024]{2,1,0:T(8,128)(2,1)} %param.35) | copy-start | bytes 3145732
  7.2 32.1 %all-gather.9.cloned.1.call-start = ((), (), s32[]{:S(2)}) async-start(), calls=%async_computation.8 | async-start | bytes 1310720 | tf_op jit(solution)/shard_map/all_gather | solution.py:589
  9.9 129.8 %all-gather.11.cloned.1.call-start = ((), (), s32[]{:S(2)}) async-start(), calls=%async_computation.9 | async-start | bytes 1310720 | tf_op jit(solution)/shard_map/all_gather | solution.py:589
  39.3 26.2 %collective-permute-start.2 = (bf16[1,4,4,128,256]{4,3,2,1,0:T(8,128)(2,1)}, bf16[1,4,4,128,256]{4,3,2,1,0:T(8,128)(2,1)S(1)}, u32[]{:S(2)}, u32[]{:S(2)}) collective-permute-start(bf16[1,4,4,128,256]{4,3,2,1,0:T(8,128)(2,1)} %bitcast.109), channel_id=1, source_target_pairs={{0,8},{1,9},{2,10},{3,11},{4,20},{5,21},{6,22},{7,23},{8,0},{9,1},... | collective-permute-start | bytes 3145736 | tf_op jit(solution)/shard_map/ppermute | solution.py:594
  40.8 103.6 %all-gather.13.cloned.1.call-start = ((), (), s32[]{:S(2)}) async-start(), calls=%async_computation.10 | async-start | bytes 1310720 | tf_op jit(solution)/shard_map/all_gather | solution.py:589
  40.8 98.5 %collective-permute-start.3 = (bf16[1,4,4,128,256]{4,3,2,1,0:T(8,128)(2,1)}, bf16[1,4,4,128,256]{4,3,2,1,0:T(8,128)(2,1)}, u32[]{:S(2)}, u32[]{:S(2)}) collective-permute-start(bf16[1,4,4,128,256]{4,3,2,1,0:T(8,128)(2,1)} %bitcast.110), channel_id=1, source_target_pairs={{0,16},{1,17},{2,18},{3,19},{4,12},{5,13},{6,14},{7,15},{8,24},{9,... | collective-permute-start | bytes 3145736 | tf_op jit(solution)/shard_map/ppermute | solution.py:594
  65.5 223.6 %copy-start.5 = (bf16[1,4,4,128,256]{4,3,2,1,0:T(8,128)(2,1)}, bf16[1,4,4,128,256]{4,3,2,1,0:T(8,128)(2,1)S(1)}, u32[]{:S(2)}) copy-start(bf16[1,4,4,128,256]{4,3,2,1,0:T(8,128)(2,1)S(1)} %collective-permute-done.2.refs_1_) | copy-start | bytes 3145732
  65.5 73.8 %collective-permute-start.4 = (bf16[1,4,4,128,256]{4,3,2,1,0:T(8,128)(2,1)S(1)}, bf16[1,4,4,128,256]{4,3,2,1,0:T(8,128)(2,1)}, u32[]{:S(2)}, u32[]{:S(2)}) collective-permute-start(bf16[1,4,4,128,256]{4,3,2,1,0:T(8,128)(2,1)S(1)} %collective-permute-done.2.refs_1_), channel_id=1, source_target_pairs={{0,16},{1,17},{2,18},{3,19},{4,12},{5,13},{6,14},{7,15},{8,24},{9,... | collective-permute-start | bytes 3145736 | tf_op jit(solution)/shard_map/ppermute | solution.py:594
  66.0 72.6 %copy-start.3 = (bf16[16,128,256]{2,1,0:T(8,128)(2,1)S(1)}, bf16[16,128,256]{2,1,0:T(8,128)(2,1)}, u32[]{:S(2)}) copy-start(bf16[16,128,256]{2,1,0:T(8,128)(2,1)} %all-gather.9.cloned.1.call-done) | copy-start | bytes 3145732
  66.1 75.5 %copy-start.28 = (s32[2,8]{1,0:T(2,128)S(1)}, s32[2,8]{1,0:T(2,128)}, u32[]{:S(2)}) copy-start(s32[2,8]{1,0:T(2,128)} %constant.67.clone) | copy-start | bytes 196
  68.4 13.0 %collective-permute-start.1 = (bf16[256,1024]{1,0:T(8,128)(2,1)}, bf16[256,1024]{1,0:T(8,128)(2,1)}, u32[]{:S(2)}, u32[]{:S(2)}) collective-permute-start(bf16[256,1024]{1,0:T(8,128)(2,1)} %get-tuple-element.125), channel_id=1, source_target_pairs={{0,2},{1,0},{2,6},{3,4},{4,3},{5,1},{6,7},{7,5},{8,10},{9,8},{10,1... | collective-permute-start | bytes 1572872 | tf_op jit(solution)/shard_map/ppermute | solution.py:629
  69.1 69.6 %collective-permute-start = (bf16[256,1024]{1,0:T(8,128)(2,1)}, bf16[256,1024]{1,0:T(8,128)(2,1)}, u32[]{:S(2)}, u32[]{:S(2)}) collective-permute-start(bf16[256,1024]{1,0:T(8,128)(2,1)} %get-tuple-element.124), channel_id=1, source_target_pairs={{0,0},{1,2},{2,4},{3,6},{4,1},{5,3},{6,5},{7,7},{8,8},{9,10},{10,1... | collective-permute-start | bytes 1572872 | tf_op jit(solution)/shard_map/ppermute | solution.py:628
  72.6 66.1 %collective-permute-start.25 = (bf16[256,1024]{1,0:T(8,128)(2,1)}, bf16[256,1024]{1,0:T(8,128)(2,1)S(1)}, u32[]{:S(2)}, u32[]{:S(2)}) collective-permute-start(bf16[256,1024]{1,0:T(8,128)(2,1)} %get-tuple-element.123), channel_id=1, source_target_pairs={{0,2},{1,0},{2,6},{3,4},{4,3},{5,1},{6,7},{7,5},{8,10},{9,8},{10,1... | collective-permute-start | bytes 1572872 | tf_op jit(solution)/shard_map/ppermute | solution.py:629
  77.5 422.2 %reduce-scatter.7.cloned.1.call-start = ((), (), s32[]{:S(2)}) async-start(), calls=%async_computation.5 | async-start | bytes 327680 | tf_op jit(solution)/shard_map/reduce_scatter | solution.py:610
  81.4 58.3 %collective-permute-start.24 = (bf16[256,1024]{1,0:T(8,128)(2,1)}, bf16[256,1024]{1,0:T(8,128)(2,1)}, u32[]{:S(2)}, u32[]{:S(2)}) collective-permute-start(bf16[256,1024]{1,0:T(8,128)(2,1)} %get-tuple-element.122), channel_id=1, source_target_pairs={{0,0},{1,2},{2,4},{3,6},{4,1},{5,3},{6,5},{7,7},{8,8},{9,10},{10,1... | collective-permute-start | bytes 1572872 | tf_op jit(solution)/shard_map/ppermute | solution.py:628
  138.7 8.2 %collective-permute-start.5 = (bf16[1,4,4,128,256]{4,3,2,1,0:T(8,128)(2,1)S(1)}, bf16[1,4,4,128,256]{4,3,2,1,0:T(8,128)(2,1)}, u32[]{:S(2)}, u32[]{:S(2)}) collective-permute-start(bf16[1,4,4,128,256]{4,3,2,1,0:T(8,128)(2,1)S(1)} %bitcast.111), channel_id=1, source_target_pairs={{0,4},{1,5},{2,6},{3,7},{4,0},{5,1},{6,2},{7,3},{8,12},{9,13},{10,... | collective-permute-start | bytes 3145736 | tf_op jit(solution)/shard_map/ppermute | solution.py:594
  138.8 9.0 %collective-permute-start.6 = (bf16[1,4,4,128,256]{4,3,2,1,0:T(8,128)(2,1)S(1)}, bf16[1,4,4,128,256]{4,3,2,1,0:T(8,128)(2,1)}, u32[]{:S(2)}, u32[]{:S(2)}) collective-permute-start(bf16[1,4,4,128,256]{4,3,2,1,0:T(8,128)(2,1)S(1)} %collective-permute-done.2.refs_1_), channel_id=1, source_target_pairs={{0,4},{1,5},{2,6},{3,7},{4,0},{5,1},{6,2},{7,3},{8,12},{9,13},{10,... | collective-permute-start | bytes 3145736 | tf_op jit(solution)/shard_map/ppermute | solution.py:594
  139.3 8.5 %collective-permute-start.7 = (bf16[1,4,4,128,256]{4,3,2,1,0:T(8,128)(2,1)}, bf16[1,4,4,128,256]{4,3,2,1,0:T(8,128)(2,1)}, u32[]{:S(2)}, u32[]{:S(2)}) collective-permute-start(bf16[1,4,4,128,256]{4,3,2,1,0:T(8,128)(2,1)} %collective-permute-done.3.refs_2_), channel_id=1, source_target_pairs={{0,4},{1,5},{2,6},{3,7},{4,0},{5,1},{6,2},{7,3},{8,12},{9,13},{10,... | collective-permute-start | bytes 3145736 | tf_op jit(solution)/shard_map/ppermute | solution.py:594
  139.4 9.1 %collective-permute-start.8 = (bf16[1,4,4,128,256]{4,3,2,1,0:T(8,128)(2,1)}, bf16[1,4,4,128,256]{4,3,2,1,0:T(8,128)(2,1)}, u32[]{:S(2)}, u32[]{:S(2)}) collective-permute-start(bf16[1,4,4,128,256]{4,3,2,1,0:T(8,128)(2,1)} %collective-permute-done.4.refs_3_), channel_id=1, source_target_pairs={{0,4},{1,5},{2,6},{3,7},{4,0},{5,1},{6,2},{7,3},{8,12},{9,13},{10,... | collective-permute-start | bytes 3145736 | tf_op jit(solution)/shard_map/ppermute | solution.py:594
  139.8 23.3 %collective-permute-start.10 = (bf16[1,4,128,1024]{3,2,1,0:T(8,128)(2,1)}, bf16[1,4,128,1024]{3,2,1,0:T(8,128)(2,1)}, u32[]{:S(2)}, u32[]{:S(2)}) collective-permute-start(bf16[1,4,128,1024]{3,2,1,0:T(8,128)(2,1)} %bitcast.118), channel_id=1, source_target_pairs={{0,8},{1,9},{2,10},{3,11},{4,20},{5,21},{6,22},{7,23},{8,0},{9,1},... | collective-permute-start | bytes 3145736 | tf_op jit(solution)/shard_map/ppermute | solution.py:594
  146.9 26.4 %collective-permute-start.11 = (bf16[1,4,128,1024]{3,2,1,0:T(8,128)(2,1)}, bf16[1,4,128,1024]{3,2,1,0:T(8,128)(2,1)}, u32[]{:S(2)}, u32[]{:S(2)}) collective-permute-start(bf16[1,4,128,1024]{3,2,1,0:T(8,128)(2,1)} %bitcast.119), channel_id=1, source_target_pairs={{0,16},{1,17},{2,18},{3,19},{4,12},{5,13},{6,14},{7,15},{8,24},{9,... | collective-permute-start | bytes 3145736 | tf_op jit(solution)/shard_map/ppermute | solution.py:594
  147.7 26.4 %collective-permute-start.13 = (bf16[1,4,128,1024]{3,2,1,0:T(8,128)(2,1)}, bf16[1,4,128,1024]{3,2,1,0:T(8,128)(2,1)S(1)}, u32[]{:S(2)}, u32[]{:S(2)}) collective-permute-start(bf16[1,4,128,1024]{3,2,1,0:T(8,128)(2,1)} %bitcast.120), channel_id=1, source_target_pairs={{0,4},{1,5},{2,6},{3,7},{4,0},{5,1},{6,2},{7,3},{8,12},{9,13},{10,... | collective-permute-start | bytes 3145736 | tf_op jit(solution)/shard_map/ppermute | solution.py:594
  147.8 35.4 %collective-permute-start.17 = (bf16[1,4,128,1024]{3,2,1,0:T(8,128)(2,1)}, bf16[1,4,128,1024]{3,2,1,0:T(8,128)(2,1)}, u32[]{:S(2)}, u32[]{:S(2)}) collective-permute-start(bf16[1,4,128,1024]{3,2,1,0:T(8,128)(2,1)} %bitcast.123), channel_id=1, source_target_pairs={{0,8},{1,9},{2,10},{3,11},{4,20},{5,21},{6,22},{7,23},{8,0},{9,1},... | collective-permute-start | bytes 3145736 | tf_op jit(solution)/shard_map/ppermute | solution.py:594
  148.4 39.3 %collective-permute-start.18 = (bf16[1,4,128,1024]{3,2,1,0:T(8,128)(2,1)}, bf16[1,4,128,1024]{3,2,1,0:T(8,128)(2,1)S(1)}, u32[]{:S(2)}, u32[]{:S(2)}) collective-permute-start(bf16[1,4,128,1024]{3,2,1,0:T(8,128)(2,1)} %bitcast.124), channel_id=1, source_target_pairs={{0,16},{1,17},{2,18},{3,19},{4,12},{5,13},{6,14},{7,15},{8,24},{9,... | collective-permute-start | bytes 3145736 | tf_op jit(solution)/shard_map/ppermute | solution.py:594
  159.9 28.9 %copy-start.20 = (f32[1024]{0:T(1024)S(1)}, f32[1024]{0:T(1024)}, u32[]{:S(2)}) copy-start(f32[1024]{0:T(1024)} %param.26) | copy-start | bytes 12292
  159.9 28.9 %copy-start.21 = (f32[1024]{0:T(1024)S(1)}, f32[1024]{0:T(1024)}, u32[]{:S(2)}) copy-start(f32[1024]{0:T(1024)} %param.27) | copy-start | bytes 12292
  160.0 28.9 %copy-start.22 = (f32[1024]{0:T(1024)S(1)}, f32[1024]{0:T(1024)}, u32[]{:S(2)}) copy-start(f32[1024]{0:T(1024)} %param.28) | copy-start | bytes 12292
  160.0 28.9 %copy-start.23 = (f32[1024]{0:T(1024)S(1)}, f32[1024]{0:T(1024)}, u32[]{:S(2)}) copy-start(f32[1024]{0:T(1024)} %param.32) | copy-start | bytes 12292
  163.1 47.8 %collective-permute-start.9 = (bf16[2,512,1024]{2,1,0:T(8,128)(2,1)}, bf16[2,512,1024]{2,1,0:T(8,128)(2,1)}, u32[]{:S(2)}, u32[]{:S(2)}) collective-permute-start(bf16[2,512,1024]{2,1,0:T(8,128)(2,1)} %slice.231), channel_id=1, source_target_pairs={{0,4},{1,5},{2,6},{3,7},{4,0},{5,1},{6,2},{7,3},{8,12},{9,13},{10,... | collective-permute-start | bytes 6291464 | tf_op jit(solution)/shard_map/ppermute | solution.py:726
  173.3 25.6 %collective-permute-start.12 = (bf16[1,4,128,1024]{3,2,1,0:T(8,128)(2,1)}, bf16[1,4,128,1024]{3,2,1,0:T(8,128)(2,1)S(1)}, u32[]{:S(2)}, u32[]{:S(2)}) collective-permute-start(bf16[1,4,128,1024]{3,2,1,0:T(8,128)(2,1)} %collective-permute-done.10.refs_1_), channel_id=1, source_target_pairs={{0,16},{1,17},{2,18},{3,19},{4,12},{5,13},{6,14},{7,15},{8,24},{9,... | collective-permute-start | bytes 3145736 | tf_op jit(solution)/shard_map/ppermute | solution.py:594
  174.2 29.3 %collective-permute-start.14 = (bf16[1,4,128,1024]{3,2,1,0:T(8,128)(2,1)}, bf16[1,4,128,1024]{3,2,1,0:T(8,128)(2,1)}, u32[]{:S(2)}, u32[]{:S(2)}) collective-permute-start(bf16[1,4,128,1024]{3,2,1,0:T(8,128)(2,1)} %collective-permute-done.10.refs_1_), channel_id=1, source_target_pairs={{0,4},{1,5},{2,6},{3,7},{4,0},{5,1},{6,2},{7,3},{8,12},{9,13},{10,... | collective-permute-start | bytes 3145736 | tf_op jit(solution)/shard_map/ppermute | solution.py:594
  183.1 20.3 %collective-permute-start.15 = (bf16[1,4,128,1024]{3,2,1,0:T(8,128)(2,1)}, bf16[1,4,128,1024]{3,2,1,0:T(8,128)(2,1)}, u32[]{:S(2)}, u32[]{:S(2)}) collective-permute-start(bf16[1,4,128,1024]{3,2,1,0:T(8,128)(2,1)} %collective-permute-done.11.refs_2_), channel_id=1, source_target_pairs={{0,4},{1,5},{2,6},{3,7},{4,0},{5,1},{6,2},{7,3},{8,12},{9,13},{10,... | collective-permute-start | bytes 3145736 | tf_op jit(solution)/shard_map/ppermute | solution.py:594
  187.7 22.6 %collective-permute-start.19 = (bf16[1,4,128,1024]{3,2,1,0:T(8,128)(2,1)}, bf16[1,4,128,1024]{3,2,1,0:T(8,128)(2,1)}, u32[]{:S(2)}, u32[]{:S(2)}) collective-permute-start(bf16[1,4,128,1024]{3,2,1,0:T(8,128)(2,1)} %collective-permute-done.17.refs_1_), channel_id=1, source_target_pairs={{0,16},{1,17},{2,18},{3,19},{4,12},{5,13},{6,14},{7,15},{8,24},{9,... | collective-permute-start | bytes 3145736 | tf_op jit(solution)/shard_map/ppermute | solution.py:594
  198.9 39.7 %collective-permute-start.16 = (bf16[1,4,128,1024]{3,2,1,0:T(8,128)(2,1)S(1)}, bf16[1,4,128,1024]{3,2,1,0:T(8,128)(2,1)S(1)}, u32[]{:S(2)}, u32[]{:S(2)}) collective-permute-start(bf16[1,4,128,1024]{3,2,1,0:T(8,128)(2,1)S(1)} %collective-permute-done.12.refs_3_), channel_id=1, source_target_pairs={{0,4},{1,5},{2,6},{3,7},{4,0},{5,1},{6,2},{7,3},{8,12},{9,13},{10,... | collective-permute-start | bytes 3145736 | tf_op jit(solution)/shard_map/ppermute | solution.py:594
  203.4 48.5 %collective-permute-start.20 = (bf16[1,4,128,1024]{3,2,1,0:T(8,128)(2,1)S(1)}, bf16[1,4,128,1024]{3,2,1,0:T(8,128)(2,1)S(1)}, u32[]{:S(2)}, u32[]{:S(2)}) collective-permute-start(bf16[1,4,128,1024]{3,2,1,0:T(8,128)(2,1)S(1)} %bitcast.125), channel_id=1, source_target_pairs={{0,4},{1,5},{2,6},{3,7},{4,0},{5,1},{6,2},{7,3},{8,12},{9,13},{10,... | collective-permute-start | bytes 3145736 | tf_op jit(solution)/shard_map/ppermute | solution.py:594
  203.5 48.5 %collective-permute-start.21 = (bf16[1,4,128,1024]{3,2,1,0:T(8,128)(2,1)}, bf16[1,4,128,1024]{3,2,1,0:T(8,128)(2,1)S(1)}, u32[]{:S(2)}, u32[]{:S(2)}) collective-permute-start(bf16[1,4,128,1024]{3,2,1,0:T(8,128)(2,1)} %collective-permute-done.17.refs_1_), channel_id=1, source_target_pairs={{0,4},{1,5},{2,6},{3,7},{4,0},{5,1},{6,2},{7,3},{8,12},{9,13},{10,... | collective-permute-start | bytes 3145736 | tf_op jit(solution)/shard_map/ppermute | solution.py:594
  210.2 41.8 %collective-permute-start.22 = (bf16[1,4,128,1024]{3,2,1,0:T(8,128)(2,1)S(1)}, bf16[1,4,128,1024]{3,2,1,0:T(8,128)(2,1)S(1)}, u32[]{:S(2)}, u32[]{:S(2)}) collective-permute-start(bf16[1,4,128,1024]{3,2,1,0:T(8,128)(2,1)S(1)} %copy-done.11), channel_id=1, source_target_pairs={{0,4},{1,5},{2,6},{3,7},{4,0},{5,1},{6,2},{7,3},{8,12},{9,13},{10,... | collective-permute-start | bytes 3145736 | tf_op jit(solution)/shard_map/ppermute | solution.py:594
  210.9 41.2 %collective-permute-start.23 = (bf16[1,4,128,1024]{3,2,1,0:T(8,128)(2,1)}, bf16[1,4,128,1024]{3,2,1,0:T(8,128)(2,1)}, u32[]{:S(2)}, u32[]{:S(2)}) collective-permute-start(bf16[1,4,128,1024]{3,2,1,0:T(8,128)(2,1)} %collective-permute-done.19.refs_3_), channel_id=1, source_target_pairs={{0,4},{1,5},{2,6},{3,7},{4,0},{5,1},{6,2},{7,3},{8,12},{9,13},{10,... | collective-permute-start | bytes 3145736 | tf_op jit(solution)/shard_map/ppermute | solution.py:594
  323.6 8.4 %collective-permute-start.28 = (bf16[2,512,1024]{2,1,0:T(8,128)(2,1)S(1)}, bf16[2,512,1024]{2,1,0:T(8,128)(2,1)S(1)}, u32[]{:S(2)}, u32[]{:S(2)}) collective-permute-start(bf16[2,512,1024]{2,1,0:T(8,128)(2,1)S(1)} %get-tuple-element.50), channel_id=1, source_target_pairs={{0,4},{1,5},{2,6},{3,7},{4,0},{5,1},{6,2},{7,3},{8,12},{9,13},{10,... | collective-permute-start | bytes 6291464 | tf_op jit(solution)/shard_map/ppermute | solution.py:742
  330.2 36.3 %collective-permute-start.45 = (bf16[4,4,128,1024]{3,2,1,0:T(8,128)(2,1)}, bf16[4,4,128,1024]{3,2,1,0:T(8,128)(2,1)}, u32[]{:S(2)}, u32[]{:S(2)}) collective-permute-start(bf16[4,4,128,1024]{3,2,1,0:T(8,128)(2,1)} %shard_map.333), channel_id=1, source_target_pairs={{0,4},{1,5},{2,6},{3,7},{4,0},{5,1},{6,2},{7,3},{8,12},{9,13},{10,... | collective-permute-start | bytes 12582920 | tf_op jit(solution)/shard_map/ppermute | solution.py:601
  335.0 115.0 %copy-start = (bf16[2,512,1024]{2,1,0:T(8,128)(2,1)}, bf16[2,512,1024]{2,1,0:T(8,128)(2,1)S(1)}, u32[]{:S(2)}) copy-start(bf16[2,512,1024]{2,1,0:T(8,128)(2,1)S(1)} %add_convert_fusion.4.dkv_ref.right_ref) | copy-start | bytes 6291460
  338.6 13.8 %collective-permute-start.31 = (bf16[4,4,3,128,256]{4,3,2,1,0:T(8,128)(2,1)S(1)}, bf16[4,4,3,128,256]{4,3,2,1,0:T(8,128)(2,1)}, u32[]{:S(2)}, u32[]{:S(2)}) collective-permute-start(bf16[4,4,3,128,256]{4,3,2,1,0:T(8,128)(2,1)S(1)} %pad_maximum_fusion), channel_id=1, source_target_pairs={{0,4},{1,5},{2,6},{3,7},{4,0},{5,1},{6,2},{7,3},{8,12},{9,13},{10,... | collective-permute-start | bytes 9437192 | tf_op jit(solution)/shard_map/ppermute | solution.py:601
  345.1 49.5 %collective-permute-start.42 = (bf16[4,4,128,1024]{3,2,1,0:T(8,128)(2,1)}, bf16[4,4,128,1024]{3,2,1,0:T(8,128)(2,1)}, u32[]{:S(2)}, u32[]{:S(2)}) collective-permute-start(bf16[4,4,128,1024]{3,2,1,0:T(8,128)(2,1)} %shard_map.331), channel_id=1, source_target_pairs={{0,4},{1,5},{2,6},{3,7},{4,0},{5,1},{6,2},{7,3},{8,12},{9,13},{10,... | collective-permute-start | bytes 12582920 | tf_op jit(solution)/shard_map/ppermute | solution.py:601
  346.9 17.0 %collective-permute-start.39 = (bf16[4,4,128,256]{3,2,1,0:T(8,128)(2,1)S(1)}, bf16[4,4,128,256]{3,2,1,0:T(8,128)(2,1)}, u32[]{:S(2)}, u32[]{:S(2)}) collective-permute-start(bf16[4,4,128,256]{3,2,1,0:T(8,128)(2,1)S(1)} %shard_map.329), channel_id=1, source_target_pairs={{0,4},{1,5},{2,6},{3,7},{4,0},{5,1},{6,2},{7,3},{8,12},{9,13},{10,... | collective-permute-start | bytes 3145736 | tf_op jit(solution)/shard_map/ppermute | solution.py:601
  356.2 28.1 %collective-permute-start.32 = (bf16[2,4,3,128,256]{4,3,2,1,0:T(8,128)(2,1)}, bf16[2,4,3,128,256]{4,3,2,1,0:T(8,128)(2,1)}, u32[]{:S(2)}, u32[]{:S(2)}) collective-permute-start(bf16[2,4,3,128,256]{4,3,2,1,0:T(8,128)(2,1)} %get-tuple-element.111), channel_id=1, source_target_pairs={{0,16},{1,17},{2,18},{3,19},{4,12},{5,13},{6,14},{7,15},{8,24},{9,... | collective-permute-start | bytes 4718600 | tf_op jit(solution)/shard_map/ppermute | solution.py:605
  365.5 17.0 %collective-permute-start.40 = (bf16[2,4,128,256]{3,2,1,0:T(8,128)(2,1)S(1)}, bf16[2,4,128,256]{3,2,1,0:T(8,128)(2,1)S(1)}, u32[]{:S(2)}, u32[]{:S(2)}) collective-permute-start(bf16[2,4,128,256]{3,2,1,0:T(8,128)(2,1)S(1)} %get-tuple-element.113), channel_id=1, source_target_pairs={{0,16},{1,17},{2,18},{3,19},{4,12},{5,13},{6,14},{7,15},{8,24},{9,... | collective-permute-start | bytes 1572872 | tf_op jit(solution)/shard_map/ppermute | solution.py:605
  371.5 44.8 %collective-permute-start.46 = (bf16[2,4,128,1024]{3,2,1,0:T(8,128)(2,1)}, bf16[2,4,128,1024]{3,2,1,0:T(8,128)(2,1)}, u32[]{:S(2)}, u32[]{:S(2)}) collective-permute-start(bf16[2,4,128,1024]{3,2,1,0:T(8,128)(2,1)} %get-tuple-element.107), channel_id=1, source_target_pairs={{0,16},{1,17},{2,18},{3,19},{4,12},{5,13},{6,14},{7,15},{8,24},{9,... | collective-permute-start | bytes 6291464 | tf_op jit(solution)/shard_map/ppermute | solution.py:605
  382.5 11.3 %collective-permute-start.41 = (bf16[1,4,128,256]{3,2,1,0:T(8,128)(2,1)S(1)}, bf16[1,4,128,256]{3,2,1,0:T(8,128)(2,1)S(1)}, u32[]{:S(2)}, u32[]{:S(2)}) collective-permute-start(bf16[1,4,128,256]{3,2,1,0:T(8,128)(2,1)S(1)} %add_convert_fusion.19), channel_id=1, source_target_pairs={{0,8},{1,9},{2,10},{3,11},{4,20},{5,21},{6,22},{7,23},{8,0},{9,1},... | collective-permute-start | bytes 786440 | tf_op jit(solution)/shard_map/ppermute | solution.py:608
  386.5 22.2 %collective-permute-start.33 = (bf16[1,4,3,128,256]{4,3,2,1,0:T(8,128)(2,1)}, bf16[1,4,3,128,256]{4,3,2,1,0:T(8,128)(2,1)}, u32[]{:S(2)}, u32[]{:S(2)}) collective-permute-start(bf16[1,4,3,128,256]{4,3,2,1,0:T(8,128)(2,1)} %add_convert_fusion.14), channel_id=1, source_target_pairs={{0,8},{1,9},{2,10},{3,11},{4,20},{5,21},{6,22},{7,23},{8,0},{9,1},... | collective-permute-start | bytes 2359304 | tf_op jit(solution)/shard_map/ppermute | solution.py:608
  394.6 138.5 %reduce-scatter.5.cloned.1.call-start = ((), (), s32[]{:S(2)}) async-start(), calls=%async_computation.4 | async-start | bytes 983040 | tf_op jit(solution)/shard_map/reduce_scatter | solution.py:610
  400.6 49.5 %collective-permute-start.43 = (bf16[2,4,128,1024]{3,2,1,0:T(8,128)(2,1)}, bf16[2,4,128,1024]{3,2,1,0:T(8,128)(2,1)}, u32[]{:S(2)}, u32[]{:S(2)}) collective-permute-start(bf16[2,4,128,1024]{3,2,1,0:T(8,128)(2,1)} %get-tuple-element.109), channel_id=1, source_target_pairs={{0,16},{1,17},{2,18},{3,19},{4,12},{5,13},{6,14},{7,15},{8,24},{9,... | collective-permute-start | bytes 6291464 | tf_op jit(solution)/shard_map/ppermute | solution.py:605
  411.4 123.4 %reduce-scatter.11.cloned.1.call-start = ((), (), s32[]{:S(2)}) async-start(), calls=%async_computation.7 | async-start | bytes 1310720 | tf_op jit(solution)/shard_map/reduce_scatter | solution.py:610
  419.2 26.4 %collective-permute-start.47 = (bf16[1,4,128,1024]{3,2,1,0:T(8,128)(2,1)}, bf16[1,4,128,1024]{3,2,1,0:T(8,128)(2,1)}, u32[]{:S(2)}, u32[]{:S(2)}) collective-permute-start(bf16[1,4,128,1024]{3,2,1,0:T(8,128)(2,1)} %add_convert_fusion.8), channel_id=1, source_target_pairs={{0,8},{1,9},{2,10},{3,11},{4,20},{5,21},{6,22},{7,23},{8,0},{9,1},... | collective-permute-start | bytes 3145736 | tf_op jit(solution)/shard_map/ppermute | solution.py:608
  425.2 29.7 %collective-permute-start.26 = (bf16[256,1024]{1,0:T(8,128)(2,1)}, bf16[256,1024]{1,0:T(8,128)(2,1)}, u32[]{:S(2)}, u32[]{:S(2)}) collective-permute-start(bf16[256,1024]{1,0:T(8,128)(2,1)} %get-tuple-element.120), channel_id=1, source_target_pairs={{2,0},{0,1},{6,2},{4,3},{3,4},{1,5},{7,6},{5,7},{10,8},{8,9},{14,1... | collective-permute-start | bytes 1572872 | tf_op jit(solution)/shard_map/ppermute | solution.py:639
  425.2 34.1 %collective-permute-start.27 = (bf16[256,1024]{1,0:T(8,128)(2,1)}, bf16[256,1024]{1,0:T(8,128)(2,1)}, u32[]{:S(2)}, u32[]{:S(2)}) collective-permute-start(bf16[256,1024]{1,0:T(8,128)(2,1)} %get-tuple-element.121), channel_id=1, source_target_pairs={{0,0},{2,1},{4,2},{6,3},{1,4},{3,5},{5,6},{7,7},{8,8},{10,9},{12,1... | collective-permute-start | bytes 1572872 | tf_op jit(solution)/shard_map/ppermute | solution.py:638
  449.1 87.7 %reduce-scatter.9.cloned.1.call-start = ((), (), s32[]{:S(2)}) async-start(), calls=%async_computation.6 | async-start | bytes 1310720 | tf_op jit(solution)/shard_map/reduce_scatter | solution.py:610
  453.0 28.8 %collective-permute-start.44 = (bf16[1,4,128,1024]{3,2,1,0:T(8,128)(2,1)S(1)}, bf16[1,4,128,1024]{3,2,1,0:T(8,128)(2,1)S(1)}, u32[]{:S(2)}, u32[]{:S(2)}) collective-permute-start(bf16[1,4,128,1024]{3,2,1,0:T(8,128)(2,1)S(1)} %add_convert_fusion.11), channel_id=1, source_target_pairs={{0,8},{1,9},{2,10},{3,11},{4,20},{5,21},{6,22},{7,23},{8,0},{9,1},... | collective-permute-start | bytes 3145736 | tf_op jit(solution)/shard_map/ppermute | solution.py:608
  454.8 5.8 %collective-permute-start.34 = (f32[12,1024]{1,0:T(8,128)S(1)}, f32[12,1024]{1,0:T(8,128)S(1)}, u32[]{:S(2)}, u32[]{:S(2)}) collective-permute-start(f32[12,1024]{1,0:T(8,128)S(1)} %pad_maximum_fusion.4), channel_id=1, source_target_pairs={{0,4},{1,5},{2,6},{3,7},{4,0},{5,1},{6,2},{7,3},{8,12},{9,13},{10,... | collective-permute-start | bytes 147464 | tf_op jit(solution)/shard_map/ppermute | solution.py:647
  460.6 8.6 %collective-permute-start.35 = (f32[12,1024]{1,0:T(8,128)S(1)}, f32[12,1024]{1,0:T(8,128)S(1)}, u32[]{:S(2)}, u32[]{:S(2)}) collective-permute-start(f32[12,1024]{1,0:T(8,128)S(1)} %fusion.30), channel_id=1, source_target_pairs={{0,8},{1,9},{2,10},{3,11},{4,12},{5,13},{6,14},{7,15},{8,0},{9,1},... | collective-permute-start | bytes 147464 | tf_op jit(solution)/shard_map/ppermute | solution.py:647
  469.3 9.1 %collective-permute-start.36 = (f32[12,1024]{1,0:T(8,128)S(1)}, f32[12,1024]{1,0:T(8,128)S(1)}, u32[]{:S(2)}, u32[]{:S(2)}) collective-permute-start(f32[12,1024]{1,0:T(8,128)S(1)} %add.174), channel_id=1, source_target_pairs={{0,16},{1,17},{2,18},{3,19},{4,20},{5,21},{6,22},{7,23},{8,24},{9,... | collective-permute-start | bytes 147464 | tf_op jit(solution)/shard_map/ppermute | solution.py:647
  478.4 7.6 %collective-permute-start.37 = (f32[12,1024]{1,0:T(8,128)S(1)}, f32[12,1024]{1,0:T(8,128)S(1)}, u32[]{:S(2)}, u32[]{:S(2)}) collective-permute-start(f32[12,1024]{1,0:T(8,128)S(1)} %add.175), channel_id=1, source_target_pairs={{0,1},{1,0},{2,3},{3,2},{4,5},{5,4},{6,7},{7,6},{8,9},{9,8},{10,11... | collective-permute-start | bytes 147464 | tf_op jit(solution)/shard_map/ppermute | solution.py:656
  486.0 11.3 %collective-permute-start.38 = (f32[12,1024]{1,0:T(8,128)S(1)}, f32[12,1024]{1,0:T(8,128)S(1)}, u32[]{:S(2)}, u32[]{:S(2)}) collective-permute-start(f32[12,1024]{1,0:T(8,128)S(1)} %add.176), channel_id=1, source_target_pairs={{0,2},{1,3},{2,0},{3,1},{4,6},{5,7},{6,4},{7,5},{8,10},{9,11},{10,... | collective-permute-start | bytes 147464 | tf_op jit(solution)/shard_map/ppermute | solution.py:656
  490.8 26.1 %collective-permute-start.29 = (bf16[256,1024]{1,0:T(8,128)(2,1)S(1)}, bf16[256,1024]{1,0:T(8,128)(2,1)S(1)}, u32[]{:S(2)}, u32[]{:S(2)}) collective-permute-start(bf16[256,1024]{1,0:T(8,128)(2,1)S(1)} %get-tuple-element.116), channel_id=1, source_target_pairs={{2,0},{0,1},{6,2},{4,3},{3,4},{1,5},{7,6},{5,7},{10,8},{8,9},{14,1... | collective-permute-start | bytes 1572872 | tf_op jit(solution)/shard_map/ppermute | solution.py:639
  490.9 40.7 %collective-permute-start.30 = (bf16[256,1024]{1,0:T(8,128)(2,1)S(1)}, bf16[256,1024]{1,0:T(8,128)(2,1)S(1)}, u32[]{:S(2)}, u32[]{:S(2)}) collective-permute-start(bf16[256,1024]{1,0:T(8,128)(2,1)S(1)} %get-tuple-element.117), channel_id=1, source_target_pairs={{0,0},{2,1},{4,2},{6,3},{1,4},{3,5},{5,6},{7,7},{8,8},{10,9},{12,1... | collective-permute-start | bytes 1572872 | tf_op jit(solution)/shard_map/ppermute | solution.py:638
  (25 other events, 308.5 us)
Sparse Core Ops, SparseCore 0:
  10.2 29.0 all-gather.8
  40.9 27.3 all-gather.10
  77.6 44.3 all-gather.12
  394.7 17.1 reduce-scatter.6
  414.1 29.2 reduce-scatter.4
  449.3 27.4 reduce-scatter.10
  484.8 40.4 reduce-scatter.8

commit v2 on v1

--- a/solution.py
+++ b/solution.py
@@ -32,12 +32,19 @@
     return lax.dot_general(left, right, (((0,), (0,)), ((), ())), preferred_element_type=F32)
 
 
-def joined(refs, pick=None):
-    parts = []
-    for ref in refs:
-        value = ref[...] if pick is None else ref[:, :, pick]
-        parts.append(value.reshape(-1, value.shape[-1]))
-    return parts[0] if len(parts) == 1 else jnp.concatenate(parts, axis=0)
+def tile_of(ref):
+    parts = [ref[i].reshape(-1, ref.shape[-1]) for i in range(ref.shape[0])]
+    return parts[0] if len(parts) == 1 else jnp.concatenate(parts, axis=1)
+
+
+def weight_spec(weights, subs, index):
+    _, slots, _, depth, cols = weights.shape
+
+    def place(*grid):
+        sub, z = index(*grid)
+        return (sub, 0, z, 0, 0)
+
+    return pl.BlockSpec((subs, slots, 1, depth, cols), place)
 
 
 def call(kernel, grid, in_specs, out_specs, out_shape, scratch, flops, moved, limit=48, exps=0):
@@ -61,52 +68,48 @@
     return min(rows, 512)
 
 
-def qkv_kernel(count, x_ref, *refs):
-    w_refs, bias_ref, out_ref = refs[:count], refs[count], refs[count + 1]
-    acc = dot_nn(x_ref[...], joined(w_refs))
+def qkv_kernel(x_ref, w_ref, bias_ref, out_ref):
+    acc = dot_nn(x_ref[...], tile_of(w_ref))
     scale = jnp.where(pl.program_id(0) == 0, SCALE, 1.0)
     out_ref[0] = ((acc + bias_ref[0]) * scale).astype(BF)
 
 
-def project_qkv(x, slots, bias):
+def project_qkv(x, weights, bias):
     rows, width = x.shape
-    parts, cols = slots[0].shape[1], slots[0].shape[-1]
-    specs = [
-        pl.BlockSpec((s.shape[0], 1, 1, s.shape[3], cols), lambda w, z: (0, z, w, 0, 0)) for s in slots
-    ]
-    return call(
-        functools.partial(qkv_kernel, len(slots)),
+    parts, cols = weights.shape[2], weights.shape[4]
+    return call(
+        qkv_kernel,
         (3, parts),
-        [whole_spec(x.shape)] + specs + [pl.BlockSpec((1, 1, cols), lambda w, z: (w, 0, z))],
+        [
+            whole_spec(x.shape),
+            weight_spec(weights, 1, lambda w, z: (w, z)),
+            pl.BlockSpec((1, 1, cols), lambda w, z: (w, 0, z)),
+        ],
         pl.BlockSpec((1, rows, cols), lambda w, z: (w, 0, z)),
         jax.ShapeDtypeStruct((3, rows, parts * cols), BF),
         [],
         2 * rows * width * 3 * parts * cols,
         2 * (rows * width * 4 + 3 * width * parts * cols),
-    )(x, *slots, bias)
-
-
-def plain_kernel(count, x_ref, *refs):
-    w_refs, out_ref = refs[:count], refs[count]
-    out_ref[...] = dot_nn(x_ref[...], joined(w_refs)).astype(BF)
-
-
-def project_back(x, slots, which):
+    )(x, weights, bias)
+
+
+def plain_kernel(x_ref, w_ref, out_ref):
+    out_ref[...] = dot_nn(x_ref[...], tile_of(w_ref)).astype(BF)
+
+
+def project_back(x, weights, which):
     rows, width = x.shape
-    parts, cols = slots[0].shape[1], slots[0].shape[-1]
-    specs = [
-        pl.BlockSpec((s.shape[0], 1, 1, s.shape[3], cols), lambda z: (0, z, which, 0, 0)) for s in slots
-    ]
-    return call(
-        functools.partial(plain_kernel, len(slots)),
+    parts, cols = weights.shape[2], weights.shape[4]
+    return call(
+        plain_kernel,
         (parts,),
-        [whole_spec(x.shape)] + specs,
+        [whole_spec(x.shape), weight_spec(weights, 1, lambda z: (which, z))],
         pl.BlockSpec((rows, cols), lambda z: (0, z)),
         jax.ShapeDtypeStruct((rows, parts * cols), BF),
         [],
         2 * rows * width * parts * cols,
         2 * (rows * width * 2 + width * parts * cols),
-    )(x, *slots)
+    )(x, weights)
 
 
 def attend_kernel(count, q_ref, *refs):
@@ -265,11 +268,9 @@
         acc_ref[...] += value
 
 
-def first_norm_kernel(count, m_ref, *refs):
-    w_refs = refs[:count]
-    x_ref, vec_ref, z_ref, r_ref, y_ref, acc_ref = refs[count:]
+def first_norm_kernel(m_ref, w_ref, x_ref, vec_ref, z_ref, r_ref, y_ref, acc_ref):
     step = pl.program_id(1)
-    accumulate(acc_ref, step, dot_nt(m_ref[...], joined(w_refs)))
+    accumulate(acc_ref, step, dot_nt(m_ref[...], tile_of(w_ref)))
 
     @pl.when(step == pl.num_programs(1) - 1)
     def _():
@@ -280,18 +281,16 @@
         y_ref[...] = (z * vector(vec_ref, FIRST_GAIN) + vector(vec_ref, FIRST_SHIFT)).astype(BF)
 
 
-def first_norm(mixed, slots, x, vectors):
+def first_norm(mixed, weights, x, vectors):
     rows, width = x.shape
     tile = row_tile(rows)
-    parts, cols = slots[0].shape[1], slots[0].shape[-1]
-    specs = [
-        pl.BlockSpec((s.shape[0], 1, 1, s.shape[3], cols), lambda i, z: (0, z, 3, 0, 0)) for s in slots
-    ]
+    parts, cols = weights.shape[2], weights.shape[4]
+    spec = weight_spec(weights, 1, lambda i, z: (3, z))
     flat = pl.BlockSpec((tile, width), lambda i, z: (i, 0))
     return call(
-        functools.partial(first_norm_kernel, len(slots)),
+        first_norm_kernel,
         (rows // tile, parts),
-        [pl.BlockSpec((tile, cols), lambda i, z: (i, z))] + specs + [flat, whole_spec(vectors.shape)],
+        [pl.BlockSpec((tile, cols), lambda i, z: (i, z)), spec, flat, whole_spec(vectors.shape)],
         (flat, pl.BlockSpec((tile, 1), lambda i, z: (i, 0)), flat),
         (
             jax.ShapeDtypeStruct((rows, width), F32),
@@ -301,50 +300,47 @@
         [pltpu.VMEM((tile, width), F32)],
         2 * rows * width * width,
         2 * (rows * width * 5 + width * width),
-    )(mixed, *slots, x, vectors)
-
-
-def up_kernel(count, y_ref, *refs):
-    w_refs, bias_ref, g_ref, slope_ref = refs[:count], refs[count], refs[count + 1], refs[count + 2]
-    upper = dot_nn(y_ref[...], joined(w_refs)) + bias_ref[...]
+    )(mixed, weights, x, vectors)
+
+
+def up_kernel(y_ref, w_ref, bias_ref, g_ref, slope_ref):
+    upper = dot_nn(y_ref[...], tile_of(w_ref)) + bias_ref[...]
     half = 0.5 + 0.5 * lax.erf(upper * (0.5**0.5))
     g_ref[...] = (upper * half).astype(BF)
     bell = jnp.exp(upper * upper * -0.5) * ((2 * math.pi) ** -0.5)
     slope_ref[...] = (half + upper * bell).astype(BF)
 
 
-def up_gelu(y, slots, bias):
+def up_gelu(y, weights, bias):
     rows, width = y.shape
-    parts, full = slots[0].shape[1], slots[0].shape[-1]
-    cols = min(512, full)
-    per = full // cols
+    parts, cols = weights.shape[2], weights.shape[4] * 2
     tile = row_tile(rows)
-    specs = [
-        pl.BlockSpec((s.shape[0], 1, s.shape[2], cols), lambda i, z: (0, z // per, 0, z % per)) for s in slots
-    ]
+    full = parts * weights.shape[4] * 4
     out = pl.BlockSpec((tile, cols), lambda i, z: (i, z))
-    shape = jax.ShapeDtypeStruct((rows, parts * full), BF)
-    return call(
-        functools.partial(up_kernel, len(slots)),
-        (rows // tile, parts * per),
-        [pl.BlockSpec((tile, width), lambda i, z: (i, 0))]
-        + specs
-        + [pl.BlockSpec((1, cols), lambda i, z: (0, z))],
+    shape = jax.ShapeDtypeStruct((rows, full), BF)
+    return call(
+        up_kernel,
+        (rows // tile, full // cols),
+        [
+            pl.BlockSpec((tile, width), lambda i, z: (i, 0)),
+            weight_spec(weights, 2, lambda i, z: (2 + z % 2, z // 2)),
+            pl.BlockSpec((1, cols), lambda i, z: (0, z)),
+        ],
         (out, out),
         (shape, shape),
         [],
-        2 * rows * width * parts * full,
-        2 * (rows * width + 2 * rows * parts * full + width * parts * full),
-        exps=2 * rows * parts * full,
-    )(y, *slots, bias)
-
-
-def second_norm_kernel(count, g_ref, *refs):
-    w_refs = refs[:count]
-    z1_ref, c_ref, vec_ref, out_ref, dh_ref, b_ref, sum_ref, acc_ref = refs[count:]
+        2 * rows * width * full,
+        2 * (rows * width + 2 * rows * full + width * full),
+        exps=2 * rows * full,
+    )(y, weights, bias)
+
+
+def second_norm_kernel(
+    g_ref, w_ref, z1_ref, c_ref, vec_ref, out_ref, dh_ref, b_ref, sum_ref, acc_ref
+):
     step = pl.program_id(1)
     first = pl.program_id(0) == 0
-    accumulate(acc_ref, step, dot_nt(g_ref[...], joined(w_refs)))
+    accumulate(acc_ref, step, dot_nt(g_ref[...], tile_of(w_ref)))
 
     @pl.when(step == pl.num_programs(1) - 1)
     def _():
@@ -360,18 +356,21 @@
         add_sums(sum_ref, first, [total_rows(grad * z), total_rows(grad), total_rows(dh)])
 
 
-def second_norm(gated, slots, z1, cot, vectors):
+def second_norm(gated, weights, z1, cot, vectors):
     rows, width = z1.shape
     tile = row_tile(rows)
-    parts, cols = slots[0].shape[1], slots[0].shape[-1]
-    specs = [pl.BlockSpec((s.shape[0], 1, s.shape[2], cols), lambda i, z: (0, z, 0, 0)) for s in slots]
+    parts, cols = weights.shape[2], weights.shape[4] * 4
     flat = pl.BlockSpec((tile, width), lambda i, z: (i, 0))
     return call(
-        functools.partial(second_norm_kernel, len(slots)),
+        second_norm_kernel,
         (rows // tile, parts),
-        [pl.BlockSpec((tile, cols), lambda i, z: (i, z))]
-        + specs
-        + [flat, flat, whole_spec(vectors.shape)],
+        [
+            pl.BlockSpec((tile, cols), lambda i, z: (i, z)),
+            weight_spec(weights, 4, lambda i, z: (2, z)),
+            flat,
+            flat,
+            whole_spec(vectors.shape),
+        ],
         (flat, flat, flat, whole_spec((8, width))),
         (
             jax.ShapeDtypeStruct((rows, width), BF),
@@ -382,12 +381,11 @@
         [pltpu.VMEM((tile, width), F32)],
         2 * rows * width * parts * cols,
         2 * (rows * width * 7 + (rows + width) * parts * cols),
-    )(gated, *slots, z1, cot, vectors)
-
-
-def gate_back_kernel(count, b_ref, *refs):
-    w_refs, slope_ref, du_ref, sum_ref = refs[:count], refs[count], refs[count + 1], refs[count + 2]
-    grad = dot_nn(b_ref[...], joined(w_refs))
+    )(gated, weights, z1, cot, vectors)
+
+
+def gate_back_kernel(b_ref, w_ref, slope_ref, du_ref, sum_ref):
+    grad = dot_nn(b_ref[...], tile_of(w_ref))
     low = (grad * slope_ref[...].astype(F32)).astype(BF)
     du_ref[...] = low
     value = total_rows(low.astype(F32))
@@ -402,37 +400,37 @@
         sum_ref[...] += value
 
 
-def gate_back(b, slots, slope):
+def gate_back(b, weights, slope):
     rows, width = b.shape
-    parts, full = slots[0].shape[1], slots[0].shape[-1]
-    cols = min(512, full)
-    per = full // cols
+    parts, cols = weights.shape[2], weights.shape[4] * 2
     tile = row_tile(rows)
-    specs = [
-        pl.BlockSpec((s.shape[0], 1, s.shape[2], cols), lambda z, i: (0, z // per, 0, z % per)) for s in slots
-    ]
+    full = parts * weights.shape[4] * 4
     out = pl.BlockSpec((tile, cols), lambda z, i: (i, z))
     return call(
-        functools.partial(gate_back_kernel, len(slots)),
-        (parts * per, rows // tile),
-        [pl.BlockSpec((tile, width), lambda z, i: (i, 0))] + specs + [out],
+        gate_back_kernel,
+        (full // cols, rows // tile),
+        [
+            pl.BlockSpec((tile, width), lambda z, i: (i, 0)),
+            weight_spec(weights, 2, lambda z, i: (4 + z % 2, z // 2)),
+            out,
+        ],
         (out, pl.BlockSpec((1, cols), lambda z, i: (0, z))),
         (
-            jax.ShapeDtypeStruct((rows, parts * full), BF),
-            jax.ShapeDtypeStruct((1, parts * full), F32),
+            jax.ShapeDtypeStruct((rows, full), BF),
+            jax.ShapeDtypeStruct((1, full), F32),
         ),
         [],
-        2 * rows * width * parts * full,
-        2 * (rows * width + 2 * rows * parts * full + width * parts * full),
-    )(b, *slots, slope)
-
-
-def first_back_kernel(count, du_ref, *refs):
-    w_refs = refs[:count]
-    dh2_ref, z1_ref, r1_ref, vec_ref, dh_ref, b_ref, sum_ref, acc_ref = refs[count:]
+        2 * rows * width * full,
+        2 * (rows * width + 2 * rows * full + width * full),
+    )(b, weights, slope)
+
+
+def first_back_kernel(
+    du_ref, w_ref, dh2_ref, z1_ref, r1_ref, vec_ref, dh_ref, b_ref, sum_ref, acc_ref
+):
     step = pl.program_id(1)
     first = pl.program_id(0) == 0
-    accumulate(acc_ref, step, dot_nt(du_ref[...], joined(w_refs)))
+    accumulate(acc_ref, step, dot_nt(du_ref[...], tile_of(w_ref)))
 
     @pl.when(step == pl.num_programs(1) - 1)
     def _():
@@ -444,18 +442,22 @@
         add_sums(sum_ref, first, [total_rows(grad * z), total_rows(grad), total_rows(dh)])
 
 
-def first_back(du, slots, dh2, z1, r1, vectors):
+def first_back(du, weights, dh2, z1, r1, vectors):
     rows, width = z1.shape
     tile = row_tile(rows)
-    parts, cols = slots[0].shape[1], slots[0].shape[-1]
-    specs = [pl.BlockSpec((s.shape[0], 1, s.shape[2], cols), lambda i, z: (0, z, 0, 0)) for s in slots]
+    parts, cols = weights.shape[2], weights.shape[4] * 4
     flat = pl.BlockSpec((tile, width), lambda i, z: (i, 0))
     return call(
-        functools.partial(first_back_kernel, len(slots)),
+        first_back_kernel,
         (rows // tile, parts),
-        [pl.BlockSpec((tile, cols), lambda i, z: (i, z))]
-        + specs
-        + [flat, flat, pl.BlockSpec((tile, 1), lambda i, z: (i, 0)), whole_spec(vectors.shape)],
+        [
+            pl.BlockSpec((tile, cols), lambda i, z: (i, z)),
+            weight_spec(weights, 4, lambda i, z: (1, z)),
+            flat,
+            flat,
+            pl.BlockSpec((tile, 1), lambda i, z: (i, 0)),
+            whole_spec(vectors.shape),
+        ],
         (flat, flat, whole_spec((8, width))),
         (
             jax.ShapeDtypeStruct((rows, width), F32),
@@ -465,16 +467,14 @@
         [pltpu.VMEM((tile, width), F32)],
         2 * rows * width * parts * cols,
         2 * (rows * width * 8 + (rows + width) * parts * cols),
-    )(du, *slots, dh2, z1, r1, vectors)
-
-
-def input_back_kernel(count, dq_ref, dkv_ref, *refs):
-    w_refs = refs[:count]
-    dh_ref, out_ref, acc_ref = refs[count:]
+    )(du, weights, dh2, z1, r1, vectors)
+
+
+def input_back_kernel(dq_ref, dkv_ref, w_ref, dh_ref, out_ref, acc_ref):
     step = pl.program_id(1)
-    value = dot_nt(dq_ref[...], joined(w_refs, 0))
-    value += dot_nt(dkv_ref[0], joined(w_refs, 1))
-    value += dot_nt(dkv_ref[1], joined(w_refs, 2))
+    value = dot_nt(dq_ref[...], w_ref[0].reshape(-1, w_ref.shape[-1]))
+    value += dot_nt(dkv_ref[0], w_ref[1].reshape(-1, w_ref.shape[-1]))
+    value += dot_nt(dkv_ref[1], w_ref[2].reshape(-1, w_ref.shape[-1]))
     accumulate(acc_ref, step, value)
 
     @pl.when(step == pl.num_programs(1) - 1)
@@ -482,29 +482,26 @@
         out_ref[...] = (acc_ref[...] + dh_ref[...]).astype(BF)
 
 
-def input_back(dq, dkv, slots, dh1):
+def input_back(dq, dkv, weights, dh1):
     rows, width = dh1.shape
     tile = row_tile(rows)
-    parts, kinds, cols = slots[0].shape[1], slots[0].shape[2], slots[0].shape[-1]
-    specs = [
-        pl.BlockSpec((s.shape[0], 1, kinds, s.shape[3], cols), lambda i, z: (0, z, 0, 0, 0)) for s in slots
-    ]
+    parts, cols = weights.shape[2], weights.shape[4]
     flat = pl.BlockSpec((tile, width), lambda i, z: (i, 0))
     return call(
-        functools.partial(input_back_kernel, len(slots)),
+        input_back_kernel,
         (rows // tile, parts),
         [
             pl.BlockSpec((tile, cols), lambda i, z: (i, z)),
             pl.BlockSpec((2, tile, cols), lambda i, z: (0, i, z)),
-        ]
-        + specs
-        + [flat],
+            weight_spec(weights, 3, lambda i, z: (0, z)),
+            flat,
+        ],
         flat,
         jax.ShapeDtypeStruct((rows, width), BF),
         [pltpu.VMEM((tile, width), F32)],
         6 * rows * width * parts * cols,
         2 * (rows * width * 6 + 4 * width * parts * cols),
-    )(dq, dkv, *slots, dh1)
+    )(dq, dkv, weights, dh1)
 
 
 def outer_kernel(left_ref, right_ref, out_ref):
@@ -550,24 +547,136 @@
     )(left, stack)
 
 
+def remote(source, target, send, receive, device):
+    return pltpu.make_async_remote_copy(
+        source, target, send, receive, device_id=device, device_id_type=pl.DeviceIdType.MESH
+    )
+
+
+def greet(devices):
+    barrier = pltpu.get_barrier_semaphore()
+    for device in devices:
+        pl.semaphore_signal(barrier, 1, device_id=device, device_id_type=pl.DeviceIdType.MESH)
+    pl.semaphore_wait(barrier, len(devices))
+
+
+class Cube:
+    def __init__(self, count, parts):
+        self.count, self.parts = count, parts
+        self.place, self.z = lax.axis_index("dp"), lax.axis_index("tensor")
+        self.core = lax.rem(self.place, 2)
+        bits = [1 << i for i in range(1, count.bit_length() - 1)]
+        self.orders = [bits, bits[::-1]]
+
+    def stages(self):
+        ups, downs = self.orders
+        out = []
+        for up, down in zip(ups, downs):
+            out.append(self.place ^ jnp.where(self.core == 0, up, down))
+        return out + [self.place ^ 1]
+
+    def masks(self):
+        table = []
+        for order in self.orders:
+            held = [0]
+            for bit in order:
+                held = held + [m ^ bit for m in held]
+            table.append(held)
+        return [a + [m ^ 1 for m in b] for a, b in (table, table[::-1])]
+
+
+def gather_kernel(count, parts, ahead, w_ref, out_ref, local_sem, zs, zr, ss, sr):
+    cube = Cube(count, parts)
+    subs = w_ref.shape[0]
+    partners = cube.stages()
+    levels = len(partners)
+    shifts = [lax.rem(cube.z + d, parts) for d in range(1, parts)]
+    greet(
+        [{"dp": cube.place, "tensor": z} for z in shifts]
+        + [{"dp": p, "tensor": cube.z} for p in partners]
+    )
+
+    def own(sub):
+        return pltpu.make_async_copy(w_ref.at[sub], out_ref.at[sub, 0, cube.z], local_sem.at[sub])
+
+    def along(sub, d):
+        return remote(
+            w_ref.at[sub],
+            out_ref.at[sub, 0, cube.z],
+            zs.at[sub, d],
+            zr.at[sub, d],
+            {"dp": cube.place, "tensor": shifts[d]},
+        )
+
+    def stage(sub, level):
+        size = 1 << level
+        return remote(
+            out_ref.at[sub, pl.ds(0, size)],
+            out_ref.at[sub, pl.ds(size, size)],
+            ss.at[sub, level],
+            sr.at[sub, level],
+            {"dp": partners[level], "tensor": cube.z},
+        )
+
+    def begin(sub):
+        own(sub).start()
+        for d in range(parts - 1):
+            along(sub, d).start()
+
+    for sub in range(min(ahead, subs)):
+        begin(sub)
+    for step in range(subs + levels):
+        if step < subs:
+            own(step).wait()
+            for d in range(parts - 1):
+                along(step, d).wait_recv()
+            stage(step, 0).start()
+            if step + ahead < subs:
+                begin(step + ahead)
+        for level in range(levels):
+            sub = step - level - 1
+            if 0 <= sub < subs:
+                stage(sub, level).wait_recv()
+                if level + 1 < levels:
+                    stage(sub, level + 1).start()
+    for sub in range(subs):
+        for d in range(parts - 1):
+            along(sub, d).wait_send()
+        for level in range(levels):
+            stage(sub, level).wait_send()
+
+
+def gather(local, count, parts):
+    subs, depth, cols = local.shape
+    levels = count.bit_length() - 1
+    dma = pltpu.SemaphoreType.DMA
+    return pl.pallas_call(
+        functools.partial(gather_kernel, count, parts, 6),
+        in_specs=[pl.BlockSpec(memory_space=pl.ANY)],
+        out_specs=pl.BlockSpec(memory_space=pl.ANY),
+        out_shape=jax.ShapeDtypeStruct((subs, count, parts, depth, cols), BF),
+        scratch_shapes=[
+            dma((subs,)),
+            dma((subs, parts - 1)),
+            dma((subs, parts - 1)),
+            dma((subs, levels)),
+            dma((subs, levels)),
+        ],
+        compiler_params=pltpu.CompilerParams(collective_id=1, has_side_effects=True),
+    )(local)
+
+
 class Links:
     def __init__(self, count, parts):
         self.count, self.parts = count, parts
         self.cube = count == 8
         self.place = lax.axis_index("dp")
         self.core = self.place % 2
-        if self.cube:
-            masks = [[0, 2, 4, 6, 1, 5, 3, 7], [0, 4, 2, 6, 1, 3, 5, 7]]
-        else:
-            masks = None
-        if masks is None:
-            self.owner = jnp.arange(count)
-            self.inverse = jnp.arange(count)
-        else:
-            table = jnp.asarray(masks, jnp.int32)
-            back = jnp.asarray([list(np.argsort(m)) for m in masks], jnp.int32)
-            self.owner = table[self.core] ^ self.place
-            self.inverse = back[self.core][jnp.arange(count) ^ self.place]
+        masks = Cube(count, parts).masks()
+        table = jnp.asarray(masks, jnp.int32)
+        back = jnp.asarray([list(np.argsort(m)) for m in masks], jnp.int32)
+        self.owner = table[self.core] ^ self.place
+        self.inverse = back[self.core][jnp.arange(count) ^ self.place]
 
     def pairs(self, flip):
         out = []
@@ -585,21 +694,17 @@
     def second_pairs(self):
         return self.pairs(lambda place: place ^ (2 if place % 2 else 4))
 
-    def gather(self, local):
-        block = lax.all_gather(local, "tensor", axis=0, tiled=False)
+    def terms(self, make):
+        half = self.count // 2
+        return make(half, half), make(0, half)
+
+    def scatter(self, terms):
+        away, held = terms
         if not self.cube:
-            return [lax.all_gather(block, "dp", axis=0, tiled=False)]
-        blocks = [block[None]]
-        for pairs in (self.first_pairs(), self.second_pairs(), self.core_pairs()):
-            blocks = blocks + [lax.ppermute(b, AXES, pairs) for b in blocks]
-        return blocks
-
-    def scatter(self, make):
-        if not self.cube:
-            full = lax.psum_scatter(make(0, self.count), "dp", scatter_dimension=0, tiled=False)
+            full = jnp.concatenate([held, away])[self.inverse]
+            full = lax.psum_scatter(full, "dp", scatter_dimension=0, tiled=False)
             return lax.psum_scatter(full, "tensor", scatter_dimension=0, tiled=False)
-        far = lax.ppermute(make(4, 4), AXES, self.core_pairs())
-        held = make(0, 4)
+        far = lax.ppermute(away, AXES, self.core_pairs())
         away = summed(held[2:4], far[2:4])
         held = summed(held[0:2], far[0:2])
         far = lax.ppermute(away, AXES, self.second_pairs())
@@ -706,8 +811,15 @@
     )
     vectors = vectors.reshape(8, count, depth)[:, links.owner].reshape(8, width)
 
-    shared = jnp.stack([query_weight, key_weight, value_weight, out_weight.T])
-    att_slots = links.gather(shared)
+    cols = query_weight.shape[1]
+    up_parts = [up_weight[:, i : i + cols] for i in range(0, up_weight.shape[1], cols)]
+    down = down_weight.T
+    down_parts = [down[:, i : i + cols] for i in range(0, down.shape[1], cols)]
+    weights = gather(
+        jnp.stack([query_weight, key_weight, value_weight, out_weight.T] + up_parts + down_parts),
+        count,
+        parts,
+    )
     biases = lax.all_gather(
         jnp.concatenate([query_bias, value_bias, up_bias]), "tensor", axis=0, tiled=False
     )
@@ -717,33 +829,35 @@
     up_full = biases[:, 2 * local :].reshape(1, -1)
     qkv_bias = jnp.concatenate([query_full, jnp.zeros_like(query_full), value_full], axis=0)
     x = ordered(links.rows_in(inputs))
-    up_slots = links.gather(up_weight)
     cot = ordered(links.rows_in(cotangent))
-    down_slots = links.gather(down_weight.T)
-
-    qkv = project_qkv(x, att_slots, qkv_bias)
+
+    qkv = project_qkv(x, weights, qkv_bias)
     share = x.shape[0] < LEN
     other = lax.ppermute(qkv[1:], AXES, links.core_pairs()) if share else None
     mixed, logs = attend_forward(qkv, other)
-    z1, r1, y1 = first_norm(mixed, att_slots, x, vectors)
-    gated, slope = up_gelu(y1, up_slots, up_full)
-    out, dh2, b2, second_sums = second_norm(gated, down_slots, z1, cot, vectors)
+    z1, r1, y1 = first_norm(mixed, weights, x, vectors)
+    gated, slope = up_gelu(y1, weights, up_full)
+    out, dh2, b2, second_sums = second_norm(gated, weights, z1, cot, vectors)
     outputs = links.rows_out(restored(out))
 
-    down_grad = links.scatter(lambda begin, n: outer(b2, gated, begin, n, depth, parts))
-    du, up_bias_sum = gate_back(b2, down_slots, slope)
-    up_grad = links.scatter(lambda begin, n: outer(y1, du, begin, n, depth, parts))
-    dh1, b1, first_sums = first_back(du, up_slots, dh2, z1, r1, vectors)
-    dm = project_back(b1, att_slots, 3)
-    out_grad = links.scatter(lambda begin, n: outer(b1, mixed, begin, n, depth, parts))
+    down_terms = links.terms(lambda begin, n: outer(b2, gated, begin, n, depth, parts))
+    b2, down_terms = lax.optimization_barrier((b2, down_terms))
+    down_grad = links.scatter(down_terms)
+    du, up_bias_sum = gate_back(b2, weights, slope)
+    up_terms = links.terms(lambda begin, n: outer(y1, du, begin, n, depth, parts))
+    du, up_terms = lax.optimization_barrier((du, up_terms))
+    up_grad = links.scatter(up_terms)
+    dh1, b1, first_sums = first_back(du, weights, dh2, z1, r1, vectors)
+    dm = project_back(b1, weights, 3)
+    out_terms = links.terms(lambda begin, n: outer(b1, mixed, begin, n, depth, parts))
+    dm, out_terms = lax.optimization_barrier((dm, out_terms))
+    out_grad = links.scatter(out_terms)
     back = attend_backward(qkv, other, dm, logs)
     if share:
         dq, near, far = back
         dkv = (near + lax.ppermute(far, AXES, links.core_pairs()).astype(F32)).astype(BF)
     else:
         dq, dkv = back
-    dx = input_back(dq, dkv, att_slots, dh1)
-    input_grad = links.rows_out(restored(dx)).astype(F32)
 
     def qkv_outer(begin, n):
         return jnp.concatenate(
@@ -754,7 +868,11 @@
             axis=2,
         )
 
-    qkv_grad = links.scatter(qkv_outer).astype(F32)
+    qkv_terms = links.terms(qkv_outer)
+    dq, dkv, qkv_terms = lax.optimization_barrier((dq, dkv, qkv_terms))
+    qkv_grad = links.scatter(qkv_terms).astype(F32)
+    dx = input_back(dq, dkv, weights, dh1)
+    input_grad = links.rows_out(restored(dx)).astype(F32)
 
     sums = jnp.concatenate(
         [

time: 552 us -> 592 us (1.072)
  Pallas kernels: 164 us -> 308 us
  waiting for transfers between devices: 176 us -> 130 us
  blocking collectives: 51 us -> 18 us
  starting transfers between devices: 57.2 us -> 37.3 us
    pallas_call x8 -> x9, Pallas kernels: 76.7 us -> 220 us  [the longest x1 150 us: gather(): pl.pallas_call(functools.partial(gather_kernel, count, parts, 6), in_spec...]
    ppermute x25 -> x4, waiting for transfers between devices: 62.6 us -> 8.08 us  [scatter(): far = lax.ppermute(away, AXES, self.core_pairs())]
    all_gather x1, blocking collectives: 51 us -> 18 us  [shards(): lax.all_gather(jnp.concatenate([query_bias, value_bias, up_bias]), 'tenso...]
    all_gather x3 -> x0, waiting for transfers between devices: 29.3 us -> none  [gather(): block = lax.all_gather(local, 'tensor', axis=0, tiled=False)]
    ppermute x2, waiting for transfers between devices: 0.01 us -> 20.8 us  [rows_in(): lax.ppermute(first, AXES, self.row_pairs(0))]
    ppermute x25 -> x4, starting transfers between devices: 14.1 us -> 1.02 us  [scatter(): far = lax.ppermute(away, AXES, self.core_pairs())]
    unnamed x77 -> x101, local copies, waits for them, and re-layouts: 8.68 us -> 18 us
    ppermute x4, waiting for transfers between devices: 14.6 us -> 23.3 us  [scatter(): far = lax.ppermute(away, AXES, self.second_pairs())]
  transfers between devices with their start and end apart: 55 -> 31, of which waited for: 17 -> 14; matrix products, arithmetic and copies ran while one was open for 13% -> 9% of each run, Pallas kernels for 17% -> 29%
where the time goes in v2:
time: 592 us; the launch traced here: 586 us
  Pallas kernels  308 us (52%)
  waiting for transfers between devices  130 us (22%)
  other arithmetic  42.3 us (7%)
  starting transfers between devices  37.3 us (6%)
  local copies, waits for them, and re-layouts  27.6 us (5%)
  blocking collectives  18 us (3%)
  between operations  15.4 us (3%)
  matrix products  7.54 us (1%)
    pallas_call x1, Pallas kernels, gather(): pl.pallas_call(functools.partial(gather_kernel, count, parts, 6), in_spec...  150 us
    pallas_call x1, Pallas kernels, attend_backward(): call(functools.partial(attend_back_kernel, count), (number, pairs), [one(...  31 us
    ppermute x4, waiting for transfers between devices, scatter(): far = lax.ppermute(away, AXES, self.first_pairs())  29.9 us
    pallas_call x6, Pallas kernels, outer(): call(outer_kernel, (parts,), [pl.BlockSpec((rows, count * depth), lambda...  25.5 us
    ppermute x4, waiting for transfers between devices, scatter(): far = lax.ppermute(away, AXES, self.second_pairs())  23.3 us
    pallas_call x1, Pallas kernels, attend_forward(): call(functools.partial(attend_kernel, count), (number, pairs), [one(0)] +...  21 us
    ppermute x2, waiting for transfers between devices, rows_in(): lax.ppermute(first, AXES, self.row_pairs(0))  20.8 us
    convert_element_type x8, other arithmetic, summed(): return (left.astype(F32) + right.astype(F32)).astype(BF)  18.7 us
  transfers between devices with their start and end apart: 31, of which 14 were waited for; matrix products, arithmetic and copies ran while one was open for 9% of the time, Pallas kernels for 29%

profile of v2, /device:TPU:8, one launch (start us, length us, event | category | flops | bytes accessed | tf_op | source)
XLA Modules:
  0.0 585.5 jit_solution(1339964303402649913)
XLA Ops:
  8.7 3.5 collective-permute-start
  13.7 150.3 %shard_map.314.w_ref = bf16[12,8,4,128,256]{4,3,2,1,0:T(8,128)(2,1)} custom-call(bf16[12,128,256]{2,1,0:T(8,128)(2,1)} %copy-done.21), custom_call_target="tpu_custom_call" | custom-call | tf_op jit(solution)/shard_map/pallas_call | solution.py:653
  164.0 18.0 %all-gather.1 = f32[4,1,1536]{2,1,0:T(1,128)S(1)} all-gather(f32[1,1,1536]{2,1,0:T(1,128)S(1)} %reshape.192), channel_id=2, replica_groups=mesh['dp'=8,'tensor'=4] {'tensor'}, dimensions={0}, use_global_device_ids=true | all-gather | bytes 30720 | tf_op jit(solution)/shard_map/all_gather | solution.py:823
  183.2 2.5 fusion.8.x_ref.left_ref
  185.7 9.8 %shard_map.315.q_ref.refs_0_.refs_2_ = bf16[3,512,1024]{2,1,0:T(8,128)(2,1)S(1)} custom-call(bf16[512,1024]{1,0:T(8,128)(2,1)S(1)} %fusion.8.x_ref.left_ref, bf16[12,8,4,128,256]{4,3,2,1,0:T(8,128)(2,1)} %shard_map.314.w_ref, f32[3,1,1024]{2,1,0:T(1,128)S(1)} %pad_maximum_fusion.4.bias_ref), custom_call_target="tpu_custom_call" | custom-call | flops 3221225472 | bytes 10485760 | tf_op jit(solution)/shard_map/pallas_call | solution.py:80
  195.5 1.5 slice.267
  198.0 1.9 collective-permute-start.3
  200.8 20.8 %collective-permute-done.3 = bf16[256,1024]{1,0:T(8,128)(2,1)S(1)} collective-permute-done((bf16[256,1024]{1,0:T(8,128)(2,1)S(1)}, bf16[256,1024]{1,0:T(8,128)(2,1)S(1)}, u32[]{:S(2)}, u32[]{:S(2)}) %collective-permute-start.3) | collective-permute-done | bytes 524320 | tf_op jit(solution)/shard_map/ppermute | solution.py:733
  221.6 2.4 fusion.9.c_ref
  224.0 21.0 %shard_map.316 = (bf16[512,1024]{1,0:T(8,128)(2,1)S(1)}, f32[1,8,2,512]{3,2,1,0:T(2,128)S(1)}) custom-call(bf16[3,512,1024]{2,1,0:T(8,128)(2,1)} %copy-done.5, bf16[3,512,1024]{2,1,0:T(8,128)(2,1)} %copy-done.5, bf16[2,512,1024]{2,1,0:T(8,128)(2,1)} %collective-permute-done.2.refs_1_.refs_3_, bf16[3,512,1024]{2,1,0:T(8,128)(2,1)} %copy-done.5, ...), custom_call_target="tpu_custom_call" | custom-call | flops 8589934592 | bytes 6291456 | tf_op jit(solution)/shard_map/pallas_call | solution.py:147
  245.0 5.1 shard_map.317
  251.4 12.0 %shard_map.318 = (bf16[512,4096]{1,0:T(8,128)(2,1)S(1)}, bf16[512,4096]{1,0:T(8,128)(2,1)}) custom-call(bf16[512,1024]{1,0:T(8,128)(2,1)S(1)} %get-tuple-element.50.y_ref.left_ref, bf16[12,8,4,128,256]{4,3,2,1,0:T(8,128)(2,1)} %shard_map.314.w_ref, f32[1,4096]{1,0:T(1,128)S(1)} %bitcast.139), custom_call_target="tpu_custom_call" | custom-call | flops 4294967296 | bytes 17825792 | tf_op jit(solution)/shard_map/pallas_call | solution.py:321
  263.4 1.9 copy-done.1
  265.3 11.0 %shard_map.319 = (bf16[512,1024]{1,0:T(8,128)(2,1)S(1)}, f32[512,1024]{1,0:T(8,128)S(1)}, bf16[512,1024]{1,0:T(8,128)(2,1)S(1)}, f32[8,1024]{1,0:T(8,128)S(1)}) custom-call(bf16[512,4096]{1,0:T(8,128)(2,1)} %copy-done.1, bf16[12,8,4,128,256]{4,3,2,1,0:T(8,128)(2,1)} %shard_map.314.w_ref, f32[512,1024]{1,0:T(8,128)} %copy-done.6, ...), custom_call_target="tpu_custom_call" | custom-call | flops 4294967296 | bytes 19922944 | tf_op jit(solution)/shard_map/pallas_call | solution.py:364
  277.3 4.9 shard_map.321
  282.3 6.1 %shard_map.320 = bf16[4,4,128,1024]{3,2,1,0:T(8,128)(2,1)} custom-call(bf16[512,1024]{1,0:T(8,128)(2,1)S(1)} %get-tuple-element.55.left_ref.b_ref, bf16[512,4096]{1,0:T(8,128)(2,1)} %copy-done.1), custom_call_target="tpu_custom_call" | custom-call | flops 2147483648 | bytes 8912896 | tf_op jit(solution)/shard_map/pallas_call | solution.py:516
  288.4 9.8 %shard_map.322 = (bf16[512,4096]{1,0:T(8,128)(2,1)S(1)}, f32[1,4096]{1,0:T(1,128)S(1)}) custom-call(bf16[512,1024]{1,0:T(8,128)(2,1)S(1)} %get-tuple-element.55.left_ref.b_ref, bf16[12,8,4,128,256]{4,3,2,1,0:T(8,128)(2,1)} %shard_map.314.w_ref, bf16[512,4096]{1,0:T(8,128)(2,1)} %get-tuple-element.56.slope_ref), custom_call_target="tpu_custom_call" | custom-call | flops 4294967296 | bytes 17825792 | tf_op jit(solution)/shard_map/pallas_call | solution.py:409
  298.2 2.0 copy-done
  300.2 5.0 shard_map.324
  305.2 2.1 copy-done.4
  307.3 6.1 %shard_map.323 = bf16[4,4,128,1024]{3,2,1,0:T(8,128)(2,1)} custom-call(bf16[512,1024]{1,0:T(8,128)(2,1)S(1)} %get-tuple-element.50.y_ref.left_ref, bf16[512,4096]{1,0:T(8,128)(2,1)} %copy-done), custom_call_target="tpu_custom_call" | custom-call | flops 2147483648 | bytes 8912896 | tf_op jit(solution)/shard_map/pallas_call | solution.py:516
  313.4 10.4 %shard_map.325 = (f32[512,1024]{1,0:T(8,128)S(1)}, bf16[512,1024]{1,0:T(8,128)(2,1)S(1)}, f32[8,1024]{1,0:T(8,128)S(1)}) custom-call(bf16[512,4096]{1,0:T(8,128)(2,1)} %copy-done, bf16[12,8,4,128,256]{4,3,2,1,0:T(8,128)(2,1)} %shard_map.314.w_ref, f32[512,1024]{1,0:T(8,128)S(1)} %get-tuple-element.59.dh2_ref, f32[512,1024]{1,0:T(8,128)} %copy-done.6, ...), custom_call_target="tpu_custom_call" | custom-call | flops 4294967296 | bytes 20971520 | tf_op jit(solution)/shard_map/pallas_call | solution.py:450
  325.1 1.7 shard_map.328
  326.8 1.7 shard_map.327
  328.5 3.5 shard_map.326.refs_4_
  332.0 31.0 %shard_map.329 = (bf16[512,1024]{1,0:T(8,128)(2,1)S(1)}, f32[2,512,1024]{2,1,0:T(8,128)}, bf16[2,512,1024]{2,1,0:T(8,128)(2,1)S(1)}) custom-call(bf16[3,512,1024]{2,1,0:T(8,128)(2,1)} %copy-done.5, bf16[3,512,1024]{2,1,0:T(8,128)(2,1)} %copy-done.5, bf16[2,512,1024]{2,1,0:T(8,128)(2,1)} %collective-permute-done.2.refs_1_.refs_3_, ...), custom_call_target="tpu_custom_call" | custom-call | flops 21474836480 | bytes 12582912 | tf_op jit(solution)/shard_map/pallas_call | solution.py:210
  363.1 3.6 collective-permute-start.7
  366.8 1.7 shard_map.332
  368.4 1.7 shard_map.330
  370.1 2.6 collective-permute-done.7
  374.1 3.6 add_convert_fusion.4.right_ref.dkv_ref
  377.7 3.3 shard_map.333
  381.1 1.9 pad_maximum_fusion.1
  383.0 3.5 shard_map.331
  387.8 7.9 %collective-permute-done.10 = bf16[4,4,3,128,256]{4,3,2,1,0:T(8,128)(2,1)S(1)} collective-permute-done((bf16[4,4,3,128,256]{4,3,2,1,0:T(8,128)(2,1)S(1)}, bf16[4,4,3,128,256]{4,3,2,1,0:T(8,128)(2,1)S(1)}, u32[]{:S(2)}, u32[]{:S(2)}) %collective-permute-start.10) | collective-permute-done | bytes 3145760 | tf_op jit(solution)/shard_map/ppermute | solution.py:707
  397.1 1.5 collective-permute-start.11
  399.0 1.5 collective-permute-start.19
  400.5 5.0 add_convert_fusion.1
  406.1 17.0 %collective-permute-done.19 = bf16[2,4,128,256]{3,2,1,0:T(8,128)(2,1)S(1)} collective-permute-done((bf16[2,4,128,256]{3,2,1,0:T(8,128)(2,1)S(1)}, bf16[2,4,128,256]{3,2,1,0:T(8,128)(2,1)S(1)}, u32[]{:S(2)}, u32[]{:S(2)}) %collective-permute-start.19) | collective-permute-done | bytes 524320 | tf_op jit(solution)/shard_map/ppermute | solution.py:710
  423.2 1.4 collective-permute-start.20
  426.8 5.7 collective-permute-done.20
  433.4 6.0 %add_convert_fusion.3 = (bf16[2,4,128,1024]{3,2,1,0:T(8,128)(2,1)}, bf16[2,4,128,1024]{3,2,1,0:T(8,128)(2,1)}) fusion(bf16[4,4,128,1024]{3,2,1,0:T(8,128)(2,1)} %collective-permute-done.21, bf16[4,4,128,1024]{3,2,1,0:T(8,128)(2,1)} %copy-done.4), kind=kLoop, calls=%fused_computation.6 | loop fusion | flops 8388608 | bytes 12582912 | tf_op jit(solution)/shard_map/convert_element_type | solution.py:767
  440.8 8.6 %collective-permute-done.12 = bf16[1,4,3,128,256]{4,3,2,1,0:T(8,128)(2,1)S(1)} collective-permute-done((bf16[1,4,3,128,256]{4,3,2,1,0:T(8,128)(2,1)}, bf16[1,4,3,128,256]{4,3,2,1,0:T(8,128)(2,1)S(1)}, u32[]{:S(2)}, u32[]{:S(2)}) %collective-permute-start.12) | collective-permute-done | bytes 786464 | tf_op jit(solution)/shard_map/ppermute | solution.py:713
  450.7 6.3 %collective-permute-done.25 = bf16[2,4,128,1024]{3,2,1,0:T(8,128)(2,1)} collective-permute-done((bf16[2,4,128,1024]{3,2,1,0:T(8,128)(2,1)}, bf16[2,4,128,1024]{3,2,1,0:T(8,128)(2,1)}, u32[]{:S(2)}, u32[]{:S(2)}) %collective-permute-start.25) | collective-permute-done | bytes 2097184 | tf_op jit(solution)/shard_map/ppermute | solution.py:710
  457.0 2.9 add_convert_fusion.8
  465.6 5.1 collective-permute-start.6
  470.7 15.6 %collective-permute-done.26 = bf16[1,4,128,1024]{3,2,1,0:T(8,128)(2,1)} collective-permute-done((bf16[1,4,128,1024]{3,2,1,0:T(8,128)(2,1)}, bf16[1,4,128,1024]{3,2,1,0:T(8,128)(2,1)}, u32[]{:S(2)}, u32[]{:S(2)}) %collective-permute-start.26) | collective-permute-done | bytes 1048608 | tf_op jit(solution)/shard_map/ppermute | solution.py:713
  486.3 3.1 fusion.13
  491.8 1.6 add_convert_fusion.11
  493.4 1.4 collective-permute-start.23
  495.0 2.2 collective-permute-done.6
  498.5 1.6 collective-permute-start.14
  501.1 8.5 %collective-permute-done.14 = f32[12,1024]{1,0:T(8,128)S(1)} collective-permute-done((f32[12,1024]{1,0:T(8,128)S(1)}, f32[12,1024]{1,0:T(8,128)S(1)}, u32[]{:S(2)}, u32[]{:S(2)}) %collective-permute-start.14) | collective-permute-done | bytes 49184 | tf_op jit(solution)/shard_map/ppermute | solution.py:752
  509.7 1.5 collective-permute-start.15
  511.2 7.9 %shard_map.334 = bf16[512,1024]{1,0:T(8,128)(2,1)S(1)} custom-call(bf16[512,1024]{1,0:T(8,128)(2,1)S(1)} %copy-done.3, bf16[2,512,1024]{2,1,0:T(8,128)(2,1)S(1)} %add_convert_fusion.4.right_ref.dkv_ref, bf16[12,8,4,128,256]{4,3,2,1,0:T(8,128)(2,1)} %shard_map.314.w_ref, f32[512,1024]{1,0:T(8,128)} %copy-done.7), custom_call_target="tpu_custom_call" | custom-call | flops 3221225472 | bytes 14680064 | tf_op jit(solution)/shard_map/pallas_call | solution.py:490
  520.1 1.5 collective-permute-start.16
  521.6 2.9 fusion.12
  525.9 4.0 collective-permute-start.17
  530.1 3.1 collective-permute-start.9
  533.2 2.7 collective-permute-done.17
  539.9 16.2 %collective-permute-done.8 = bf16[256,1024]{1,0:T(8,128)(2,1)S(1)} collective-permute-done((bf16[256,1024]{1,0:T(8,128)(2,1)S(1)}, bf16[256,1024]{1,0:T(8,128)(2,1)S(1)}, u32[]{:S(2)}, u32[]{:S(2)}) %collective-permute-start.8) | collective-permute-done | bytes 524320 | tf_op jit(solution)/shard_map/ppermute | solution.py:744
  556.1 15.4 %collective-permute-done.9 = bf16[256,1024]{1,0:T(8,128)(2,1)S(1)} collective-permute-done((bf16[256,1024]{1,0:T(8,128)(2,1)S(1)}, bf16[256,1024]{1,0:T(8,128)(2,1)S(1)}, u32[]{:S(2)}, u32[]{:S(2)}) %collective-permute-start.9) | collective-permute-done | bytes 524320 | tf_op jit(solution)/shard_map/ppermute | solution.py:743
  571.5 1.5 maximum_convert_fusion
  576.7 1.8 bitcast_convert_fusion
  (196 shorter events, 40.6 us)
Async XLA Ops:
  7.2 5.1 copy-start.22
  7.2 5.2 copy-start.24
  7.2 5.3 copy-start.25
  7.2 5.4 copy-start.26
  7.2 5.4 copy-start.27
  7.2 5.4 copy-start.23
  7.3 531.0 %reduce-scatter.7.cloned.1.call-start = ((), (), s32[]{:S(2)}) async-start(), calls=%async_computation.5 | async-start | bytes 327680 | tf_op jit(solution)/shard_map/reduce_scatter | solution.py:715
  8.7 173.7 %collective-permute-start = (bf16[256,1024]{1,0:T(8,128)(2,1)S(1)}, bf16[256,1024]{1,0:T(8,128)(2,1)S(1)}, u32[]{:S(2)}, u32[]{:S(2)}) collective-permute-start(bf16[256,1024]{1,0:T(8,128)(2,1)S(1)} %get-tuple-element.150), channel_id=1, source_target_pairs={{0,0},{1,2},{2,4},{3,6},{4,1},{5,3},{6,5},{7,7},{8,8},{9,10},{10,1... | collective-permute-start | bytes 1572872 | tf_op jit(solution)/shard_map/ppermute | solution.py:733
  12.2 171.0 %collective-permute-start.1 = (bf16[256,1024]{1,0:T(8,128)(2,1)S(1)}, bf16[256,1024]{1,0:T(8,128)(2,1)}, u32[]{:S(2)}, u32[]{:S(2)}) collective-permute-start(bf16[256,1024]{1,0:T(8,128)(2,1)S(1)} %get-tuple-element.151), channel_id=1, source_target_pairs={{0,2},{1,0},{2,6},{3,4},{4,3},{5,1},{6,7},{7,5},{8,10},{9,8},{10,1... | collective-permute-start | bytes 1572872 | tf_op jit(solution)/shard_map/ppermute | solution.py:734
  13.7 150.3 %copy-start.28 = (f32[1024]{0:T(1024)S(1)}, f32[1024]{0:T(1024)}, u32[]{:S(2)}) copy-start(f32[1024]{0:T(1024)} %param.30) | copy-start | bytes 12292
  13.7 150.3 %copy-start.35 = (f32[256]{0:T(256)S(1)}, f32[256]{0:T(256)}, u32[]{:S(2)}) copy-start(f32[256]{0:T(256)} %param.24) | copy-start | bytes 3076
  13.7 150.3 %copy-start.36 = (f32[256]{0:T(256)S(1)}, f32[256]{0:T(256)}, u32[]{:S(2)}) copy-start(f32[256]{0:T(256)} %param.21) | copy-start | bytes 3076
  13.7 168.5 %copy-start.37 = (s32[2,8]{1,0:T(2,128)S(1)}, s32[2,8]{1,0:T(2,128)}, u32[]{:S(2)}) copy-start(s32[2,8]{1,0:T(2,128)} %constant.67.clone) | copy-start | bytes 196
  195.5 2.3 copy-start.5
  195.5 2.4 copy-start.20
  197.8 2.3 copy-start.29
  197.8 2.3 copy-start.30
  197.8 2.3 copy-start.31
  197.8 2.3 copy-start.32
  197.8 2.3 copy-start.33
  197.8 2.3 copy-start.34
  197.8 26.1 %collective-permute-start.2 = (bf16[2,512,1024]{2,1,0:T(8,128)(2,1)}, bf16[2,512,1024]{2,1,0:T(8,128)(2,1)}, u32[]{:S(2)}, u32[]{:S(2)}) collective-permute-start(bf16[2,512,1024]{2,1,0:T(8,128)(2,1)} %slice.267), channel_id=1, source_target_pairs={{0,4},{1,5},{2,6},{3,7},{4,0},{5,1},{6,2},{7,3},{8,12},{9,13},{10,... | collective-permute-start | bytes 6291464 | tf_op jit(solution)/shard_map/ppermute | solution.py:836
  198.0 23.6 %collective-permute-start.3 = (bf16[256,1024]{1,0:T(8,128)(2,1)S(1)}, bf16[256,1024]{1,0:T(8,128)(2,1)S(1)}, u32[]{:S(2)}, u32[]{:S(2)}) collective-permute-start(bf16[256,1024]{1,0:T(8,128)(2,1)S(1)} %get-tuple-element.148), channel_id=1, source_target_pairs={{0,0},{1,2},{2,4},{3,6},{4,1},{5,3},{6,5},{7,7},{8,8},{9,10},{10,1... | collective-permute-start | bytes 1572872 | tf_op jit(solution)/shard_map/ppermute | solution.py:733
  199.9 21.7 %collective-permute-start.4 = (bf16[256,1024]{1,0:T(8,128)(2,1)S(1)}, bf16[256,1024]{1,0:T(8,128)(2,1)}, u32[]{:S(2)}, u32[]{:S(2)}) collective-permute-start(bf16[256,1024]{1,0:T(8,128)(2,1)S(1)} %get-tuple-element.149), channel_id=1, source_target_pairs={{0,2},{1,0},{2,6},{3,4},{4,3},{5,1},{6,7},{7,5},{8,10},{9,8},{10,1... | collective-permute-start | bytes 1572872 | tf_op jit(solution)/shard_map/ppermute | solution.py:734
  250.1 1.3 copy-start.6
  263.4 1.9 copy-start.1
  298.2 2.0 copy-start
  305.2 2.1 copy-start.4
  363.0 7.1 %copy-start.2 = (bf16[512,1024]{1,0:T(8,128)(2,1)}, bf16[512,1024]{1,0:T(8,128)(2,1)S(1)}, u32[]{:S(2)}) copy-start(bf16[512,1024]{1,0:T(8,128)(2,1)S(1)} %get-tuple-element.67.dq_ref) | copy-start | bytes 3145732
  363.1 9.7 %collective-permute-start.7 = (bf16[2,512,1024]{2,1,0:T(8,128)(2,1)S(1)}, bf16[2,512,1024]{2,1,0:T(8,128)(2,1)S(1)}, u32[]{:S(2)}, u32[]{:S(2)}) collective-permute-start(bf16[2,512,1024]{2,1,0:T(8,128)(2,1)S(1)} %get-tuple-element.66), channel_id=1, source_target_pairs={{0,4},{1,5},{2,6},{3,7},{4,0},{5,1},{6,2},{7,3},{8,12},{9,13},{10,... | collective-permute-start | bytes 6291464 | tf_op jit(solution)/shard_map/ppermute | solution.py:858
  366.7 33.8 %collective-permute-start.24 = (bf16[4,4,128,1024]{3,2,1,0:T(8,128)(2,1)}, bf16[4,4,128,1024]{3,2,1,0:T(8,128)(2,1)}, u32[]{:S(2)}, u32[]{:S(2)}) collective-permute-start(bf16[4,4,128,1024]{3,2,1,0:T(8,128)(2,1)} %shard_map.320), channel_id=1, source_target_pairs={{0,4},{1,5},{2,6},{3,7},{4,0},{5,1},{6,2},{7,3},{8,12},{9,13},{10,... | collective-permute-start | bytes 12582920 | tf_op jit(solution)/shard_map/ppermute | solution.py:707
  386.5 9.2 %copy-start.12 = (bf16[4,4,3,128,256]{4,3,2,1,0:T(8,128)(2,1)S(1)}, bf16[4,4,3,128,256]{4,3,2,1,0:T(8,128)(2,1)}, u32[]{:S(2)}) copy-start(bf16[4,4,3,128,256]{4,3,2,1,0:T(8,128)(2,1)} %pad_maximum_fusion.1) | copy-start | bytes 9437188
  386.8 8.9 %collective-permute-start.10 = (bf16[4,4,3,128,256]{4,3,2,1,0:T(8,128)(2,1)S(1)}, bf16[4,4,3,128,256]{4,3,2,1,0:T(8,128)(2,1)S(1)}, u32[]{:S(2)}, u32[]{:S(2)}) collective-permute-start(bf16[4,4,3,128,256]{4,3,2,1,0:T(8,128)(2,1)S(1)} %pad_maximum_fusion), channel_id=1, source_target_pairs={{0,4},{1,5},{2,6},{3,7},{4,0},{5,1},{6,2},{7,3},{8,12},{9,13},{10,... | collective-permute-start | bytes 9437192 | tf_op jit(solution)/shard_map/ppermute | solution.py:707
  387.2 46.2 %collective-permute-start.21 = (bf16[4,4,128,1024]{3,2,1,0:T(8,128)(2,1)}, bf16[4,4,128,1024]{3,2,1,0:T(8,128)(2,1)}, u32[]{:S(2)}, u32[]{:S(2)}) collective-permute-start(bf16[4,4,128,1024]{3,2,1,0:T(8,128)(2,1)} %shard_map.323), channel_id=1, source_target_pairs={{0,4},{1,5},{2,6},{3,7},{4,0},{5,1},{6,2},{7,3},{8,12},{9,13},{10,... | collective-permute-start | bytes 12582920 | tf_op jit(solution)/shard_map/ppermute | solution.py:707
  387.4 11.3 %collective-permute-start.18 = (bf16[4,4,128,256]{3,2,1,0:T(8,128)(2,1)S(1)}, bf16[4,4,128,256]{3,2,1,0:T(8,128)(2,1)S(1)}, u32[]{:S(2)}, u32[]{:S(2)}) collective-permute-start(bf16[4,4,128,256]{3,2,1,0:T(8,128)(2,1)S(1)} %shard_map.327), channel_id=1, source_target_pairs={{0,4},{1,5},{2,6},{3,7},{4,0},{5,1},{6,2},{7,3},{8,12},{9,13},{10,... | collective-permute-start | bytes 3145736 | tf_op jit(solution)/shard_map/ppermute | solution.py:707
  397.0 27.6 %copy-start.15 = (bf16[2,4,3,128,256]{4,3,2,1,0:T(8,128)(2,1)}, bf16[2,4,3,128,256]{4,3,2,1,0:T(8,128)(2,1)S(1)}, u32[]{:S(2)}) copy-start(bf16[2,4,3,128,256]{4,3,2,1,0:T(8,128)(2,1)S(1)} %get-tuple-element.136) | copy-start | bytes 4718596
  397.1 27.6 %collective-permute-start.11 = (bf16[2,4,3,128,256]{4,3,2,1,0:T(8,128)(2,1)S(1)}, bf16[2,4,3,128,256]{4,3,2,1,0:T(8,128)(2,1)S(1)}, u32[]{:S(2)}, u32[]{:S(2)}) collective-permute-start(bf16[2,4,3,128,256]{4,3,2,1,0:T(8,128)(2,1)S(1)} %get-tuple-element.137), channel_id=1, source_target_pairs={{0,16},{1,17},{2,18},{3,19},{4,12},{5,13},{6,14},{7,15},{8,24},{9,... | collective-permute-start | bytes 4718600 | tf_op jit(solution)/shard_map/ppermute | solution.py:710
  399.0 24.1 %collective-permute-start.19 = (bf16[2,4,128,256]{3,2,1,0:T(8,128)(2,1)S(1)}, bf16[2,4,128,256]{3,2,1,0:T(8,128)(2,1)S(1)}, u32[]{:S(2)}, u32[]{:S(2)}) collective-permute-start(bf16[2,4,128,256]{3,2,1,0:T(8,128)(2,1)S(1)} %get-tuple-element.139), channel_id=1, source_target_pairs={{0,16},{1,17},{2,18},{3,19},{4,12},{5,13},{6,14},{7,15},{8,24},{9,... | collective-permute-start | bytes 1572872 | tf_op jit(solution)/shard_map/ppermute | solution.py:710
  405.5 51.4 %collective-permute-start.25 = (bf16[2,4,128,1024]{3,2,1,0:T(8,128)(2,1)}, bf16[2,4,128,1024]{3,2,1,0:T(8,128)(2,1)}, u32[]{:S(2)}, u32[]{:S(2)}) collective-permute-start(bf16[2,4,128,1024]{3,2,1,0:T(8,128)(2,1)} %get-tuple-element.133), channel_id=1, source_target_pairs={{0,16},{1,17},{2,18},{3,19},{4,12},{5,13},{6,14},{7,15},{8,24},{9,... | collective-permute-start | bytes 6291464 | tf_op jit(solution)/shard_map/ppermute | solution.py:710
  423.2 9.3 %collective-permute-start.20 = (bf16[1,4,128,256]{3,2,1,0:T(8,128)(2,1)S(1)}, bf16[1,4,128,256]{3,2,1,0:T(8,128)(2,1)S(1)}, u32[]{:S(2)}, u32[]{:S(2)}) collective-permute-start(bf16[1,4,128,256]{3,2,1,0:T(8,128)(2,1)S(1)} %add_convert_fusion.19), channel_id=1, source_target_pairs={{0,8},{1,9},{2,10},{3,11},{4,20},{5,21},{6,22},{7,23},{8,0},{9,1},... | collective-permute-start | bytes 786440 | tf_op jit(solution)/shard_map/ppermute | solution.py:713
  424.6 1.5 copy-start.18
  426.1 23.3 %collective-permute-start.12 = (bf16[1,4,3,128,256]{4,3,2,1,0:T(8,128)(2,1)}, bf16[1,4,3,128,256]{4,3,2,1,0:T(8,128)(2,1)S(1)}, u32[]{:S(2)}, u32[]{:S(2)}) collective-permute-start(bf16[1,4,3,128,256]{4,3,2,1,0:T(8,128)(2,1)} %add_convert_fusion.14), channel_id=1, source_target_pairs={{0,8},{1,9},{2,10},{3,11},{4,20},{5,21},{6,22},{7,23},{8,0},{9,1},... | collective-permute-start | bytes 2359304 | tf_op jit(solution)/shard_map/ppermute | solution.py:713
  433.4 139.6 %reduce-scatter.5.cloned.1.call-start = ((), (), s32[]{:S(2)}) async-start(), calls=%async_computation.4 | async-start | bytes 983040 | tf_op jit(solution)/shard_map/reduce_scatter | solution.py:715
  433.4 16.0 %copy-start.16 = (bf16[2,4,3,128,256]{4,3,2,1,0:T(8,128)(2,1)S(1)}, bf16[2,4,3,128,256]{4,3,2,1,0:T(8,128)(2,1)}, u32[]{:S(2)}) copy-start(bf16[2,4,3,128,256]{4,3,2,1,0:T(8,128)(2,1)} %copy-done.15) | copy-start | bytes 4718596
  433.4 16.0 %copy-start.19 = (bf16[2,4,3,128,256]{4,3,2,1,0:T(8,128)(2,1)S(1)}, bf16[2,4,3,128,256]{4,3,2,1,0:T(8,128)(2,1)}, u32[]{:S(2)}) copy-start(bf16[2,4,3,128,256]{4,3,2,1,0:T(8,128)(2,1)} %copy-done.18) | copy-start | bytes 4718596
  439.4 51.4 %collective-permute-start.22 = (bf16[2,4,128,1024]{3,2,1,0:T(8,128)(2,1)}, bf16[2,4,128,1024]{3,2,1,0:T(8,128)(2,1)}, u32[]{:S(2)}, u32[]{:S(2)}) collective-permute-start(bf16[2,4,128,1024]{3,2,1,0:T(8,128)(2,1)} %get-tuple-element.135), channel_id=1, source_target_pairs={{0,16},{1,17},{2,18},{3,19},{4,12},{5,13},{6,14},{7,15},{8,24},{9,... | collective-permute-start | bytes 6291464 | tf_op jit(solution)/shard_map/ppermute | solution.py:710
  450.6 10.6 %copy-start.39 = (s32[2,8]{1,0:T(2,128)S(1)}, s32[2,8]{1,0:T(2,128)}, u32[]{:S(2)}) copy-start(s32[2,8]{1,0:T(2,128)} %constant.68.clone) | copy-start | bytes 196
  450.6 12.5 %copy-start.11 = (bf16[512,1024]{1,0:T(8,128)(2,1)S(1)}, bf16[512,1024]{1,0:T(8,128)(2,1)}, u32[]{:S(2)}) copy-start(bf16[512,1024]{1,0:T(8,128)(2,1)} %copy-done.10) | copy-start | bytes 3145732
  450.7 124.0 %reduce-scatter.11.cloned.1.call-start = ((), (), s32[]{:S(2)}) async-start(), calls=%async_computation.7 | async-start | bytes 1310720 | tf_op jit(solution)/shard_map/reduce_scatter | solution.py:715
  459.9 26.4 %collective-permute-start.26 = (bf16[1,4,128,1024]{3,2,1,0:T(8,128)(2,1)}, bf16[1,4,128,1024]{3,2,1,0:T(8,128)(2,1)}, u32[]{:S(2)}, u32[]{:S(2)}) collective-permute-start(bf16[1,4,128,1024]{3,2,1,0:T(8,128)(2,1)} %add_convert_fusion.8), channel_id=1, source_target_pairs={{0,8},{1,9},{2,10},{3,11},{4,20},{5,21},{6,22},{7,23},{8,0},{9,1},... | collective-permute-start | bytes 3145736 | tf_op jit(solution)/shard_map/ppermute | solution.py:713
  464.5 21.8 %copy-start.14 = (bf16[2,4,128,1024]{3,2,1,0:T(8,128)(2,1)S(1)}, bf16[2,4,128,1024]{3,2,1,0:T(8,128)(2,1)}, u32[]{:S(2)}) copy-start(bf16[2,4,128,1024]{3,2,1,0:T(8,128)(2,1)} %get-tuple-element.132) | copy-start | bytes 6291460
  465.6 29.4 %collective-permute-start.5 = (bf16[256,1024]{1,0:T(8,128)(2,1)}, bf16[256,1024]{1,0:T(8,128)(2,1)}, u32[]{:S(2)}, u32[]{:S(2)}) collective-permute-start(bf16[256,1024]{1,0:T(8,128)(2,1)} %get-tuple-element.146), channel_id=1, source_target_pairs={{2,0},{0,1},{6,2},{4,3},{3,4},{1,5},{7,6},{5,7},{10,8},{8,9},{14,1... | collective-permute-start | bytes 1572872 | tf_op jit(solution)/shard_map/ppermute | solution.py:744
  465.6 31.6 %collective-permute-start.6 = (bf16[256,1024]{1,0:T(8,128)(2,1)}, bf16[256,1024]{1,0:T(8,128)(2,1)}, u32[]{:S(2)}, u32[]{:S(2)}) collective-permute-start(bf16[256,1024]{1,0:T(8,128)(2,1)} %get-tuple-element.147), channel_id=1, source_target_pairs={{0,0},{2,1},{4,2},{6,3},{1,4},{3,5},{5,6},{7,7},{8,8},{10,9},{12,1... | collective-permute-start | bytes 1572872 | tf_op jit(solution)/shard_map/ppermute | solution.py:743
  489.5 87.2 %reduce-scatter.9.cloned.1.call-start = ((), (), s32[]{:S(2)}) async-start(), calls=%async_computation.6 | async-start | bytes 1310720 | tf_op jit(solution)/shard_map/reduce_scatter | solution.py:715
  490.1 1.7 copy-start.13
  493.4 28.2 %collective-permute-start.23 = (bf16[1,4,128,1024]{3,2,1,0:T(8,128)(2,1)S(1)}, bf16[1,4,128,1024]{3,2,1,0:T(8,128)(2,1)S(1)}, u32[]{:S(2)}, u32[]{:S(2)}) collective-permute-start(bf16[1,4,128,1024]{3,2,1,0:T(8,128)(2,1)S(1)} %add_convert_fusion.11), channel_id=1, source_target_pairs={{0,8},{1,9},{2,10},{3,11},{4,20},{5,21},{6,22},{7,23},{8,0},{9,1},... | collective-permute-start | bytes 3145736 | tf_op jit(solution)/shard_map/ppermute | solution.py:713
  494.9 3.6 collective-permute-start.13
  498.5 11.2 %collective-permute-start.14 = (f32[12,1024]{1,0:T(8,128)S(1)}, f32[12,1024]{1,0:T(8,128)S(1)}, u32[]{:S(2)}, u32[]{:S(2)}) collective-permute-start(f32[12,1024]{1,0:T(8,128)S(1)} %fusion.33), channel_id=1, source_target_pairs={{0,8},{1,9},{2,10},{3,11},{4,12},{5,13},{6,14},{7,15},{8,0},{9,1},... | collective-permute-start | bytes 147464 | tf_op jit(solution)/shard_map/ppermute | solution.py:752
  509.7 10.4 %collective-permute-start.15 = (f32[12,1024]{1,0:T(8,128)S(1)}, f32[12,1024]{1,0:T(8,128)S(1)}, u32[]{:S(2)}, u32[]{:S(2)}) collective-permute-start(f32[12,1024]{1,0:T(8,128)S(1)} %add.174), channel_id=1, source_target_pairs={{0,16},{1,17},{2,18},{3,19},{4,20},{5,21},{6,22},{7,23},{8,24},{9,... | collective-permute-start | bytes 147464 | tf_op jit(solution)/shard_map/ppermute | solution.py:752
  520.1 4.5 copy-start.9
  520.1 5.8 collective-permute-start.16
  525.9 10.0 %collective-permute-start.17 = (f32[12,1024]{1,0:T(8,128)S(1)}, f32[12,1024]{1,0:T(8,128)S(1)}, u32[]{:S(2)}, u32[]{:S(2)}) collective-permute-start(f32[12,1024]{1,0:T(8,128)S(1)} %add.176), channel_id=1, source_target_pairs={{0,2},{1,3},{2,0},{3,1},{4,6},{5,7},{6,4},{7,5},{8,10},{9,11},{10,... | collective-permute-start | bytes 147464 | tf_op jit(solution)/shard_map/ppermute | solution.py:761
  530.0 26.1 %collective-permute-start.8 = (bf16[256,1024]{1,0:T(8,128)(2,1)S(1)}, bf16[256,1024]{1,0:T(8,128)(2,1)S(1)}, u32[]{:S(2)}, u32[]{:S(2)}) collective-permute-start(bf16[256,1024]{1,0:T(8,128)(2,1)S(1)} %get-tuple-element.142), channel_id=1, source_target_pairs={{2,0},{0,1},{6,2},{4,3},{3,4},{1,5},{7,6},{5,7},{10,8},{8,9},{14,1... | collective-permute-start | bytes 1572872 | tf_op jit(solution)/shard_map/ppermute | solution.py:744
  530.1 41.4 %collective-permute-start.9 = (bf16[256,1024]{1,0:T(8,128)(2,1)S(1)}, bf16[256,1024]{1,0:T(8,128)(2,1)S(1)}, u32[]{:S(2)}, u32[]{:S(2)}) collective-permute-start(bf16[256,1024]{1,0:T(8,128)(2,1)S(1)} %get-tuple-element.143), channel_id=1, source_target_pairs={{0,0},{2,1},{4,2},{6,3},{1,4},{3,5},{5,6},{7,7},{8,8},{10,9},{12,1... | collective-permute-start | bytes 1572872 | tf_op jit(solution)/shard_map/ppermute | solution.py:743
  (7 other events, 7.5 us)
Sparse Core Ops, SparseCore 0:
  433.5 16.2 reduce-scatter.6
  452.2 27.2 reduce-scatter.4
  489.6 25.7 reduce-scatter.10
  524.7 40.8 reduce-scatter.8
